TPU v7x, 128 devices: a whole 4x4x4 slice. The times are simulated.
128 devices in a mesh: row: 8 (over z_hi, x), col: 16 (over y, z_lo, core).
Axes of the slice: x: 4, y: 4, z: 4 (z_hi: 2, z_lo: 2; z = z_hi * 2 + z_lo), core: 2. Of those that a mesh axis runs over, the one named last changes fastest.
Arguments:
- occupancy: int32 [128, 128], replicated, may hold values from 0 to 1, as said below
- stored: bfloat16 [8, 16, 8, 256, 256], P('row', 'col'), as said below
Outputs:
- window: float32 [4096, 32768], P('row', 'col')
Inputs may be any that keep to these rules, and one draw needn't show every extreme that they name: occupancy[i, j] is 0 where i > j. Each tile holds at most 8 blocks with occupancy 1, and tile (0, 15) holds exactly 8. Slots past a tile's number of occupied blocks are zero; stored blocks on the diagonal are symmetric.
All inputs are finite; a program needn't handle non-finite values.
Results may differ from a plain program's by a relative error of at most 0.0003.
Values may be sent and summed in bfloat16 or wider, within the bound.
No kernel may reach another device: no remote copies, remote signals or barrier semaphores. Data moves between devices by JAX's collectives and lax.ppermute only.
A program may use at most 768 MiB of HBM per device.

v0:
```python
import jax
import jax.numpy as jnp
from jax import lax
from jax.sharding import PartitionSpec as P

BS = 256
CB = 8
SLOTS = 8
SR = 2


def from_partner_2(block, axis, bit):
    count = lax.axis_size(axis)
    route = []
    for low in range(count):
        high = low | 1 << bit
        if high != low and high < count:
            route += [(low, high), (high, low)]
    return lax.ppermute(block, axis, route)


def passed_along(array, axis, by):
    peers = lax.axis_size(axis)
    pairs = [(i, i + by) for i in range(peers) if 0 <= i + by < peers]
    return lax.ppermute(array, axis, pairs)


def from_behind(block, axis, distance):
    devices = range(lax.axis_size(axis))
    route = [((i - distance) % len(devices), i) for i in devices]
    return lax.ppermute(block, axis, route)


def panel_blocks(row_panel, row_count):
    leading = row_panel * CB + jnp.arange(CB, dtype=jnp.int32)
    return jnp.concatenate([leading, leading + row_count * CB])


def tile_occupancy(pattern, row_panel, column, row_count):
    picked = jnp.take(pattern, panel_blocks(row_panel, row_count), axis=0)
    return lax.dynamic_slice_in_dim(picked, column * CB, CB, 1)


def unpack(packed, occupied):
    flat_mask = occupied.reshape(-1)
    position = jnp.clip(jnp.cumsum(flat_mask) - 1, 0, packed.shape[0] - 1)
    pieces = jnp.take(packed, position, axis=0) * flat_mask[:, None, None].astype(packed.dtype)
    row_blocks, col_blocks = occupied.shape
    edge = packed.shape[1]
    return (
        pieces.reshape(row_blocks, col_blocks, edge, edge)
        .transpose(0, 2, 1, 3)
        .reshape(row_blocks * edge, col_blocks * edge)
    )


def pack(dense, occupied, capacity):
    row_blocks, col_blocks = occupied.shape
    flat_mask = occupied.reshape(-1)
    running = jnp.cumsum(flat_mask)
    wanted = jnp.arange(capacity, dtype=jnp.int32)
    position = jnp.sum((running[None, :] <= wanted[:, None]).astype(jnp.int32), axis=1)
    present = (wanted < running[-1]).astype(dense.dtype)
    position = jnp.minimum(position, row_blocks * col_blocks - 1)
    pieces = (
        dense.reshape(row_blocks, BS, col_blocks, BS)
        .transpose(0, 2, 1, 3)
        .reshape(row_blocks * col_blocks, BS, BS)
    )
    return jnp.take(pieces, position, axis=0) * present[:, None, None]


def assemble(upper_part, mirror, partner, col_half, row_panel, column, row_count):
    breadth = mirror.shape[1]
    from_mirror = lax.dynamic_slice_in_dim(mirror, col_half * breadth, breadth, 0).T
    from_partner = lax.dynamic_slice_in_dim(partner, col_half * breadth, breadth, 0).T
    lower_part = jnp.where(
        col_half == 0,
        jnp.concatenate([from_mirror, from_partner], 0),
        jnp.concatenate([from_partner, from_mirror], 0),
    )
    block_rows = panel_blocks(row_panel, row_count)
    block_cols = column * CB + jnp.arange(CB, dtype=jnp.int32)
    strictly = (block_rows[:, None] > block_cols[None, :]).astype(lower_part.dtype)
    count_rows = block_rows.shape[0]
    lower_part = (lower_part.reshape(count_rows, BS, CB, BS) * strictly[:, None, :, None]).reshape(
        count_rows * BS, breadth
    )
    return upper_part + lower_part


def build_tile(stored_here, mirror_pack, partner_pack, pattern, row_panel, column, row_count):
    source_row = column % row_count
    col_half = column // row_count
    here_col = row_panel + row_count * col_half
    there_col = row_panel + row_count * (1 - col_half)
    upper_part = unpack(stored_here, tile_occupancy(pattern, row_panel, column, row_count))
    mirror = unpack(mirror_pack, tile_occupancy(pattern, source_row, here_col, row_count))
    partner = unpack(partner_pack, tile_occupancy(pattern, source_row, there_col, row_count))
    return assemble(upper_part, mirror, partner, col_half, row_panel, column, row_count)


def local(occupancy, stored):
    row_count = lax.axis_size("row")
    col_count = lax.axis_size("col")
    levels = row_count.bit_length() - 1
    my_row = lax.axis_index("row")
    my_col = lax.axis_index("col")
    my_half = my_col // row_count
    own_blocks = stored.reshape(SLOTS, BS, BS)
    symmetric = jnp.maximum(occupancy, occupancy.T)
    mirrored = own_blocks
    for bit_number in range(levels):
        crossed = from_partner_2(from_partner_2(mirrored, "row", bit_number), "col", bit_number)
        differ = my_row // (1 << bit_number) % 2 != my_col // (1 << bit_number) % 2
        mirrored = jnp.where(differ, crossed, mirrored)
    slab_rows = SR * BS
    skew_amount = my_col % row_count
    partner = passed_along(mirrored, "col", -row_count)
    own_tile = build_tile(own_blocks, mirrored, partner, occupancy, my_row, my_col, row_count)
    slab = own_tile[:slab_rows]
    carried = pack(own_tile, tile_occupancy(symmetric, my_row, my_col, row_count), 3 * SLOTS)
    for bit_number in range(levels):
        moved = from_behind(carried, "row", row_count - (1 << bit_number))
        carried = jnp.where(skew_amount // (1 << bit_number) % 2 == 1, moved, carried)
    factors = []
    for section in range(2):
        middle = (my_row + skew_amount + section) % row_count
        if section == 1:
            carried = from_behind(carried, "row", row_count - 1)
        factors.append(unpack(carried, tile_occupancy(symmetric, middle, my_col, row_count)))
    result = jnp.zeros((slab_rows, CB * BS), jnp.float32)
    opposite = from_partner_2(slab, "col", levels)
    panel_now = jnp.where(
        my_half == 0, jnp.concatenate([slab, opposite], 1), jnp.concatenate([opposite, slab], 1)
    )
    for bit_number in range(levels):
        moved = from_behind(panel_now, "col", col_count - (1 << bit_number))
        panel_now = jnp.where(my_row // (1 << bit_number) % 2 == 1, moved, panel_now)
    for section in range(2):
        if section == 1:
            panel_now = from_behind(panel_now, "col", col_count - 1)
        result = result + jnp.dot(panel_now, factors[section], preferred_element_type=jnp.float32)
    return result


def solution(mesh):
    placed = (P(), P("row", "col", None, None, None))
    return jax.shard_map(
        local, mesh=mesh, in_specs=placed, out_specs=P("row", "col"), check_vma=False
    )
```

profile of v0, /device:TPU:94, one launch (start us, length us, event | category | flops | bytes accessed | tf_op | source)
XLA Modules:
  0.0 969.6 jit_solution(8780118222391610266)
XLA Ops:
  0.8 24.4 %collective-permute-done = bf16[8,256,256]{2,1,0:T(8,128)(2,1)} collective-permute-done((bf16[8,256,256]{2,1,0:T(8,128)(2,1)}, bf16[8,256,256]{2,1,0:T(8,128)(2,1)}, u32[]{:S(2)}, u32[]{:S(2)}) %collective-permute-start) | collective-permute-done | bytes 1048608 | tf_op jit(solution)/shard_map/ppermute | solution.py:19
  35.8 20.6 %collective-permute-done.2 = bf16[8,256,256]{2,1,0:T(8,128)(2,1)} collective-permute-done((bf16[8,256,256]{2,1,0:T(8,128)(2,1)S(1)}, bf16[8,256,256]{2,1,0:T(8,128)(2,1)}, u32[]{:S(2)}, u32[]{:S(2)}) %collective-permute-start.2) | collective-permute-done | bytes 1048608 | tf_op jit(solution)/shard_map/ppermute | solution.py:19
  67.3 13.7 %collective-permute-done.3 = bf16[8,256,256]{2,1,0:T(8,128)(2,1)} collective-permute-done((bf16[8,256,256]{2,1,0:T(8,128)(2,1)}, bf16[8,256,256]{2,1,0:T(8,128)(2,1)}, u32[]{:S(2)}, u32[]{:S(2)}) %collective-permute-start.3) | collective-permute-done | bytes 1048608 | tf_op jit(solution)/shard_map/ppermute | solution.py:19
  82.4 14.2 %select_multiply_fusion.4 = bf16[128,256,256]{2,1,0:T(8,128)(2,1)} fusion(bf16[128,256,256]{2,1,0:T(8,128)(2,1)} %gather_fusion.2, pred[128]{0:T(512)(128)(4,1)S(1)} %compare_and_fusion.7, bf16[128]{0:T(256)(128)(2,1)S(1)} %convert_element_type.73), kind=kLoop, calls=%fused_computation.18 | loop fusion | flops 16777216 | bytes 33554816 | tf_op jit(solution)/shard_map/mul | solution.py:47
  96.7 10.8 %collective-permute-done.4 = bf16[8,256,256]{2,1,0:T(8,128)(2,1)} collective-permute-done((bf16[8,256,256]{2,1,0:T(8,128)(2,1)S(1)}, bf16[8,256,256]{2,1,0:T(8,128)(2,1)}, u32[]{:S(2)}, u32[]{:S(2)}) %collective-permute-start.4) | collective-permute-done | bytes 1048608 | tf_op jit(solution)/shard_map/ppermute | solution.py:19
  108.2 15.8 %copy.38 = bf16[16,256,8,256]{3,2,1,0:T(8,128)(2,1)S(1)} copy(bf16[16,256,8,256]{3,1,2,0:T(8,128)(2,1)} %bitcast.54) | data formatting | bytes 33554432 | tf_op jit(solution)/shard_map/transpose | solution.py:52
  124.0 9.7 %copy.56 = bf16[512,8,8,256]{3,1,2,0:T(8,128)(2,1)} copy(bf16[512,8,8,256]{3,2,1,0:T(8,128)(2,1)S(1)} %bitcast.66) | data formatting | bytes 33554432
  135.5 9.7 %copy.59 = bf16[512,8,8,256]{3,1,2,0:T(8,128)(2,1)} copy(bf16[512,8,8,256]{3,2,1,0:T(8,128)(2,1)S(1)} %bitcast.67) | data formatting | bytes 33554432
  166.4 41.7 %copy.40 = bf16[16,8,256,256]{3,1,2,0:T(8,128)(2,1)S(1)} copy(bf16[16,8,256,256]{3,2,1,0:T(8,128)(2,1)S(1)} %bitcast.58) | data formatting | bytes 33554432 | tf_op jit(solution)/shard_map/reshape | solution.py:51
  208.1 9.6 copy.57
  226.1 12.3 %copy.53 = bf16[2048,2048]{0,1:T(8,128)(2,1)} copy(bf16[2048,2048]{1,0:T(8,128)(2,1)} %constant_dynamic-slice_fusion.2) | data formatting | bytes 16777216
  255.0 41.7 %copy.43 = bf16[16,8,256,256]{3,1,2,0:T(8,128)(2,1)S(1)} copy(bf16[16,8,256,256]{3,2,1,0:T(8,128)(2,1)S(1)} %bitcast.59) | data formatting | bytes 33554432 | tf_op jit(solution)/shard_map/reshape | solution.py:51
  296.8 9.6 copy.58
  314.7 12.3 %copy.54 = bf16[2048,2048]{0,1:T(8,128)(2,1)} copy(bf16[2048,2048]{1,0:T(8,128)(2,1)} %constant_dynamic-slice_fusion) | data formatting | bytes 16777216
  327.0 13.3 %maximum_select_fusion = bf16[4096,2048]{1,0:T(8,128)(2,1)S(1)} fusion(bf16[2048,2048]{1,0:T(8,128)(2,1)} %bitcast.71, bf16[2048,2048]{1,0:T(8,128)(2,1)} %bitcast.70, pred[]{:T(512)S(6)} %eq.42), kind=kLoop, calls=%fused_computation.11 | loop fusion | flops 75497472 | bytes 33554432 | tf_op jit(solution)/shard_map/jit(_where)/select_n | solution.py:77
  346.3 45.9 %collective-permute-done.7 = bf16[512,2048]{1,0:T(8,128)(2,1)S(1)} collective-permute-done((bf16[512,2048]{1,0:T(8,128)(2,1)S(1)}, bf16[512,2048]{1,0:T(8,128)(2,1)S(1)}, u32[]{:S(2)}, u32[]{:S(2)}) %collective-permute-start.7) | collective-permute-done | bytes 2097184 | tf_op jit(solution)/shard_map/ppermute | solution.py:19
  397.3 10.8 %copy.60 = bf16[512,8,8,256]{3,2,1,0:T(8,128)(2,1)S(1)} copy(bf16[512,8,8,256]{3,1,2,0:T(8,128)(2,1)} %bitcast.56) | data formatting | bytes 33554432
  408.1 12.5 %fusion = bf16[16,256,8,256]{3,1,2,0:T(8,128)(2,1)} fusion(bf16[16,256,8,256]{3,1,2,0:T(8,128)(2,1)} %bitcast.55, bf16[16,256,8,256]{3,2,1,0:T(8,128)(2,1)S(1)} %bitcast.57, bf16[16,8]{1,0:T(8,128)(2,1)S(1)} %compare_convert_fusion), kind=kLoop, calls=%fused_computation.13 | loop fusion | flops 16777216 | bytes 50331904 | tf_op jit(solution)/shard_map/add | solution.py:89
  430.0 24.7 %collective-permute-done.8 = bf16[512,4096]{1,0:T(8,128)(2,1)} collective-permute-done((bf16[512,4096]{1,0:T(8,128)(2,1)}, bf16[512,4096]{1,0:T(8,128)(2,1)}, u32[]{:S(2)}, u32[]{:S(2)}) %collective-permute-start.8) | collective-permute-done | bytes 4194336 | tf_op jit(solution)/shard_map/ppermute | solution.py:31
  459.3 55.5 %collective-permute-start.9 = (bf16[512,4096]{1,0:T(8,128)(2,1)}, bf16[512,4096]{1,0:T(8,128)(2,1)}, u32[]{:S(2)}, u32[]{:S(2)}) collective-permute-start(bf16[512,4096]{1,0:T(8,128)(2,1)} %broadcast_select_fusion), channel_id=1, source_target_pairs={{2,0},{3,1},{4,2},{5,3},{6,4},{7,5},{8,6},{9,7},{10,8},{11,9},{12,... | collective-permute-start | bytes 12582920 | tf_op jit(solution)/shard_map/ppermute | solution.py:31
  516.9 155.8 %collective-permute-done.9 = bf16[512,4096]{1,0:T(8,128)(2,1)} collective-permute-done((bf16[512,4096]{1,0:T(8,128)(2,1)}, bf16[512,4096]{1,0:T(8,128)(2,1)}, u32[]{:S(2)}, u32[]{:S(2)}) %collective-permute-start.9) | collective-permute-done | bytes 4194336 | tf_op jit(solution)/shard_map/ppermute | solution.py:31
  682.2 70.1 %collective-permute-done.13 = bf16[24,256,256]{2,1,0:T(8,128)(2,1)} collective-permute-done((bf16[24,256,256]{2,1,0:T(8,128)(2,1)S(1)}, bf16[24,256,256]{2,1,0:T(8,128)(2,1)}, u32[]{:S(2)}, u32[]{:S(2)}) %collective-permute-start.13) | collective-permute-done | bytes 3145760 | tf_op jit(solution)/shard_map/ppermute | solution.py:31
  754.6 17.3 %collective-permute-done.10 = bf16[512,4096]{1,0:T(8,128)(2,1)} collective-permute-done((bf16[512,4096]{1,0:T(8,128)(2,1)}, bf16[512,4096]{1,0:T(8,128)(2,1)}, u32[]{:S(2)}, u32[]{:S(2)}) %collective-permute-start.10) | collective-permute-done | bytes 4194336 | tf_op jit(solution)/shard_map/ppermute | solution.py:31
  793.8 41.7 %copy.50 = bf16[16,256,8,256]{3,2,1,0:T(8,128)(2,1)S(1)} copy(bf16[16,256,8,256]{3,1,2,0:T(8,128)(2,1)S(1)} %bitcast.60) | data formatting | bytes 33554432 | tf_op jit(solution)/shard_map/transpose | solution.py:52
  835.6 9.7 %copy.61 = bf16[512,8,8,256]{3,1,2,0:T(8,128)(2,1)} copy(bf16[512,8,8,256]{3,2,1,0:T(8,128)(2,1)S(1)} %bitcast.64) | data formatting | bytes 33554432
  845.3 28.2 %collective-permute-done.15 = bf16[24,256,256]{2,1,0:T(8,128)(2,1)} collective-permute-done((bf16[24,256,256]{2,1,0:T(8,128)(2,1)S(1)}, bf16[24,256,256]{2,1,0:T(8,128)(2,1)}, u32[]{:S(2)}, u32[]{:S(2)}) %collective-permute-start.15) | collective-permute-done | bytes 3145760 | tf_op jit(solution)/shard_map/ppermute | solution.py:31
  873.5 10.2 %gather_fusion.10 = bf16[128,256,256]{2,1,0:T(8,128)(2,1)} fusion(bf16[24,256,256]{2,1,0:T(8,128)(2,1)} %collective-permute-done.15, s32[1024]{0:T(1024)S(1)} %pad_clamp_fusion), kind=kCustom, calls=%fused_computation.9.clone | custom fusion | bytes 33554944 | tf_op jit(solution)/shard_map/jit(_take)/gather | solution.py:47
  883.7 8.6 select_multiply_fusion
  892.3 41.7 %copy.52 = bf16[16,256,8,256]{3,2,1,0:T(8,128)(2,1)S(1)} copy(bf16[16,256,8,256]{3,1,2,0:T(8,128)(2,1)S(1)} %bitcast.61) | data formatting | bytes 33554432 | tf_op jit(solution)/shard_map/transpose | solution.py:52
  934.1 9.8 %copy.62 = bf16[512,8,8,256]{3,1,2,0:T(8,128)(2,1)} copy(bf16[512,8,8,256]{3,2,1,0:T(8,128)(2,1)S(1)} %bitcast.65) | data formatting | bytes 33554432
  943.8 13.0 %fusion.7 = f32[512,2048]{1,0:T(8,128)S(1)} fusion(bf16[512,4096]{1,0:T(8,128)(2,1)} %collective-permute-done.14, bf16[4096,2048]{1,0:T(8,128)(2,1)} %bitcast.78), kind=kOutput, calls=%fused_computation.99 | convolution fusion | flops 8589934592 | bytes 25165824 | tf_op jit(solution)/shard_map/dot_general | solution.py:143
  956.9 12.5 %convolution_add_fusion = f32[512,2048]{1,0:T(8,128)} fusion(f32[512,2048]{1,0:T(8,128)S(1)} %fusion.7, bf16[512,4096]{1,0:T(8,128)(2,1)} %broadcast_select_fusion.2, bf16[4096,2048]{1,0:T(8,128)(2,1)S(1)} %bitcast.77), kind=kOutput, calls=%fused_computation.23 | convolution fusion | flops 8590983168 | bytes 29360128 | tf_op jit(solution)/shard_map/dot_general | solution.py:143
  (140 shorter events, 140.9 us)
Async XLA Ops:
  0.0 58.0 %copy-start = (bf16[1,1,8,256,256]{4,3,2,1,0:T(8,128)(2,1)S(1)}, bf16[1,1,8,256,256]{4,3,2,1,0:T(8,128)(2,1)}, u32[]{:S(2)}) copy-start(bf16[1,1,8,256,256]{4,3,2,1,0:T(8,128)(2,1)} %param.9) | copy-start | bytes 3145732
  0.0 25.2 %collective-permute-start = (bf16[8,256,256]{2,1,0:T(8,128)(2,1)}, bf16[8,256,256]{2,1,0:T(8,128)(2,1)}, u32[]{:S(2)}, u32[]{:S(2)}) collective-permute-start(bf16[8,256,256]{2,1,0:T(8,128)(2,1)} %bitcast.52), channel_id=1, source_target_pairs={{0,16},{16,0},{32,48},{48,32},{64,80},{80,64},{96,112},{112,96},{1... | collective-permute-start | bytes 3145736 | tf_op jit(solution)/shard_map/ppermute | solution.py:19
  25.2 2.9 collective-permute-start.1
  29.4 26.9 %collective-permute-start.2 = (bf16[8,256,256]{2,1,0:T(8,128)(2,1)S(1)}, bf16[8,256,256]{2,1,0:T(8,128)(2,1)}, u32[]{:S(2)}, u32[]{:S(2)}) collective-permute-start(bf16[8,256,256]{2,1,0:T(8,128)(2,1)S(1)} %broadcast_select_fusion.6), channel_id=1, source_target_pairs={{0,32},{32,0},{16,48},{48,16},{64,96},{96,64},{80,112},{112,80},{1... | collective-permute-start | bytes 3145736 | tf_op jit(solution)/shard_map/ppermute | solution.py:19
  34.1 23.8 %copy-start.4 = (s32[128,128]{1,0:T(8,128)}, s32[128,128]{1,0:T(8,128)S(1)}, u32[]{:S(2)}) copy-start(s32[128,128]{1,0:T(8,128)S(1)} %bitcast_maximum_fusion) | copy-start | bytes 196612
  56.3 24.7 %collective-permute-start.3 = (bf16[8,256,256]{2,1,0:T(8,128)(2,1)}, bf16[8,256,256]{2,1,0:T(8,128)(2,1)}, u32[]{:S(2)}, u32[]{:S(2)}) collective-permute-start(bf16[8,256,256]{2,1,0:T(8,128)(2,1)} %collective-permute-done.2), channel_id=1, source_target_pairs={{0,2},{2,0},{1,3},{3,1},{4,6},{6,4},{5,7},{7,5},{8,10},{10,8},{9,1... | collective-permute-start | bytes 3145736 | tf_op jit(solution)/shard_map/ppermute | solution.py:19
  58.0 8.1 copy-start.3
  82.3 25.1 %collective-permute-start.4 = (bf16[8,256,256]{2,1,0:T(8,128)(2,1)S(1)}, bf16[8,256,256]{2,1,0:T(8,128)(2,1)}, u32[]{:S(2)}, u32[]{:S(2)}) collective-permute-start(bf16[8,256,256]{2,1,0:T(8,128)(2,1)S(1)} %broadcast_select_fusion.7), channel_id=1, source_target_pairs={{0,64},{64,0},{16,80},{80,16},{32,96},{96,32},{48,112},{112,48},{1... | collective-permute-start | bytes 3145736 | tf_op jit(solution)/shard_map/ppermute | solution.py:19
  107.5 38.4 %collective-permute-start.5 = (bf16[8,256,256]{2,1,0:T(8,128)(2,1)}, bf16[8,256,256]{2,1,0:T(8,128)(2,1)S(1)}, u32[]{:S(2)}, u32[]{:S(2)}) collective-permute-start(bf16[8,256,256]{2,1,0:T(8,128)(2,1)} %collective-permute-done.4), channel_id=1, source_target_pairs={{0,4},{4,0},{1,5},{5,1},{2,6},{6,2},{3,7},{7,3},{8,12},{12,8},{9,1... | collective-permute-start | bytes 3145736 | tf_op jit(solution)/shard_map/ppermute | solution.py:19
  146.0 92.4 %collective-permute-start.6 = (bf16[8,256,256]{2,1,0:T(8,128)(2,1)S(1)}, bf16[8,256,256]{2,1,0:T(8,128)(2,1)S(1)}, u32[]{:S(2)}, u32[]{:S(2)}) collective-permute-start(bf16[8,256,256]{2,1,0:T(8,128)(2,1)S(1)} %broadcast_select_fusion.8), channel_id=1, source_target_pairs={{8,0},{9,1},{10,2},{11,3},{12,4},{13,5},{14,6},{15,7},{24,16},{25,... | collective-permute-start | bytes 3145736 | tf_op jit(solution)/shard_map/ppermute | solution.py:25
  340.3 55.1 %copy-start.1 = (bf16[4096,2048]{1,0:T(8,128)(2,1)}, bf16[4096,2048]{1,0:T(8,128)(2,1)S(1)}, u32[]{:S(2)}) copy-start(bf16[4096,2048]{1,0:T(8,128)(2,1)S(1)} %maximum_select_fusion) | copy-start | bytes 50331652
  340.3 55.2 %copy-start.6 = (s32[16,8]{1,0:T(8,128)S(1)}, s32[16,8]{1,0:T(8,128)}, u32[]{:S(2)}) copy-start(s32[16,8]{1,0:T(8,128)} %get-tuple-element.28) | copy-start | bytes 1540
  346.2 46.0 %collective-permute-start.7 = (bf16[512,2048]{1,0:T(8,128)(2,1)S(1)}, bf16[512,2048]{1,0:T(8,128)(2,1)S(1)}, u32[]{:S(2)}, u32[]{:S(2)}) collective-permute-start(bf16[512,2048]{1,0:T(8,128)(2,1)S(1)} %slice_add_fusion), channel_id=1, source_target_pairs={{0,8},{8,0},{1,9},{9,1},{2,10},{10,2},{3,11},{11,3},{4,12},{12,4},... | collective-permute-start | bytes 6291464 | tf_op jit(solution)/shard_map/ppermute | solution.py:19
  395.4 59.3 %collective-permute-start.8 = (bf16[512,4096]{1,0:T(8,128)(2,1)}, bf16[512,4096]{1,0:T(8,128)(2,1)}, u32[]{:S(2)}, u32[]{:S(2)}) collective-permute-start(bf16[512,4096]{1,0:T(8,128)(2,1)} %maximum_select_fusion.1), channel_id=1, source_target_pairs={{1,0},{2,1},{3,2},{4,3},{5,4},{6,5},{7,6},{8,7},{9,8},{10,9},{11,1... | collective-permute-start | bytes 12582920 | tf_op jit(solution)/shard_map/ppermute | solution.py:31
  429.2 85.6 %collective-permute-start.11 = (bf16[24,256,256]{2,1,0:T(8,128)(2,1)}, bf16[24,256,256]{2,1,0:T(8,128)(2,1)}, u32[]{:S(2)}, u32[]{:S(2)}) collective-permute-start(bf16[24,256,256]{2,1,0:T(8,128)(2,1)} %select_multiply_fusion.5), channel_id=1, source_target_pairs={{16,0},{32,16},{48,32},{64,48},{80,64},{96,80},{112,96},{0,112},{1... | collective-permute-start | bytes 9437192 | tf_op jit(solution)/shard_map/ppermute | solution.py:31
  459.3 213.4 %collective-permute-start.9 = (bf16[512,4096]{1,0:T(8,128)(2,1)}, bf16[512,4096]{1,0:T(8,128)(2,1)}, u32[]{:S(2)}, u32[]{:S(2)}) collective-permute-start(bf16[512,4096]{1,0:T(8,128)(2,1)} %broadcast_select_fusion), channel_id=1, source_target_pairs={{2,0},{3,1},{4,2},{5,3},{6,4},{7,5},{8,6},{9,7},{10,8},{11,9},{12,... | collective-permute-start | bytes 12582920 | tf_op jit(solution)/shard_map/ppermute | solution.py:31
  516.9 160.6 %collective-permute-start.12 = (bf16[24,256,256]{2,1,0:T(8,128)(2,1)}, bf16[24,256,256]{2,1,0:T(8,128)(2,1)}, u32[]{:S(2)}, u32[]{:S(2)}) collective-permute-start(bf16[24,256,256]{2,1,0:T(8,128)(2,1)} %broadcast_select_fusion.3), channel_id=1, source_target_pairs={{32,0},{48,16},{64,32},{80,48},{96,64},{112,80},{0,96},{16,112},{3... | collective-permute-start | bytes 9437192 | tf_op jit(solution)/shard_map/ppermute | solution.py:31
  516.9 163.2 %copy-start.5 = (s32[128,128]{1,0:T(8,128)S(1)}, s32[128,128]{1,0:T(8,128)}, u32[]{:S(2)}) copy-start(s32[128,128]{1,0:T(8,128)} %copy-done.4) | copy-start | bytes 196612
  677.4 94.6 %collective-permute-start.10 = (bf16[512,4096]{1,0:T(8,128)(2,1)}, bf16[512,4096]{1,0:T(8,128)(2,1)}, u32[]{:S(2)}, u32[]{:S(2)}) collective-permute-start(bf16[512,4096]{1,0:T(8,128)(2,1)} %broadcast_select_fusion.1), channel_id=1, source_target_pairs={{4,0},{5,1},{6,2},{7,3},{8,4},{9,5},{10,6},{11,7},{12,8},{13,9},{1... | collective-permute-start | bytes 12582920 | tf_op jit(solution)/shard_map/ppermute | solution.py:31
  679.8 2.4 copy-start.2
  679.8 72.5 %collective-permute-start.13 = (bf16[24,256,256]{2,1,0:T(8,128)(2,1)S(1)}, bf16[24,256,256]{2,1,0:T(8,128)(2,1)}, u32[]{:S(2)}, u32[]{:S(2)}) collective-permute-start(bf16[24,256,256]{2,1,0:T(8,128)(2,1)S(1)} %broadcast_select_fusion.4), channel_id=1, source_target_pairs={{64,0},{80,16},{96,32},{112,48},{0,64},{16,80},{32,96},{48,112},{6... | collective-permute-start | bytes 9437192 | tf_op jit(solution)/shard_map/ppermute | solution.py:31
  754.5 119.0 %collective-permute-start.15 = (bf16[24,256,256]{2,1,0:T(8,128)(2,1)S(1)}, bf16[24,256,256]{2,1,0:T(8,128)(2,1)}, u32[]{:S(2)}, u32[]{:S(2)}) collective-permute-start(bf16[24,256,256]{2,1,0:T(8,128)(2,1)S(1)} %broadcast_select_fusion.5), channel_id=1, source_target_pairs={{16,0},{32,16},{48,32},{64,48},{80,64},{96,80},{112,96},{0,112},{1... | collective-permute-start | bytes 9437192 | tf_op jit(solution)/shard_map/ppermute | solution.py:31
  776.6 167.2 %collective-permute-start.14 = (bf16[512,4096]{1,0:T(8,128)(2,1)}, bf16[512,4096]{1,0:T(8,128)(2,1)}, u32[]{:S(2)}, u32[]{:S(2)}) collective-permute-start(bf16[512,4096]{1,0:T(8,128)(2,1)} %broadcast_select_fusion.2), channel_id=1, source_target_pairs={{1,0},{2,1},{3,2},{4,3},{5,4},{6,5},{7,6},{8,7},{9,8},{10,9},{11,1... | collective-permute-start | bytes 12582920 | tf_op jit(solution)/shard_map/ppermute | solution.py:31
  934.1 22.8 %slice-start = ((s8[16777216]{0:T(1024)(128)(4,1)}), s8[4194304]{0:T(1024)(128)(4,1)S(1)}, s32[]{:S(2)}) async-start(s8[16777216]{0:T(1024)(128)(4,1)} %bitcast.75), calls=%async_computation | async-start | bytes 8388608
  934.1 22.8 %slice-start.1 = ((s8[16777216]{0:T(1024)(128)(4,1)}), s8[4194304]{0:T(1024)(128)(4,1)S(1)}, s32[]{:S(2)}) async-start(s8[16777216]{0:T(1024)(128)(4,1)} %bitcast.75), calls=%async_computation.1 | async-start | bytes 8388608
  943.8 13.0 %slice-start.2 = ((s8[16777216]{0:T(1024)(128)(4,1)}), s8[4194304]{0:T(1024)(128)(4,1)S(1)}, s32[]{:S(2)}) async-start(s8[16777216]{0:T(1024)(128)(4,1)} %bitcast.75), calls=%async_computation.2 | async-start | bytes 8388608
  943.8 13.0 %slice-start.3 = ((s8[16777216]{0:T(1024)(128)(4,1)}), s8[4194304]{0:T(1024)(128)(4,1)S(1)}, s32[]{:S(2)}) async-start(s8[16777216]{0:T(1024)(128)(4,1)} %bitcast.75), calls=%async_computation.3 | async-start | bytes 8388608
where the time goes:
time: 978 us; the launch traced here: 970 us
  waiting for transfers between devices  414 us (42%)
  local copies, waits for them, and re-layouts  350 us (36%)
  other arithmetic  114 us (12%)
  starting transfers between devices  65.2 us (7%)
  matrix products  25.5 us (3%)
    ppermute x8, waiting for transfers between devices, from_behind(): return lax.ppermute(block, axis, route)  296 us
    ppermute x7, waiting for transfers between devices, from_partner_2(): return lax.ppermute(block, axis, route)  118 us
    transpose x3, local copies, waits for them, and re-layouts, unpack(): return pieces.reshape(row_blocks, col_blocks, edge, edge).transpose(0, 2,...  99.2 us
    unnamed x32, local copies, waits for them, and re-layouts  94.6 us
    reshape x2, local copies, waits for them, and re-layouts, unpack(): pieces.reshape(row_blocks, col_blocks, edge, edge).transpose(0, 2, 1, 3)  83.4 us
    ppermute x8, starting transfers between devices, from_behind(): return lax.ppermute(block, axis, route)  57 us
    mul x5, other arithmetic, unpack(): jnp.take(packed, position, axis=0)  48.7 us
    gather x5, local copies, waits for them, and re-layouts, unpack(): jnp.take(packed, position, axis=0)  42.7 us
  transfers between devices with their start and end apart: 16, of which 11 were waited for; matrix products, arithmetic and copies ran while one was open for 36% of the time, Pallas kernels for 0%

commit v1 on v0

v1 whole, which is shorter than its diff:
```python
import functools

import jax
import jax.numpy as jnp
import numpy as np
from jax import lax
from jax.experimental import pallas as pl
from jax.experimental.pallas import tpu as pltpu
from jax.sharding import PartitionSpec as P

BS = 256
CB = 8
SLOTS = 8
SR = 2
NB = 128
NR = 8
NC = 16
GROUPS = "ABCDEF"


def routes():
    plan = []
    for s in range(2):
        g = {n: [] for n in GROUPS}
        for a in range(NR):
            for b in range(NC):
                k = (a + b + s) % NR
                here = a * NC + b
                low = b < NR
                up = a <= k
                if not low or k <= b:
                    g["A"].append((k * NC + b, here))
                else:
                    g["B"].append((b * NC + k, here))
                if low:
                    g["C"].append((b * NC + k + NR, here))
                elif k + NR > b:
                    g["B"].append(((b - NR) * NC + k + NR, here))
                g["D" if low else "E"].append((a * NC + k + NR, here))
                name = {(False, True): "C", (False, False): "D", (True, True): "E", (True, False): "F"}[(low, up)]
                g[name].append((a * NC + k if up else k * NC + a, here))
        plan.append(g)
    return plan


def slot_table(occupancy):
    i = np.arange(NB)
    before_col = (i[:, None] // CB == i[None, :] // CB) & (i[:, None] < i[None, :])
    panel = i[:, None] // CB == i[None, :] // CB
    before_row = (i[:, None] // CB % NR == i[None, :] // CB % NR) & (i[None, :] < i[:, None])
    occ = occupancy.astype(jnp.float32)
    dot = functools.partial(jnp.dot, precision=lax.Precision.HIGHEST)
    rank = dot(occ, jnp.asarray(before_col, jnp.float32)) + dot(
        jnp.asarray(before_row, jnp.float32), dot(occ, jnp.asarray(panel, jnp.float32))
    )
    return jnp.where(occupancy == 1, rank.astype(jnp.int32), -1)


def product_kernel(table, *refs):
    bufs = refs[:12]
    out, tiles, left, sems = refs[12:]
    a = lax.axis_index("row")
    b = lax.axis_index("col")
    low = b < NR
    n = {g: i for i, g in enumerate(GROUPS)}

    def fetch(cond, s, name, kind):
        @pl.when(cond)
        def _():
            pltpu.make_async_copy(bufs[6 * s + n[name]], tiles.at[4 * s + kind], sems.at[4 * s + kind]).start()

    for s in range(2):
        k = lax.rem(a + b + s, NR)
        up = a <= k
        high = jnp.logical_not(low)
        straight = jnp.logical_or(high, k <= b)
        fetch(straight, s, "A", 0)
        fetch(jnp.logical_not(straight), s, "B", 0)
        fetch(low, s, "C", 1)
        fetch(jnp.logical_and(high, k + NR <= b), s, "A", 1)
        fetch(jnp.logical_and(high, k + NR > b), s, "B", 1)
        fetch(jnp.logical_and(low, up), s, "E", 2)
        fetch(jnp.logical_and(low, jnp.logical_not(up)), s, "F", 2)
        fetch(jnp.logical_and(high, up), s, "C", 2)
        fetch(jnp.logical_and(high, jnp.logical_not(up)), s, "D", 2)
        fetch(low, s, "D", 3)
        fetch(high, s, "E", 3)
    out[...] = jnp.zeros_like(out)
    for t in range(8):
        pltpu.make_async_copy(bufs[0], tiles.at[t], sems.at[t]).wait()

    def step(t, carry):
        s = t // 16
        kk = lax.rem(t, 16)
        half = kk // CB
        k = lax.rem(a + b + s, NR)
        inner = (half * NR + k) * CB + lax.rem(kk, CB)

        def one_row(i, carry):
            row = a * CB + i
            slot = table[jnp.minimum(row, inner), jnp.maximum(row, inner)]

            @pl.when(slot >= 0)
            def _():
                lt = tiles.at[4 * s + 2 + half, slot]

                @pl.when(row <= inner)
                def _():
                    left[...] = lt[...]

                @pl.when(row > inner)
                def _():
                    left[...] = lt[...].T

                def one_col(j, carry):
                    col = b * CB + j
                    rslot = table[jnp.minimum(inner, col), jnp.maximum(inner, col)]

                    @pl.when(rslot >= 0)
                    def _():
                        where = (
                            pl.ds(pl.multiple_of(i * BS, BS), BS),
                            pl.ds(pl.multiple_of(j * BS, BS), BS),
                        )
                        rt = tiles.at[4 * s + half, rslot]

                        @pl.when(inner <= col)
                        def _():
                            out[where] += jnp.dot(left[...], rt[...], preferred_element_type=jnp.float32)

                        @pl.when(inner > col)
                        def _():
                            out[where] += lax.dot_general(
                                left[...], rt[...], (((1,), (1,)), ((), ())), preferred_element_type=jnp.float32
                            )

                    return carry

                lax.fori_loop(0, CB, one_col, 0)

            return carry

        return lax.fori_loop(0, SR, one_row, carry)

    lax.fori_loop(0, 32, step, 0)


def local(occupancy, stored):
    own = stored.reshape(SLOTS, BS, BS)
    table = slot_table(occupancy)
    bufs = []
    for g in routes():
        for name in GROUPS:
            bufs.append(lax.ppermute(own, ("row", "col"), g[name]))
    return pl.pallas_call(
        product_kernel,
        out_shape=jax.ShapeDtypeStruct((SR * BS, CB * BS), jnp.float32),
        in_specs=[pl.BlockSpec(memory_space=pltpu.SMEM)] + [pl.BlockSpec(memory_space=pl.ANY)] * 12,
        out_specs=pl.BlockSpec(memory_space=pltpu.VMEM),
        scratch_shapes=[
            pltpu.VMEM((8, SLOTS, BS, BS), jnp.bfloat16),
            pltpu.VMEM((BS, BS), jnp.bfloat16),
            pltpu.SemaphoreType.DMA((8,)),
        ],
        compiler_params=pltpu.CompilerParams(vmem_limit_bytes=32 * 1024 * 1024),
        cost_estimate=pl.CostEstimate(flops=10**9, bytes_accessed=12 * 2**20, transcendentals=0),
        name="products",
    )(table, *bufs)


def solution(mesh):
    placed = (P(), P("row", "col", None, None, None))
    return jax.shard_map(
        local, mesh=mesh, in_specs=placed, out_specs=P("row", "col"), check_vma=False
    )
```

time: 978 us -> 254 us (0.26)
  the two profiles are of different devices: /device:TPU:94 before, /device:TPU:5 now
where the time goes in v1:
time: 254 us; the launch traced here: 253 us
  waiting for transfers between devices  228 us (90%)
  starting transfers between devices  13.2 us (5%)
  Pallas kernels  8 us (3%)
  matrix products  3.38 us (1%)
    ppermute x12, waiting for transfers between devices, local(): bufs.append(lax.ppermute(own, ('row', 'col'), g[name]))  228 us
    ppermute x12, starting transfers between devices, local(): bufs.append(lax.ppermute(own, ('row', 'col'), g[name]))  13.2 us
    pallas_call x1, Pallas kernels, local(): pl.pallas_call(product_kernel, out_shape=jax.ShapeDtypeStruct((SR * BS, C...  8 us
  transfers between devices with their start and end apart: 12, of which 3 were waited for; matrix products, arithmetic and copies ran while one was open for 1% of the time, Pallas kernels for 0%

profile of v1, /device:TPU:5, one launch (start us, length us, event | category | flops | bytes accessed | tf_op | source)
XLA Modules:
  0.0 252.8 jit_solution(12903915386970479216)
XLA Ops:
  0.0 0.7 collective-permute-start.11
  0.7 1.3 collective-permute-start.10
  2.0 1.3 collective-permute-start.9
  3.3 1.3 collective-permute-start.8
  4.6 1.3 collective-permute-start.7
  5.9 0.0 collective-permute-done.11.refs_11_
  5.9 0.7 collective-permute-start.6
  6.7 37.7 %collective-permute-done.10.refs_10_ = bf16[8,256,256]{2,1,0:T(8,128)(2,1)S(1)} collective-permute-done((bf16[8,256,256]{2,1,0:T(8,128)(2,1)}, bf16[8,256,256]{2,1,0:T(8,128)(2,1)S(1)}, u32[]{:S(2)}, u32[]{:S(2)}) %collective-permute-start.10) | collective-permute-done | bytes 1048608 | tf_op jit(solution)/shard_map/ppermute | solution.py:154
  44.4 0.7 collective-permute-start.5
  45.1 18.3 %collective-permute-done.9.refs_9_ = bf16[8,256,256]{2,1,0:T(8,128)(2,1)S(1)} collective-permute-done((bf16[8,256,256]{2,1,0:T(8,128)(2,1)}, bf16[8,256,256]{2,1,0:T(8,128)(2,1)S(1)}, u32[]{:S(2)}, u32[]{:S(2)}) %collective-permute-start.9) | collective-permute-done | bytes 1048608 | tf_op jit(solution)/shard_map/ppermute | solution.py:154
  63.5 1.3 collective-permute-start.4
  64.7 0.0 collective-permute-done.8.refs_8_
  64.8 1.3 collective-permute-start.3
  66.1 0.0 collective-permute-done.7.refs_7_
  66.1 1.3 collective-permute-start.2
  67.4 0.0 collective-permute-done.6.refs_6_
  67.4 1.3 collective-permute-start.1
  68.7 0.0 collective-permute-done.5.refs_5_
  68.7 0.7 collective-permute-start
  69.4 1.1 convolution_bitcast_fusion
  70.5 1.2 fusion.2
  71.7 1.1 fusion.1.table
  72.8 172.0 %collective-permute-done.4.refs_4_ = bf16[8,256,256]{2,1,0:T(8,128)(2,1)S(1)} collective-permute-done((bf16[8,256,256]{2,1,0:T(8,128)(2,1)}, bf16[8,256,256]{2,1,0:T(8,128)(2,1)S(1)}, u32[]{:S(2)}, u32[]{:S(2)}) %collective-permute-start.4) | collective-permute-done | bytes 1048608 | tf_op jit(solution)/shard_map/ppermute | solution.py:154
  244.8 0.0 collective-permute-done.3.refs_3_
  244.8 0.0 collective-permute-done.2.refs_2_
  244.8 0.0 collective-permute-done.1.refs_1_
  244.8 0.0 collective-permute-done.refs_0_
  244.8 8.0 %products.1 = f32[512,2048]{1,0:T(8,128)} custom-call(s32[128,128]{1,0:T(8,128)S(1)} %fusion.1.table, bf16[8,256,256]{2,1,0:T(8,128)(2,1)S(1)} %collective-permute-done.refs_0_, bf16[8,256,256]{2,1,0:T(8,128)(2,1)S(1)} %collective-permute-done.1.refs_1_, bf16[8,256,256]{2,1,0:T(8,128)(2,1)S(1)} %collective-permute-done.2.refs_2_, ...), custom_call_target="tpu_custom_call" | custom-call | flops 1000000000 | bytes 12582912 | tf_op jit(solution)/shard_map/products/pallas_call | solution.py:155
Async XLA Ops:
  0.0 5.9 %collective-permute-start.11 = (bf16[8,256,256]{2,1,0:T(8,128)(2,1)}, bf16[8,256,256]{2,1,0:T(8,128)(2,1)S(1)}, u32[]{:S(2)}, u32[]{:S(2)}) collective-permute-start(bf16[8,256,256]{2,1,0:T(8,128)(2,1)} %bitcast.7), channel_id=1, source_target_pairs={{1,22},{2,37},{18,38},{3,52},{19,53},{35,54},{4,67},{20,68},{36,69... | collective-permute-start | bytes 3145736 | tf_op jit(solution)/shard_map/ppermute | solution.py:154
  0.7 43.7 %collective-permute-start.10 = (bf16[8,256,256]{2,1,0:T(8,128)(2,1)}, bf16[8,256,256]{2,1,0:T(8,128)(2,1)S(1)}, u32[]{:S(2)}, u32[]{:S(2)}) collective-permute-start(bf16[8,256,256]{2,1,0:T(8,128)(2,1)} %bitcast.8), channel_id=1, source_target_pairs={{1,0},{2,1},{3,2},{4,3},{5,4},{6,5},{7,6},{0,7},{9,8},{10,9},{11,1... | collective-permute-start | bytes 3145736 | tf_op jit(solution)/shard_map/ppermute | solution.py:154
  2.0 61.4 %collective-permute-start.9 = (bf16[8,256,256]{2,1,0:T(8,128)(2,1)}, bf16[8,256,256]{2,1,0:T(8,128)(2,1)S(1)}, u32[]{:S(2)}, u32[]{:S(2)}) collective-permute-start(bf16[8,256,256]{2,1,0:T(8,128)(2,1)} %bitcast.9), channel_id=1, source_target_pairs={{9,0},{10,1},{11,2},{12,3},{13,4},{14,5},{15,6},{8,7},{26,16},{27,... | collective-permute-start | bytes 3145736 | tf_op jit(solution)/shard_map/ppermute | solution.py:154
  3.3 61.4 %collective-permute-start.8 = (bf16[8,256,256]{2,1,0:T(8,128)(2,1)}, bf16[8,256,256]{2,1,0:T(8,128)(2,1)S(1)}, u32[]{:S(2)}, u32[]{:S(2)}) collective-permute-start(bf16[8,256,256]{2,1,0:T(8,128)(2,1)} %bitcast.10), channel_id=1, source_target_pairs={{9,0},{26,1},{43,2},{60,3},{77,4},{94,5},{111,6},{120,7},{1,8},{2,... | collective-permute-start | bytes 3145736 | tf_op jit(solution)/shard_map/ppermute | solution.py:154
  4.6 61.4 %collective-permute-start.7 = (bf16[8,256,256]{2,1,0:T(8,128)(2,1)}, bf16[8,256,256]{2,1,0:T(8,128)(2,1)S(1)}, u32[]{:S(2)}, u32[]{:S(2)}) collective-permute-start(bf16[8,256,256]{2,1,0:T(8,128)(2,1)} %bitcast.11), channel_id=1, source_target_pairs={{1,0},{18,1},{35,2},{52,3},{69,4},{86,5},{103,6},{9,8},{26,9},{43,... | collective-permute-start | bytes 3145736 | tf_op jit(solution)/shard_map/ppermute | solution.py:154
  5.9 61.4 %collective-permute-start.6 = (bf16[8,256,256]{2,1,0:T(8,128)(2,1)}, bf16[8,256,256]{2,1,0:T(8,128)(2,1)S(1)}, u32[]{:S(2)}, u32[]{:S(2)}) collective-permute-start(bf16[8,256,256]{2,1,0:T(8,128)(2,1)} %bitcast.12), channel_id=1, source_target_pairs={{7,7},{24,8},{41,9},{58,10},{75,11},{92,12},{109,13},{126,14},{15,... | collective-permute-start | bytes 3145736 | tf_op jit(solution)/shard_map/ppermute | solution.py:154
  44.4 24.3 %collective-permute-start.5 = (bf16[8,256,256]{2,1,0:T(8,128)(2,1)}, bf16[8,256,256]{2,1,0:T(8,128)(2,1)S(1)}, u32[]{:S(2)}, u32[]{:S(2)}) collective-permute-start(bf16[8,256,256]{2,1,0:T(8,128)(2,1)} %bitcast.13), channel_id=1, source_target_pairs={{1,23},{2,38},{18,39},{3,53},{19,54},{35,55},{4,68},{20,69},{36,70... | collective-permute-start | bytes 3145736 | tf_op jit(solution)/shard_map/ppermute | solution.py:154
  63.5 181.3 %collective-permute-start.4 = (bf16[8,256,256]{2,1,0:T(8,128)(2,1)}, bf16[8,256,256]{2,1,0:T(8,128)(2,1)S(1)}, u32[]{:S(2)}, u32[]{:S(2)}) collective-permute-start(bf16[8,256,256]{2,1,0:T(8,128)(2,1)} %bitcast.14), channel_id=1, source_target_pairs={{0,0},{1,1},{2,2},{3,3},{4,4},{5,5},{6,6},{7,7},{8,8},{9,9},{10,10... | collective-permute-start | bytes 3145736 | tf_op jit(solution)/shard_map/ppermute | solution.py:154
  64.8 180.0 %collective-permute-start.3 = (bf16[8,256,256]{2,1,0:T(8,128)(2,1)}, bf16[8,256,256]{2,1,0:T(8,128)(2,1)S(1)}, u32[]{:S(2)}, u32[]{:S(2)}) collective-permute-start(bf16[8,256,256]{2,1,0:T(8,128)(2,1)} %bitcast.15), channel_id=1, source_target_pairs={{8,0},{9,1},{10,2},{11,3},{12,4},{13,5},{14,6},{15,7},{25,16},{26,... | collective-permute-start | bytes 3145736 | tf_op jit(solution)/shard_map/ppermute | solution.py:154
  66.1 178.7 %collective-permute-start.2 = (bf16[8,256,256]{2,1,0:T(8,128)(2,1)}, bf16[8,256,256]{2,1,0:T(8,128)(2,1)S(1)}, u32[]{:S(2)}, u32[]{:S(2)}) collective-permute-start(bf16[8,256,256]{2,1,0:T(8,128)(2,1)} %bitcast.16), channel_id=1, source_target_pairs={{8,0},{25,1},{42,2},{59,3},{76,4},{93,5},{110,6},{127,7},{0,8},{1,... | collective-permute-start | bytes 3145736 | tf_op jit(solution)/shard_map/ppermute | solution.py:154
  67.4 177.4 %collective-permute-start.1 = (bf16[8,256,256]{2,1,0:T(8,128)(2,1)}, bf16[8,256,256]{2,1,0:T(8,128)(2,1)S(1)}, u32[]{:S(2)}, u32[]{:S(2)}) collective-permute-start(bf16[8,256,256]{2,1,0:T(8,128)(2,1)} %bitcast.17), channel_id=1, source_target_pairs={{1,16},{18,17},{35,18},{52,19},{69,20},{86,21},{103,22},{9,24},{26... | collective-permute-start | bytes 3145736 | tf_op jit(solution)/shard_map/ppermute | solution.py:154
  68.7 176.1 %collective-permute-start = (bf16[8,256,256]{2,1,0:T(8,128)(2,1)}, bf16[8,256,256]{2,1,0:T(8,128)(2,1)S(1)}, u32[]{:S(2)}, u32[]{:S(2)}) collective-permute-start(bf16[8,256,256]{2,1,0:T(8,128)(2,1)} %bitcast.18), channel_id=1, source_target_pairs={{0,0},{17,1},{34,2},{51,3},{68,4},{85,5},{102,6},{119,7},{8,8},{25... | collective-permute-start | bytes 3145736 | tf_op jit(solution)/shard_map/ppermute | solution.py:154

commit v2 on v1

v2 whole, which is shorter than its diff:
```python
import functools

import jax
import jax.numpy as jnp
import numpy as np
from jax import lax
from jax.experimental import pallas as pl
from jax.experimental.pallas import tpu as pltpu
from jax.sharding import PartitionSpec as P

BS = 256
CB = 8
SLOTS = 8
SR = 2
NB = 128
NR = 8
NC = 16
ND = NR * NC
MIB = 1024 * 1024
FETCH = 640

FIRST = [
    [
        (1, 9, 1), (3, 48, 3), (4, 52, 4), (5, 4, 5), (6, 96, 6), (7, 113, 7), (10, 32, 10), (11, 75, 11),
        (13, 5, 13), (14, 104, 14), (15, 7, 15), (17, 39, 17), (18, 46, 18), (19, 18, 19), (20, 68, 20), (21, 91, 21),
        (22, 29, 22), (23, 21, 23), (24, 23, 24), (25, 24, 25), (26, 17, 26), (27, 26, 27), (28, 92, 28), (29, 28, 29),
        (30, 65, 30), (31, 22, 31), (35, 54, 35), (36, 41, 36), (37, 35, 37), (38, 100, 38), (39, 37, 39), (40, 45, 40),
        (41, 114, 41), (42, 122, 42), (43, 107, 43), (44, 33, 44), (45, 77, 45), (46, 78, 46), (47, 44, 47), (51, 63, 51),
        (52, 71, 52), (53, 86, 53), (54, 58, 54), (56, 67, 56), (57, 83, 57), (58, 10, 58), (59, 119, 59), (60, 57, 60),
        (61, 109, 61), (62, 50, 62), (63, 60, 63), (68, 64, 68), (69, 87, 69), (70, 20, 70), (71, 124, 71), (72, 76, 72),
        (73, 69, 73), (75, 70, 75), (76, 79, 76), (77, 72, 77), (78, 1, 78), (79, 36, 79), (85, 117, 85), (86, 103, 86),
        (87, 82, 87), (88, 53, 88), (89, 84, 89), (90, 93, 90), (91, 27, 91), (92, 101, 92), (93, 125, 93), (94, 80, 94),
        (95, 90, 95), (102, 118, 102), (103, 97, 103), (104, 88, 104), (105, 98, 105), (106, 99, 106), (107, 43, 107), (108, 47, 108),
        (109, 111, 109), (110, 14, 110), (119, 123, 119), (121, 105, 121), (122, 55, 122), (124, 127, 124), (127, 112, 127),
    ],
    [
        (1, 97, 1), (2, 16, 2), (3, 2, 3), (4, 48, 4), (5, 82, 5), (6, 5, 6), (7, 6, 7), (9, 1, 9),
        (10, 9, 10), (11, 56, 11), (14, 30, 14), (17, 113, 17), (18, 38, 18), (19, 54, 19), (20, 27, 20), (21, 69, 21),
        (22, 21, 22), (23, 121, 23), (24, 8, 24), (25, 20, 25), (26, 24, 26), (28, 19, 28), (29, 49, 29), (30, 73, 30),
        (31, 81, 31), (34, 51, 34), (35, 18, 35), (36, 100, 36), (37, 84, 37), (38, 99, 38), (39, 66, 39), (40, 37, 40),
        (41, 25, 41), (42, 39, 42), (43, 10, 43), (45, 43, 45), (46, 44, 46), (47, 108, 47), (51, 115, 51), (52, 3, 52),
        (53, 57, 53), (54, 50, 54), (55, 52, 55), (56, 40, 56), (57, 53, 57), (58, 62, 58), (59, 55, 59), (60, 28, 60),
        (61, 58, 61), (62, 35, 62), (69, 101, 69), (70, 102, 70), (71, 67, 71), (73, 41, 73), (74, 26, 74), (75, 116, 75),
        (76, 64, 76), (77, 4, 77), (78, 65, 78), (79, 75, 79), (85, 88, 85), (86, 80, 86), (87, 90, 87), (88, 91, 88),
        (89, 92, 89), (90, 72, 90), (91, 94, 91), (92, 86, 92), (93, 13, 93), (94, 78, 94), (95, 45, 95), (102, 22, 102),
        (103, 127, 103), (104, 98, 104), (105, 89, 105), (106, 74, 106), (107, 109, 107), (110, 126, 110), (111, 105, 111), (119, 7, 119),
        (121, 114, 121), (122, 123, 122), (123, 59, 123), (124, 117, 124), (126, 14, 126),
    ],
    [
        (0, 4, 0), (1, 22, 1), (2, 46, 2), (3, 10, 3), (4, 64, 4), (5, 37, 5), (6, 14, 6), (7, 23, 7),
        (8, 7, 8), (9, 105, 9), (10, 90, 10), (11, 2, 11), (12, 56, 12), (13, 45, 13), (15, 112, 15), (17, 16, 17),
        (18, 114, 18), (19, 26, 19), (20, 19, 20), (21, 20, 21), (22, 54, 22), (23, 97, 23), (24, 31, 24), (25, 121, 25),
        (26, 9, 26), (27, 18, 27), (28, 27, 28), (29, 73, 29), (30, 28, 30), (31, 89, 31), (34, 32, 34), (35, 62, 35),
        (36, 33, 36), (38, 36, 38), (39, 42, 39), (40, 98, 40), (41, 38, 41), (42, 47, 42), (43, 40, 43), (44, 41, 44),
        (46, 35, 46), (51, 3, 51), (52, 116, 52), (53, 49, 53), (54, 70, 54), (55, 51, 55), (56, 52, 56), (57, 61, 57),
        (58, 127, 58), (60, 124, 60), (62, 58, 62), (63, 79, 63), (68, 71, 68), (69, 65, 69), (70, 74, 70), (71, 117, 71),
        (72, 8, 72), (73, 77, 73), (74, 78, 74), (75, 11, 75), (76, 1, 76), (77, 12, 77), (78, 44, 78), (79, 66, 79),
        (85, 80, 85), (86, 21, 86), (87, 81, 87), (88, 83, 88), (89, 57, 89), (91, 101, 91), (93, 88, 93), (94, 24, 94),
        (95, 94, 95), (102, 111, 102), (103, 104, 103), (104, 43, 104), (105, 106, 105), (106, 108, 106), (107, 86, 107), (108, 110, 108),
        (109, 29, 109), (110, 96, 110), (111, 30, 111), (120, 113, 120), (121, 39, 121), (122, 115, 122), (123, 75, 123), (124, 60, 124),
        (125, 118, 125), (127, 122, 127),
    ],
    [
        (1, 16, 1), (2, 10, 2), (3, 67, 3), (4, 11, 4), (5, 12, 5), (6, 38, 6), (7, 15, 7), (8, 57, 8),
        (9, 24, 9), (10, 2, 10), (11, 48, 11), (12, 76, 12), (13, 88, 13), (14, 6, 14), (15, 120, 15), (17, 1, 17),
        (18, 25, 18), (19, 83, 19), (20, 33, 20), (21, 28, 21), (22, 81, 22), (23, 22, 23), (27, 107, 27), (28, 41, 28),
        (29, 19, 29), (30, 20, 30), (31, 47, 31), (34, 39, 34), (35, 32, 35), (36, 70, 36), (37, 42, 37), (38, 43, 38),
        (39, 123, 39), (41, 46, 41), (43, 26, 43), (44, 92, 44), (45, 34, 45), (46, 62, 46), (47, 36, 47), (52, 56, 52),
        (53, 50, 53), (54, 101, 54), (55, 116, 55), (56, 53, 56), (57, 9, 57), (58, 54, 58), (60, 3, 60), (61, 49, 61),
        (62, 94, 62), (68, 72, 68), (69, 117, 69), (70, 66, 70), (71, 87, 71), (72, 75, 72), (73, 84, 73), (74, 69, 74),
        (75, 79, 75), (76, 124, 76), (77, 65, 77), (78, 74, 78), (79, 60, 79), (85, 5, 85), (86, 89, 86), (87, 37, 87),
        (89, 73, 89), (90, 85, 90), (92, 95, 92), (93, 80, 93), (94, 29, 94), (95, 82, 95), (102, 103, 102), (103, 118, 103),
        (104, 105, 104), (105, 99, 105), (106, 58, 106), (107, 100, 107), (108, 109, 108), (109, 102, 109), (110, 111, 110), (111, 96, 111),
        (119, 112, 119), (120, 7, 120), (121, 122, 121), (122, 90, 122), (123, 115, 123), (125, 45, 125), (126, 119, 126), (127, 63, 127),
    ],
]
SECOND = [
    [
        (0, 112, 0), (1, 20, 78), (3, 11, 60), (4, 8, 0), (7, 0, 8), (9, 40, 10), (10, 2, 43), (12, 60, 12),
        (14, 13, 14), (15, 31, 15), (16, 1, 2), (18, 17, 18), (19, 33, 19), (20, 110, 70), (21, 5, 86), (22, 6, 102),
        (23, 22, 24), (24, 23, 25), (25, 24, 18), (26, 18, 43), (27, 26, 28), (28, 29, 30), (29, 28, 22), (30, 46, 30),
        (31, 30, 24), (32, 16, 10), (33, 49, 20), (35, 50, 37), (37, 117, 87), (38, 70, 38), (39, 36, 39), (40, 32, 43),
        (42, 43, 37), (43, 108, 38), (44, 66, 47), (45, 37, 95), (46, 47, 41), (47, 63, 47), (48, 12, 4), (50, 93, 53),
        (51, 114, 34), (52, 57, 52), (53, 101, 53), (54, 35, 54), (56, 79, 52), (57, 53, 89), (58, 59, 62), (59, 55, 123),
        (60, 48, 60), (61, 62, 57), (62, 41, 35), (63, 51, 63), (64, 67, 4), (65, 81, 30), (66, 82, 39), (68, 69, 20),
        (69, 72, 69), (70, 86, 54), (71, 52, 71), (72, 58, 90), (73, 27, 29), (74, 73, 78), (75, 56, 72), (76, 64, 12),
        (77, 109, 77), (78, 77, 74), (79, 75, 63), (80, 89, 94), (81, 125, 87), (82, 21, 95), (83, 61, 19), (84, 83, 89),
        (85, 42, 90), (86, 85, 53), (87, 4, 69), (88, 95, 85), (89, 91, 89), (90, 106, 10), (91, 90, 88), (92, 76, 28),
        (93, 92, 90), (94, 78, 62), (95, 111, 95), (96, 97, 111), (97, 96, 103), (99, 44, 38), (100, 84, 36), (101, 100, 54),
        (102, 104, 102), (103, 102, 86), (104, 88, 14), (105, 38, 105), (107, 25, 27), (109, 19, 61), (110, 103, 110), (112, 7, 127),
        (113, 120, 7), (114, 98, 41), (115, 116, 123), (116, 115, 55), (117, 71, 124), (118, 87, 125), (119, 118, 126), (120, 121, 120),
        (121, 113, 25), (122, 74, 122), (123, 122, 39), (125, 126, 125), (127, 99, 58),
    ],
    [
        (1, 0, 9), (3, 52, 3), (4, 7, 0), (7, 112, 8), (9, 8, 1), (10, 60, 3), (11, 10, 11), (12, 48, 12),
        (13, 95, 93), (15, 14, 7), (16, 98, 2), (17, 16, 26), (18, 2, 35), (19, 18, 20), (20, 84, 21), (21, 107, 22),
        (22, 23, 1), (23, 30, 23), (24, 5, 94), (25, 31, 25), (26, 25, 19), (27, 43, 91), (28, 27, 60), (29, 13, 94),
        (30, 22, 111), (31, 97, 24), (32, 33, 35), (33, 34, 44), (34, 47, 34), (37, 21, 87), (38, 39, 18), (39, 40, 34),
        (40, 24, 40), (41, 42, 44), (42, 92, 37), (43, 38, 104), (44, 36, 78), (45, 29, 125), (46, 45, 2), (47, 28, 108),
        (48, 32, 11), (49, 57, 29), (50, 19, 53), (51, 124, 55), (52, 49, 52), (54, 55, 35), (55, 3, 59), (56, 61, 56),
        (57, 41, 57), (58, 59, 54), (59, 11, 59), (60, 44, 124), (62, 63, 58), (64, 71, 76), (65, 64, 69), (66, 67, 79),
        (67, 75, 71), (69, 53, 21), (70, 77, 36), (71, 4, 68), (72, 73, 77), (73, 89, 30), (74, 70, 106), (75, 74, 79),
        (76, 72, 12), (77, 76, 73), (78, 66, 46), (79, 78, 75), (80, 81, 86), (81, 65, 22), (82, 91, 5), (83, 99, 57),
        (84, 69, 37), (87, 20, 69), (88, 87, 93), (89, 105, 31), (90, 126, 87), (91, 83, 21), (92, 108, 44), (94, 93, 91),
        (95, 94, 92), (96, 80, 6), (97, 113, 1), (98, 82, 40), (99, 50, 38), (100, 54, 38), (101, 109, 54), (102, 103, 109),
        (103, 118, 86), (104, 106, 104), (105, 121, 9), (108, 101, 108), (109, 35, 61), (110, 86, 108), (111, 110, 109), (112, 96, 15),
        (114, 1, 18), (115, 114, 122), (116, 100, 75), (117, 116, 124), (118, 6, 103), (119, 123, 59), (120, 104, 120), (121, 122, 23),
        (122, 119, 127), (124, 125, 71), (125, 117, 93), (126, 127, 126), (127, 115, 58),
    ],
    [
        (1, 4, 76), (2, 1, 10), (3, 19, 52), (4, 20, 77), (5, 72, 13), (6, 5, 14), (7, 23, 120), (9, 25, 57),
        (10, 11, 3), (12, 13, 5), (13, 12, 13), (14, 30, 126), (16, 32, 2), (17, 31, 17), (18, 17, 27), (19, 18, 28),
        (20, 86, 70), (21, 49, 21), (22, 38, 22), (23, 113, 24), (24, 21, 94), (25, 16, 25), (26, 62, 19), (27, 26, 20),
        (28, 27, 21), (29, 106, 22), (30, 6, 111), (31, 29, 31), (32, 99, 35), (34, 35, 45), (35, 34, 37), (36, 52, 79),
        (37, 103, 87), (38, 39, 41), (39, 55, 39), (40, 33, 43), (41, 42, 36), (43, 59, 107), (44, 110, 78), (46, 43, 46),
        (47, 90, 47), (48, 61, 3), (49, 65, 29), (50, 51, 62), (51, 2, 34), (52, 67, 55), (53, 37, 88), (54, 53, 19),
        (56, 60, 56), (57, 58, 53), (58, 54, 106), (59, 56, 59), (60, 44, 79), (61, 57, 61), (62, 50, 46), (63, 15, 127),
        (64, 116, 76), (65, 94, 69), (66, 114, 39), (67, 83, 56), (68, 76, 20), (69, 100, 74), (70, 69, 36), (71, 70, 52),
        (72, 68, 72), (73, 77, 29), (74, 73, 70), (75, 71, 123), (76, 3, 12), (77, 125, 77), (78, 74, 46), (79, 95, 79),
        (82, 64, 5), (83, 82, 88), (85, 84, 90), (86, 87, 92), (87, 118, 87), (88, 80, 13), (89, 88, 86), (90, 24, 10),
        (95, 28, 92), (96, 98, 6), (97, 81, 23), (98, 97, 104), (99, 66, 38), (100, 101, 107), (101, 85, 91), (102, 36, 70),
        (103, 22, 103), (104, 96, 14), (105, 89, 121), (106, 107, 106), (107, 123, 43), (109, 93, 61), (110, 104, 110), (111, 14, 111),
        (113, 112, 120), (115, 48, 51), (118, 117, 125), (119, 115, 59), (121, 9, 25), (122, 40, 42), (124, 108, 60), (127, 120, 127),
    ],
    [
        (1, 0, 1), (2, 3, 11), (3, 19, 60), (4, 53, 5), (5, 4, 13), (6, 22, 6), (7, 6, 15), (8, 15, 8),
        (9, 122, 26), (10, 9, 2), (11, 27, 75), (12, 28, 77), (13, 5, 93), (14, 13, 6), (16, 37, 2), (17, 24, 17),
        (18, 16, 18), (19, 49, 28), (20, 1, 25), (21, 20, 22), (22, 21, 31), (23, 39, 23), (24, 25, 26), (26, 84, 74),
        (27, 77, 20), (28, 33, 28), (30, 80, 14), (32, 115, 35), (33, 18, 36), (34, 50, 45), (36, 82, 47), (37, 38, 40),
        (38, 35, 38), (39, 23, 17), (40, 41, 43), (41, 57, 73), (42, 10, 42), (43, 42, 45), (44, 45, 47), (45, 46, 40),
        (46, 47, 18), (47, 97, 31), (48, 32, 3), (49, 61, 29), (50, 51, 54), (51, 55, 51), (52, 71, 55), (55, 59, 55),
        (56, 40, 11), (57, 120, 8), (58, 43, 62), (59, 63, 59), (60, 52, 63), (62, 58, 46), (64, 76, 4), (65, 64, 77),
        (66, 65, 70), (67, 66, 71), (68, 116, 68), (69, 68, 73), (70, 78, 36), (71, 36, 71), (73, 69, 89), (74, 109, 70),
        (75, 67, 72), (77, 93, 45), (78, 94, 78), (79, 12, 76), (80, 88, 94), (81, 99, 22), (82, 83, 5), (83, 17, 19),
        (84, 85, 37), (85, 87, 85), (86, 70, 107), (87, 95, 69), (88, 72, 88), (89, 110, 86), (90, 89, 95), (91, 86, 91),
        (92, 26, 44), (94, 81, 95), (95, 29, 95), (96, 106, 6), (97, 30, 1), (99, 100, 106), (101, 117, 92), (102, 118, 109),
        (103, 111, 86), (104, 105, 103), (105, 54, 105), (106, 107, 105), (107, 91, 27), (108, 74, 47), (109, 108, 107), (110, 44, 108),
        (111, 127, 111), (113, 96, 7), (114, 98, 18), (115, 56, 51), (116, 123, 55), (117, 73, 69), (118, 103, 125), (119, 48, 59),
        (120, 104, 15), (121, 113, 23), (122, 114, 42), (124, 125, 124), (127, 126, 103),
    ],
    [
        (0, 15, 0), (1, 16, 9), (3, 78, 52), (4, 68, 4), (5, 90, 5), (7, 121, 7), (8, 52, 72), (9, 8, 9),
        (10, 26, 58), (11, 75, 4), (12, 4, 12), (13, 64, 13), (14, 6, 110), (15, 14, 15), (16, 82, 2), (17, 1, 26),
        (18, 33, 27), (19, 20, 29), (20, 21, 30), (21, 29, 23), (22, 31, 1), (24, 106, 26), (25, 9, 41), (26, 42, 74),
        (28, 19, 21), (29, 13, 109), (30, 62, 30), (31, 30, 31), (32, 40, 35), (33, 34, 36), (35, 36, 46), (36, 37, 47),
        (37, 44, 39), (38, 105, 6), (39, 23, 121), (41, 57, 28), (42, 45, 39), (44, 28, 78), (45, 61, 13), (46, 38, 2),
        (47, 2, 42), (48, 53, 3), (49, 50, 61), (50, 35, 53), (51, 60, 55), (52, 48, 52), (53, 54, 57), (54, 55, 58),
        (55, 39, 122), (56, 11, 12), (57, 56, 60), (58, 27, 61), (60, 49, 60), (62, 63, 35), (63, 59, 63), (64, 3, 4),
        (65, 66, 78), (66, 115, 39), (67, 83, 3), (68, 84, 20), (69, 65, 21), (70, 71, 75), (71, 74, 71), (72, 79, 68),
        (74, 70, 74), (75, 91, 11), (76, 72, 76), (77, 58, 45), (78, 126, 94), (79, 67, 63), (80, 81, 94), (81, 98, 22),
        (82, 80, 5), (83, 99, 19), (84, 93, 37), (85, 69, 90), (86, 94, 53), (87, 86, 69), (88, 22, 104), (89, 73, 105),
        (90, 89, 87), (91, 92, 21), (92, 18, 44), (94, 110, 94), (95, 12, 92), (96, 97, 6), (97, 114, 23), (99, 107, 38),
        (101, 108, 54), (102, 101, 70), (103, 96, 102), (104, 46, 14), (105, 104, 111), (107, 41, 27), (109, 43, 61), (110, 102, 108),
        (112, 127, 119), (113, 112, 7), (114, 113, 121), (115, 124, 123), (116, 100, 52), (117, 116, 71), (118, 119, 103), (119, 103, 126),
        (122, 32, 42), (123, 120, 119), (126, 118, 110), (127, 87, 124),
    ],
]
NRELAY = 4
NBUF = 1 + len(FIRST) + len(SECOND)


def holders():
    held = [{d: 0} for d in range(ND)]
    for n, edges in enumerate(FIRST):
        for _, there, tile in edges:
            held[there].setdefault(tile, 1 + n)
    source = np.zeros((len(SECOND), ND), np.int32)
    for n, edges in enumerate(SECOND):
        for here, _, tile in edges:
            source[n, here] = held[here][tile]
    for n, edges in enumerate(SECOND):
        for _, there, tile in edges:
            held[there].setdefault(tile, 1 + len(FIRST) + n)
    place = np.zeros((ND, 8), np.int32)
    for a in range(NR):
        for b in range(NC):
            for s in range(2):
                k = (a + b + s) % NR
                low = b < NR
                need = [
                    (k, b) if not low or k <= b else (b, k),
                    (b, k + NR) if low else (k, b) if k + NR <= b else (b - NR, k + NR),
                    (a, k) if a <= k else (k, a),
                    (a, k + NR),
                ]
                d = a * NC + b
                for kind, (r, c) in enumerate(need):
                    place[d, 4 * s + kind] = held[d][r * NC + c]
    return source, place


def slot_table(occupancy):
    i = np.arange(NB)
    before_col = (i[:, None] // CB == i[None, :] // CB) & (i[:, None] < i[None, :])
    panel = i[:, None] // CB == i[None, :] // CB
    before_row = (i[:, None] // CB % NR == i[None, :] // CB % NR) & (i[None, :] < i[:, None])
    occ = occupancy.astype(jnp.float32)
    dot = functools.partial(jnp.dot, precision=lax.Precision.HIGHEST)
    rank = dot(occ, jnp.asarray(before_col, jnp.float32)) + dot(
        jnp.asarray(before_row, jnp.float32), dot(occ, jnp.asarray(panel, jnp.float32))
    )
    return jnp.where(occupancy == 1, rank.astype(jnp.int32), -1)


def pick_kernel(source, lists, *refs):
    bufs, outs, sems = refs[: 1 + NRELAY], refs[1 + NRELAY : -1], refs[-1]
    here = lax.axis_index("row") * NC + lax.axis_index("col")
    for n, out in enumerate(outs):
        which = source[n * ND + here]
        for i in range(1 + NRELAY):

            @pl.when(which == i)
            def _():
                pltpu.make_async_copy(bufs[i], out, sems.at[n]).start()

    for n, out in enumerate(outs):
        pltpu.make_async_copy(bufs[0], out, sems.at[n]).wait()


def index_kernel(table, place, lists, blank, used):
    a = lax.axis_index("row")
    b = lax.axis_index("col")
    here = a * NC + b
    blank[...] = jnp.zeros_like(blank)

    def clear_used(t, carry):
        used[t] = 0
        return carry

    lax.fori_loop(0, 80, clear_used, 0)

    def step(t, n):
        s = t // 32
        kk = lax.rem(t // 2, 16)
        i = lax.rem(t, 2)
        half = kk // CB
        k = lax.rem(a + b + s, NR)
        inner = (half * NR + k) * CB + lax.rem(kk, CB)
        row = a * CB + i
        lslot = table[jnp.minimum(row, inner), jnp.maximum(row, inner)]
        lplace = (4 * s + 2 + half) * SLOTS + lslot
        turned = jnp.where(row > inner, 1, 0)

        def one_col(j, n0):
            n, fresh = n0
            col = b * CB + j
            rslot = table[jnp.minimum(inner, col), jnp.maximum(inner, col)]
            rplace = (4 * s + half) * SLOTS + rslot
            hit = rslot >= 0

            @pl.when(hit)
            def _():
                first = jnp.where(used[64 + i * CB + j] == 0, 1, 0)
                lists[n] = (
                    lplace
                    + (rplace << 6)
                    + ((i * CB + j) << 12)
                    + (turned << 16)
                    + (jnp.where(inner > col, 1, 0) << 17)
                    + (fresh << 18)
                    + (first << 19)
                )
                used[64 + i * CB + j] = 1
                used[lplace] = 1
                used[rplace] = 1

            one = jnp.where(hit, 1, 0)
            return n + one, fresh * (1 - one)

        return lax.cond(lslot >= 0, lambda m: lax.fori_loop(0, CB, one_col, (m, 1))[0], lambda m: m, n)

    count = lax.fori_loop(0, 64, step, 1)
    lists[0] = count
    for t in range(16):
        lists[FETCH + 112 + t] = used[64 + t]

    def by_buffer(buf, n):
        lists[FETCH + buf] = n

        def by_kind(kind, n):
            def by_slot(slot, n):
                @pl.when(used[kind * SLOTS + slot] == 1)
                def _():
                    lists[FETCH + n] = kind * SLOTS + slot

                return n + used[kind * SLOTS + slot]

            return lax.cond(
                place[here * 8 + kind] == buf, lambda m: lax.fori_loop(0, SLOTS, by_slot, m), lambda m: m, n
            )

        return lax.fori_loop(0, 8, by_kind, n)

    lists[FETCH + NBUF] = lax.fori_loop(0, NBUF, by_buffer, 32)


def product_kernel(lists, *refs):
    bufs = refs[:NBUF]
    blank, out, tiles, left, acc, sems, out_sems = refs[NBUF:]
    for n, buf in enumerate(bufs):

        def start(q, carry):
            t = lists[FETCH + q]
            pltpu.make_async_copy(buf.at[lax.rem(t, SLOTS)], tiles.at[t], sems.at[t]).start()
            return carry

        lax.fori_loop(lists[FETCH + n], lists[FETCH + n + 1], start, 0)

    def finish(q, carry):
        t = lists[FETCH + q]
        pltpu.make_async_copy(bufs[0].at[0], tiles.at[t], sems.at[t]).wait()
        return carry

    lax.fori_loop(32, lists[FETCH + NBUF], finish, 0)

    def product(q, carry):
        code = lists[q]
        lt = tiles.at[code & 63]
        rt = tiles.at[(code >> 6) & 63]
        to = acc.at[(code >> 12) & 15]

        @pl.when(((code >> 18) & 1) == 1)
        def _():
            @pl.when(((code >> 16) & 1) == 0)
            def _():
                left[...] = lt[...]

            @pl.when(((code >> 16) & 1) == 1)
            def _():
                left[...] = lt[...].T

        @pl.when(((code >> 19) & 1) == 1)
        def _():
            to[...] = jnp.zeros_like(to)

        @pl.when(((code >> 17) & 1) == 0)
        def _():
            to[...] += jnp.dot(left[...], rt[...], preferred_element_type=jnp.float32)

        @pl.when(((code >> 17) & 1) == 1)
        def _():
            to[...] += lax.dot_general(
                left[...], rt[...], (((1,), (1,)), ((), ())), preferred_element_type=jnp.float32
            )

        return carry

    lax.fori_loop(1, lists[0], product, 0)

    def copy_out(t):
        return pltpu.make_async_copy(
            acc.at[t], out.at[pl.ds(t // CB * BS, BS), pl.ds(t % CB * BS, BS)], out_sems.at[t]
        )

    for t in range(16):

        @pl.when(lists[FETCH + 112 + t] == 1)
        def _():
            copy_out(t).start()

    for t in range(16):

        @pl.when(lists[FETCH + 112 + t] == 1)
        def _():
            copy_out(t).wait()


def tile_shape():
    return jax.ShapeDtypeStruct((SLOTS, BS, BS), jnp.bfloat16)


SMEM = pl.BlockSpec(memory_space=pltpu.SMEM)
ANY = pl.BlockSpec(memory_space=pl.ANY)


def local(occupancy, stored):
    own = stored.reshape(SLOTS, BS, BS)
    source, place = holders()
    bufs = [own]
    for edges in FIRST:
        bufs.append(lax.ppermute(own, ("row", "col"), [(u, v) for u, v, _ in edges]))
    lists, blank = pl.pallas_call(
        index_kernel,
        out_shape=(
            jax.ShapeDtypeStruct((FETCH + 128,), jnp.int32),
            jax.ShapeDtypeStruct((SR * BS, CB * BS), jnp.float32),
        ),
        in_specs=[SMEM, SMEM],
        out_specs=(SMEM, pl.BlockSpec(memory_space=pltpu.VMEM)),
        scratch_shapes=[pltpu.SMEM((80,), jnp.int32)],
        cost_estimate=pl.CostEstimate(flops=10**9, bytes_accessed=4 * MIB, transcendentals=0),
        name="index",
    )(slot_table(occupancy), jnp.asarray(place.reshape(-1)))
    flat_source = jnp.asarray(source.reshape(-1))
    sends = pl.pallas_call(
        pick_kernel,
        out_shape=[tile_shape()] * len(SECOND),
        in_specs=[SMEM, SMEM] + [ANY] * (1 + NRELAY),
        out_specs=[pl.BlockSpec(memory_space=pltpu.VMEM)] * len(SECOND),
        scratch_shapes=[pltpu.SemaphoreType.DMA((len(SECOND),))],
        cost_estimate=pl.CostEstimate(flops=0, bytes_accessed=2 * MIB, transcendentals=0),
        name="pick",
    )(flat_source, lists, *bufs[: 1 + NRELAY])
    later = [
        lax.ppermute(send, ("row", "col"), [(u, v) for u, v, _ in edges])
        for send, edges in zip(sends, SECOND, strict=True)
    ]
    bufs += later
    return pl.pallas_call(
        product_kernel,
        out_shape=jax.ShapeDtypeStruct((SR * BS, CB * BS), jnp.float32),
        in_specs=[SMEM] + [ANY] * (NBUF + 1),
        out_specs=ANY,
        scratch_shapes=[
            pltpu.VMEM((64, BS, BS), jnp.bfloat16),
            pltpu.VMEM((BS, BS), jnp.bfloat16),
            pltpu.VMEM((16, BS, BS), jnp.float32),
            pltpu.SemaphoreType.DMA((64,)),
            pltpu.SemaphoreType.DMA((16,)),
        ],
        input_output_aliases={1 + NBUF: 0},
        compiler_params=pltpu.CompilerParams(vmem_limit_bytes=60 * MIB),
        cost_estimate=pl.CostEstimate(flops=10**9, bytes_accessed=12 * MIB, transcendentals=0),
        name="products",
    )(lists, *bufs, blank)


def solution(mesh):
    placed = (P(), P("row", "col", None, None, None))
    return jax.shard_map(
        local, mesh=mesh, in_specs=placed, out_specs=P("row", "col"), check_vma=False
    )
```

time: 254 us -> 110 us (0.43)
  the two profiles are of different devices: /device:TPU:5 before, /device:TPU:41 now
where the time goes in v2:
time: 110 us; the launch traced here: 109 us
  waiting for transfers between devices  48.9 us (44%)
  starting transfers between devices  36.1 us (33%)
  Pallas kernels  20.1 us (18%)
  matrix products  4 us (4%)
    ppermute x5, waiting for transfers between devices, local(): lax.ppermute(send, ('row', 'col'), [(u, v) for u, v, _ in edges])  27.1 us
    ppermute x5, starting transfers between devices, local(): lax.ppermute(send, ('row', 'col'), [(u, v) for u, v, _ in edges])  24.1 us
    ppermute x4, waiting for transfers between devices, local(): lax.ppermute(own, ('row', 'col'), [(u, v) for u, v, _ in edges])  21.8 us
    ppermute x4, starting transfers between devices, local(): lax.ppermute(own, ('row', 'col'), [(u, v) for u, v, _ in edges])  12 us
    pallas_call x1, Pallas kernels, local(): pl.pallas_call(index_kernel, out_shape=(jax.ShapeDtypeStruct((FETCH + 128...  9.52 us
    pallas_call x1, Pallas kernels, local(): pl.pallas_call(pick_kernel, out_shape=[tile_shape()] * len(SECOND), in_sp...  5.69 us
    pallas_call x1, Pallas kernels, local(): pl.pallas_call(product_kernel, out_shape=jax.ShapeDtypeStruct((SR * BS, C...  4.86 us
  transfers between devices with their start and end apart: 9, of which 7 were waited for; matrix products, arithmetic and copies ran while one was open for 4% of the time, Pallas kernels for 9%

profile of v2, /device:TPU:41, one launch (start us, length us, event | category | flops | bytes accessed | tf_op | source)
XLA Modules:
  0.0 109.2 jit_solution(3506894727423050787)
XLA Ops:
  0.0 3.9 %collective-permute-start.3 = (bf16[8,256,256]{2,1,0:T(8,128)(2,1)}, bf16[8,256,256]{2,1,0:T(8,128)(2,1)S(1)}, u32[]{:S(2)}, u32[]{:S(2)}) collective-permute-start(bf16[8,256,256]{2,1,0:T(8,128)(2,1)} %bitcast.7), channel_id=1, source_target_pairs={{1,16},{2,10},{3,67},{4,11},{5,12},{6,38},{7,15},{8,57},{9,24},{10... | collective-permute-start | bytes 3145736 | tf_op jit(solution)/shard_map/ppermute | solution.py:381
  3.9 1.9 %collective-permute-start.2 = (bf16[8,256,256]{2,1,0:T(8,128)(2,1)}, bf16[8,256,256]{2,1,0:T(8,128)(2,1)S(1)}, u32[]{:S(2)}, u32[]{:S(2)}) collective-permute-start(bf16[8,256,256]{2,1,0:T(8,128)(2,1)} %bitcast.8), channel_id=1, source_target_pairs={{0,4},{1,22},{2,46},{3,10},{4,64},{5,37},{6,14},{7,23},{8,7},{9,10... | collective-permute-start | bytes 3145736 | tf_op jit(solution)/shard_map/ppermute | solution.py:381
  5.9 4.2 %collective-permute-start.1 = (bf16[8,256,256]{2,1,0:T(8,128)(2,1)}, bf16[8,256,256]{2,1,0:T(8,128)(2,1)S(1)}, u32[]{:S(2)}, u32[]{:S(2)}) collective-permute-start(bf16[8,256,256]{2,1,0:T(8,128)(2,1)} %bitcast.9), channel_id=1, source_target_pairs={{1,97},{2,16},{3,2},{4,48},{5,82},{6,5},{7,6},{9,1},{10,9},{11,56}... | collective-permute-start | bytes 3145736 | tf_op jit(solution)/shard_map/ppermute | solution.py:381
  10.1 1.9 %collective-permute-start = (bf16[8,256,256]{2,1,0:T(8,128)(2,1)}, bf16[8,256,256]{2,1,0:T(8,128)(2,1)}, u32[]{:S(2)}, u32[]{:S(2)}) collective-permute-start(bf16[8,256,256]{2,1,0:T(8,128)(2,1)} %bitcast.10), channel_id=1, source_target_pairs={{1,9},{3,48},{4,52},{5,4},{6,96},{7,113},{10,32},{11,75},{13,5},{1... | collective-permute-start | bytes 3145736 | tf_op jit(solution)/shard_map/ppermute | solution.py:381
  12.0 1.1 convolution_bitcast_fusion
  13.1 1.2 %fusion.2 = f32[128,128]{1,0:T(8,128)S(1)} fusion(f32[128,128]{1,0:T(8,128)} %constant.16.clone, s32[128,128]{1,0:T(8,128)} %param.7), kind=kOutput, calls=%fused_computation.4 | convolution fusion | flops 25182208 | bytes 196608 | tf_op jit(solution)/shard_map/dot_general | solution.py:200
  14.3 1.8 %fusion.1.table = s32[128,128]{1,0:T(8,128)} fusion(f32[128,128]{1,0:T(8,128)S(1)} %convolution_bitcast_fusion, f32[128,128]{1,0:T(8,128)} %constant.15.clone, f32[128,128]{1,0:T(8,128)S(1)} %fusion.2, s32[128,128]{1,0:T(8,128)} %param.7), kind=kOutput, calls=%fused_computation.2 | convolution fusion | flops 25231360 | bytes 327680 | tf_op jit(solution)/shard_map/dot_general | solution.py:199
  16.0 9.5 %index.1 = (s32[768]{0:T(1024)}, f32[512,2048]{1,0:T(8,128)}) custom-call(s32[128,128]{1,0:T(8,128)} %fusion.1.table, s32[1024]{0:T(1024)} %constant.17.clone.place), custom_call_target="tpu_custom_call" | custom-call | flops 1000000000 | bytes 4194304 | tf_op jit(solution)/shard_map/index/pallas_call | solution.py:382
  25.6 0.9 collective-permute-done.3.refs_4_
  26.5 0.0 copy-start
  26.5 2.7 %collective-permute-done.2.refs_3_ = bf16[8,256,256]{2,1,0:T(8,128)(2,1)S(1)} collective-permute-done((bf16[8,256,256]{2,1,0:T(8,128)(2,1)}, bf16[8,256,256]{2,1,0:T(8,128)(2,1)S(1)}, u32[]{:S(2)}, u32[]{:S(2)}) %collective-permute-start.2) | collective-permute-done | bytes 1048608 | tf_op jit(solution)/shard_map/ppermute | solution.py:381
  29.2 0.0 copy-start.1
  29.2 2.3 %collective-permute-done.1.refs_2_ = bf16[8,256,256]{2,1,0:T(8,128)(2,1)S(1)} collective-permute-done((bf16[8,256,256]{2,1,0:T(8,128)(2,1)}, bf16[8,256,256]{2,1,0:T(8,128)(2,1)S(1)}, u32[]{:S(2)}, u32[]{:S(2)}) %collective-permute-start.1) | collective-permute-done | bytes 1048608 | tf_op jit(solution)/shard_map/ppermute | solution.py:381
  31.5 15.9 %collective-permute-done.refs_1_ = bf16[8,256,256]{2,1,0:T(8,128)(2,1)} collective-permute-done((bf16[8,256,256]{2,1,0:T(8,128)(2,1)}, bf16[8,256,256]{2,1,0:T(8,128)(2,1)}, u32[]{:S(2)}, u32[]{:S(2)}) %collective-permute-start) | collective-permute-done | bytes 1048608 | tf_op jit(solution)/shard_map/ppermute | solution.py:381
  47.4 0.0 copy-done
  47.4 0.0 copy-done.1
  47.4 0.0 copy-done.2
  47.4 5.7 %pick.1 = (bf16[8,256,256]{2,1,0:T(8,128)(2,1)}, bf16[8,256,256]{2,1,0:T(8,128)(2,1)}, bf16[8,256,256]{2,1,0:T(8,128)(2,1)}, bf16[8,256,256]{2,1,0:T(8,128)(2,1)}, bf16[8,256,256]{2,1,0:T(8,128)(2,1)}) custom-call(s32[640]{0:T(1024)} %constant.18.clone.source, s32[768]{0:T(1024)} %get-tuple-element.12.lists, bf16[8,256,256]{2,1,0:T(8,128)(2,1)} %bitcast.11, ...), custom_call_target="tpu_custom_call" | custom-call | bytes 2097152 | tf_op jit(solution)/shard_map/pick/pallas_call | solution.py:395
  53.1 1.9 %collective-permute-start.4 = (bf16[8,256,256]{2,1,0:T(8,128)(2,1)}, bf16[8,256,256]{2,1,0:T(8,128)(2,1)S(1)}, u32[]{:S(2)}, u32[]{:S(2)}) collective-permute-start(bf16[8,256,256]{2,1,0:T(8,128)(2,1)} %get-tuple-element.13), channel_id=1, source_target_pairs={{0,112},{1,20},{3,11},{4,8},{7,0},{9,40},{10,2},{12,60},{14,13},{1... | collective-permute-start | bytes 3145736 | tf_op jit(solution)/shard_map/ppermute | solution.py:405
  55.0 6.7 %collective-permute-start.5 = (bf16[8,256,256]{2,1,0:T(8,128)(2,1)}, bf16[8,256,256]{2,1,0:T(8,128)(2,1)S(1)}, u32[]{:S(2)}, u32[]{:S(2)}) collective-permute-start(bf16[8,256,256]{2,1,0:T(8,128)(2,1)} %get-tuple-element.14), channel_id=1, source_target_pairs={{1,0},{3,52},{4,7},{7,112},{9,8},{10,60},{11,10},{12,48},{13,95},{... | collective-permute-start | bytes 3145736 | tf_op jit(solution)/shard_map/ppermute | solution.py:405
  61.7 2.2 %collective-permute-start.6 = (bf16[8,256,256]{2,1,0:T(8,128)(2,1)}, bf16[8,256,256]{2,1,0:T(8,128)(2,1)S(1)}, u32[]{:S(2)}, u32[]{:S(2)}) collective-permute-start(bf16[8,256,256]{2,1,0:T(8,128)(2,1)} %get-tuple-element.15), channel_id=1, source_target_pairs={{1,4},{2,1},{3,19},{4,20},{5,72},{6,5},{7,23},{9,25},{10,11},{12,1... | collective-permute-start | bytes 3145736 | tf_op jit(solution)/shard_map/ppermute | solution.py:405
  63.9 2.3 %collective-permute-start.7 = (bf16[8,256,256]{2,1,0:T(8,128)(2,1)}, bf16[8,256,256]{2,1,0:T(8,128)(2,1)}, u32[]{:S(2)}, u32[]{:S(2)}) collective-permute-start(bf16[8,256,256]{2,1,0:T(8,128)(2,1)} %get-tuple-element.16), channel_id=1, source_target_pairs={{1,0},{2,3},{3,19},{4,53},{5,4},{6,22},{7,6},{8,15},{9,122},{10,9}... | collective-permute-start | bytes 3145736 | tf_op jit(solution)/shard_map/ppermute | solution.py:405
  66.1 11.1 %collective-permute-start.8 = (bf16[8,256,256]{2,1,0:T(8,128)(2,1)}, bf16[8,256,256]{2,1,0:T(8,128)(2,1)}, u32[]{:S(2)}, u32[]{:S(2)}) collective-permute-start(bf16[8,256,256]{2,1,0:T(8,128)(2,1)} %get-tuple-element.17), channel_id=1, source_target_pairs={{0,15},{1,16},{3,78},{4,68},{5,90},{7,121},{8,52},{9,8},{10,26},{1... | collective-permute-start | bytes 3145736 | tf_op jit(solution)/shard_map/ppermute | solution.py:405
  77.2 4.1 %collective-permute-done.4.refs_5_ = bf16[8,256,256]{2,1,0:T(8,128)(2,1)S(1)} collective-permute-done((bf16[8,256,256]{2,1,0:T(8,128)(2,1)}, bf16[8,256,256]{2,1,0:T(8,128)(2,1)S(1)}, u32[]{:S(2)}, u32[]{:S(2)}) %collective-permute-start.4) | collective-permute-done | bytes 1048608 | tf_op jit(solution)/shard_map/ppermute | solution.py:405
  81.3 11.8 %collective-permute-done.5.refs_6_ = bf16[8,256,256]{2,1,0:T(8,128)(2,1)S(1)} collective-permute-done((bf16[8,256,256]{2,1,0:T(8,128)(2,1)}, bf16[8,256,256]{2,1,0:T(8,128)(2,1)S(1)}, u32[]{:S(2)}, u32[]{:S(2)}) %collective-permute-start.5) | collective-permute-done | bytes 1048608 | tf_op jit(solution)/shard_map/ppermute | solution.py:405
  93.1 0.0 collective-permute-done.6.refs_7_
  93.1 0.0 collective-permute-done.7.refs_8_
  93.1 11.2 %collective-permute-done.8.refs_9_ = bf16[8,256,256]{2,1,0:T(8,128)(2,1)} collective-permute-done((bf16[8,256,256]{2,1,0:T(8,128)(2,1)}, bf16[8,256,256]{2,1,0:T(8,128)(2,1)}, u32[]{:S(2)}, u32[]{:S(2)}) %collective-permute-start.8) | collective-permute-done | bytes 1048608 | tf_op jit(solution)/shard_map/ppermute | solution.py:405
  104.3 0.0 copy-done.3
  104.3 0.0 copy-done.4
  104.3 0.0 copy-done.5
  104.3 4.9 %products.1 = f32[512,2048]{1,0:T(8,128)} custom-call(s32[768]{0:T(1024)} %get-tuple-element.12.lists, bf16[8,256,256]{2,1,0:T(8,128)(2,1)} %bitcast.12, bf16[8,256,256]{2,1,0:T(8,128)(2,1)} %collective-permute-done.refs_1_, bf16[8,256,256]{2,1,0:T(8,128)(2,1)} %copy-done.2, bf16[8,256,256]{2,1,0:T(8,128)(2,1)} %copy-done.1, ...), custom_call_target="tpu_custom_call", output_to_operand_aliasing={{}: (11, {})} | custom-call | flops 1000000000 | bytes 12582912 | tf_op jit(solution)/shard_map/products/pallas_call | solution.py:409
  (4 shorter events, 0.0 us)
Async XLA Ops:
  0.0 26.5 %collective-permute-start.3 = (bf16[8,256,256]{2,1,0:T(8,128)(2,1)}, bf16[8,256,256]{2,1,0:T(8,128)(2,1)S(1)}, u32[]{:S(2)}, u32[]{:S(2)}) collective-permute-start(bf16[8,256,256]{2,1,0:T(8,128)(2,1)} %bitcast.7), channel_id=1, source_target_pairs={{1,16},{2,10},{3,67},{4,11},{5,12},{6,38},{7,15},{8,57},{9,24},{10... | collective-permute-start | bytes 3145736 | tf_op jit(solution)/shard_map/ppermute | solution.py:381
  3.9 25.2 %collective-permute-start.2 = (bf16[8,256,256]{2,1,0:T(8,128)(2,1)}, bf16[8,256,256]{2,1,0:T(8,128)(2,1)S(1)}, u32[]{:S(2)}, u32[]{:S(2)}) collective-permute-start(bf16[8,256,256]{2,1,0:T(8,128)(2,1)} %bitcast.8), channel_id=1, source_target_pairs={{0,4},{1,22},{2,46},{3,10},{4,64},{5,37},{6,14},{7,23},{8,7},{9,10... | collective-permute-start | bytes 3145736 | tf_op jit(solution)/shard_map/ppermute | solution.py:381
  5.9 25.6 %collective-permute-start.1 = (bf16[8,256,256]{2,1,0:T(8,128)(2,1)}, bf16[8,256,256]{2,1,0:T(8,128)(2,1)S(1)}, u32[]{:S(2)}, u32[]{:S(2)}) collective-permute-start(bf16[8,256,256]{2,1,0:T(8,128)(2,1)} %bitcast.9), channel_id=1, source_target_pairs={{1,97},{2,16},{3,2},{4,48},{5,82},{6,5},{7,6},{9,1},{10,9},{11,56}... | collective-permute-start | bytes 3145736 | tf_op jit(solution)/shard_map/ppermute | solution.py:381
  10.1 37.3 %collective-permute-start = (bf16[8,256,256]{2,1,0:T(8,128)(2,1)}, bf16[8,256,256]{2,1,0:T(8,128)(2,1)}, u32[]{:S(2)}, u32[]{:S(2)}) collective-permute-start(bf16[8,256,256]{2,1,0:T(8,128)(2,1)} %bitcast.10), channel_id=1, source_target_pairs={{1,9},{3,48},{4,52},{5,4},{6,96},{7,113},{10,32},{11,75},{13,5},{1... | collective-permute-start | bytes 3145736 | tf_op jit(solution)/shard_map/ppermute | solution.py:381
  26.5 20.9 %copy-start = (bf16[8,256,256]{2,1,0:T(8,128)(2,1)}, bf16[8,256,256]{2,1,0:T(8,128)(2,1)S(1)}, u32[]{:S(2)}) copy-start(bf16[8,256,256]{2,1,0:T(8,128)(2,1)S(1)} %collective-permute-done.3.refs_4_) | copy-start | bytes 3145732
  29.2 18.2 %copy-start.1 = (bf16[8,256,256]{2,1,0:T(8,128)(2,1)}, bf16[8,256,256]{2,1,0:T(8,128)(2,1)S(1)}, u32[]{:S(2)}) copy-start(bf16[8,256,256]{2,1,0:T(8,128)(2,1)S(1)} %collective-permute-done.2.refs_3_) | copy-start | bytes 3145732
  31.5 15.9 %copy-start.2 = (bf16[8,256,256]{2,1,0:T(8,128)(2,1)}, bf16[8,256,256]{2,1,0:T(8,128)(2,1)S(1)}, u32[]{:S(2)}) copy-start(bf16[8,256,256]{2,1,0:T(8,128)(2,1)S(1)} %collective-permute-done.1.refs_2_) | copy-start | bytes 3145732
  53.1 28.2 %collective-permute-start.4 = (bf16[8,256,256]{2,1,0:T(8,128)(2,1)}, bf16[8,256,256]{2,1,0:T(8,128)(2,1)S(1)}, u32[]{:S(2)}, u32[]{:S(2)}) collective-permute-start(bf16[8,256,256]{2,1,0:T(8,128)(2,1)} %get-tuple-element.13), channel_id=1, source_target_pairs={{0,112},{1,20},{3,11},{4,8},{7,0},{9,40},{10,2},{12,60},{14,13},{1... | collective-permute-start | bytes 3145736 | tf_op jit(solution)/shard_map/ppermute | solution.py:405
  55.0 38.1 %collective-permute-start.5 = (bf16[8,256,256]{2,1,0:T(8,128)(2,1)}, bf16[8,256,256]{2,1,0:T(8,128)(2,1)S(1)}, u32[]{:S(2)}, u32[]{:S(2)}) collective-permute-start(bf16[8,256,256]{2,1,0:T(8,128)(2,1)} %get-tuple-element.14), channel_id=1, source_target_pairs={{1,0},{3,52},{4,7},{7,112},{9,8},{10,60},{11,10},{12,48},{13,95},{... | collective-permute-start | bytes 3145736 | tf_op jit(solution)/shard_map/ppermute | solution.py:405
  61.7 31.4 %collective-permute-start.6 = (bf16[8,256,256]{2,1,0:T(8,128)(2,1)}, bf16[8,256,256]{2,1,0:T(8,128)(2,1)S(1)}, u32[]{:S(2)}, u32[]{:S(2)}) collective-permute-start(bf16[8,256,256]{2,1,0:T(8,128)(2,1)} %get-tuple-element.15), channel_id=1, source_target_pairs={{1,4},{2,1},{3,19},{4,20},{5,72},{6,5},{7,23},{9,25},{10,11},{12,1... | collective-permute-start | bytes 3145736 | tf_op jit(solution)/shard_map/ppermute | solution.py:405
  63.9 29.2 %collective-permute-start.7 = (bf16[8,256,256]{2,1,0:T(8,128)(2,1)}, bf16[8,256,256]{2,1,0:T(8,128)(2,1)}, u32[]{:S(2)}, u32[]{:S(2)}) collective-permute-start(bf16[8,256,256]{2,1,0:T(8,128)(2,1)} %get-tuple-element.16), channel_id=1, source_target_pairs={{1,0},{2,3},{3,19},{4,53},{5,4},{6,22},{7,6},{8,15},{9,122},{10,9}... | collective-permute-start | bytes 3145736 | tf_op jit(solution)/shard_map/ppermute | solution.py:405
  66.1 38.2 %collective-permute-start.8 = (bf16[8,256,256]{2,1,0:T(8,128)(2,1)}, bf16[8,256,256]{2,1,0:T(8,128)(2,1)}, u32[]{:S(2)}, u32[]{:S(2)}) collective-permute-start(bf16[8,256,256]{2,1,0:T(8,128)(2,1)} %get-tuple-element.17), channel_id=1, source_target_pairs={{0,15},{1,16},{3,78},{4,68},{5,90},{7,121},{8,52},{9,8},{10,26},{1... | collective-permute-start | bytes 3145736 | tf_op jit(solution)/shard_map/ppermute | solution.py:405
  81.3 23.0 %copy-start.3 = (bf16[8,256,256]{2,1,0:T(8,128)(2,1)}, bf16[8,256,256]{2,1,0:T(8,128)(2,1)S(1)}, u32[]{:S(2)}) copy-start(bf16[8,256,256]{2,1,0:T(8,128)(2,1)S(1)} %collective-permute-done.4.refs_5_) | copy-start | bytes 3145732
  93.1 11.2 %copy-start.4 = (bf16[8,256,256]{2,1,0:T(8,128)(2,1)}, bf16[8,256,256]{2,1,0:T(8,128)(2,1)S(1)}, u32[]{:S(2)}) copy-start(bf16[8,256,256]{2,1,0:T(8,128)(2,1)S(1)} %collective-permute-done.5.refs_6_) | copy-start | bytes 3145732
  93.1 11.2 %copy-start.5 = (bf16[8,256,256]{2,1,0:T(8,128)(2,1)}, bf16[8,256,256]{2,1,0:T(8,128)(2,1)S(1)}, u32[]{:S(2)}) copy-start(bf16[8,256,256]{2,1,0:T(8,128)(2,1)S(1)} %collective-permute-done.6.refs_7_) | copy-start | bytes 3145732

commit v3 on v2

v3 whole, which is shorter than its diff:
```python
import functools

import jax
import jax.numpy as jnp
import numpy as np
from jax import lax
from jax.experimental import pallas as pl
from jax.experimental.pallas import tpu as pltpu
from jax.sharding import PartitionSpec as P

BS = 256
CB = 8
SLOTS = 8
SR = 2
NB = 128
NR = 8
NC = 16
ND = NR * NC
MIB = 1024 * 1024
FETCH = 640

FIRST = [
    [
        (1, 9, 1), (3, 2, 3), (5, 4, 5), (11, 10, 11), (17, 16, 17), (18, 24, 18), (19, 18, 19), (20, 27, 20),
        (21, 20, 21), (22, 65, 22), (23, 81, 23), (28, 94, 28), (29, 28, 29), (30, 46, 30), (31, 30, 31), (35, 99, 35),
        (36, 41, 36), (38, 54, 38), (40, 37, 40), (43, 26, 43), (44, 33, 44), (46, 43, 46), (52, 116, 52), (53, 57, 53),
        (54, 50, 54), (55, 59, 55), (56, 52, 56), (58, 63, 58), (60, 124, 60), (69, 117, 69), (70, 86, 70), (71, 66, 71),
        (72, 56, 72), (73, 76, 73), (77, 73, 77), (85, 80, 85), (86, 88, 86), (90, 69, 90), (94, 29, 94), (95, 90, 95),
        (102, 103, 102), (103, 96, 103), (104, 105, 104), (105, 106, 105), (108, 109, 108), (111, 108, 111), (121, 89, 121), (124, 125, 124),
    ],
    [
        (1, 97, 1), (2, 82, 2), (3, 67, 3), (5, 90, 5), (6, 5, 6), (7, 23, 7), (8, 15, 8), (9, 8, 9),
        (10, 27, 10), (11, 75, 11), (12, 48, 12), (13, 72, 13), (14, 80, 14), (15, 120, 15), (17, 29, 17), (18, 38, 18),
        (19, 53, 19), (20, 33, 20), (21, 19, 21), (22, 107, 22), (23, 22, 23), (25, 16, 25), (27, 26, 27), (28, 41, 28),
        (29, 20, 29), (30, 89, 30), (31, 47, 31), (34, 114, 34), (35, 18, 35), (36, 100, 36), (37, 84, 37), (38, 35, 38),
        (39, 37, 39), (41, 9, 41), (42, 10, 42), (43, 32, 43), (44, 108, 44), (45, 93, 45), (46, 44, 46), (47, 63, 47),
        (52, 70, 52), (53, 49, 53), (54, 86, 54), (55, 116, 55), (56, 40, 56), (57, 61, 57), (58, 55, 58), (59, 56, 59),
        (60, 3, 60), (61, 57, 61), (62, 50, 62), (68, 64, 68), (69, 95, 69), (70, 102, 70), (71, 74, 71), (73, 69, 73),
        (74, 78, 74), (75, 11, 75), (76, 124, 76), (77, 65, 77), (78, 66, 78), (79, 36, 79), (85, 87, 85), (86, 81, 86),
        (87, 117, 87), (88, 42, 88), (89, 83, 89), (91, 94, 91), (92, 101, 92), (93, 13, 93), (94, 126, 94), (95, 21, 95),
        (102, 118, 102), (103, 104, 103), (104, 98, 104), (105, 54, 105), (106, 58, 106), (107, 109, 107), (110, 111, 110), (111, 30, 111),
        (119, 7, 119), (120, 113, 120), (121, 105, 121), (123, 115, 123), (124, 60, 124), (126, 119, 126),
    ],
    [
        (0, 8, 0), (1, 16, 1), (2, 45, 2), (3, 11, 3), (4, 12, 4), (5, 53, 5), (6, 96, 6), (9, 105, 9),
        (10, 1, 10), (11, 56, 11), (12, 76, 12), (13, 4, 13), (14, 30, 14), (15, 6, 15), (17, 113, 17), (18, 17, 18),
        (19, 26, 19), (20, 68, 20), (21, 83, 21), (22, 20, 22), (23, 121, 23), (24, 23, 24), (26, 24, 26), (27, 18, 27),
        (28, 19, 28), (29, 61, 29), (30, 29, 30), (31, 22, 31), (34, 39, 34), (35, 62, 35), (36, 70, 36), (37, 35, 37),
        (38, 43, 38), (39, 115, 39), (40, 98, 40), (41, 38, 41), (42, 32, 42), (43, 107, 43), (45, 58, 45), (46, 78, 46),
        (47, 36, 47), (51, 3, 51), (52, 48, 52), (53, 86, 53), (54, 101, 54), (55, 52, 55), (56, 67, 56), (57, 25, 57),
        (58, 10, 58), (59, 55, 59), (60, 49, 60), (61, 109, 61), (62, 47, 62), (63, 59, 63), (68, 71, 68), (69, 65, 69),
        (70, 66, 70), (71, 124, 71), (72, 75, 72), (73, 41, 73), (74, 84, 74), (75, 79, 75), (76, 64, 76), (77, 28, 77),
        (78, 44, 78), (79, 60, 79), (85, 117, 85), (86, 21, 86), (87, 82, 87), (88, 91, 88), (89, 73, 89), (90, 42, 90),
        (91, 27, 91), (93, 80, 93), (94, 5, 94), (95, 81, 95), (102, 106, 102), (103, 119, 103), (105, 99, 105), (106, 74, 106),
        (107, 100, 107), (108, 102, 108), (109, 111, 109), (110, 126, 110), (111, 97, 111), (119, 120, 119), (120, 7, 120), (121, 114, 121),
        (122, 123, 122), (123, 116, 123), (124, 87, 124), (125, 118, 125), (126, 14, 126), (127, 112, 127),
    ],
    [
        (0, 12, 0), (1, 63, 1), (2, 10, 2), (3, 60, 3), (4, 64, 4), (5, 37, 5), (6, 14, 6), (7, 113, 7),
        (8, 7, 8), (9, 0, 9), (10, 40, 10), (11, 2, 11), (12, 11, 12), (13, 45, 13), (14, 6, 14), (15, 124, 15),
        (17, 1, 17), (18, 47, 18), (19, 83, 19), (20, 19, 20), (21, 49, 21), (22, 28, 22), (23, 97, 23), (24, 31, 24),
        (25, 121, 25), (26, 9, 26), (27, 91, 27), (28, 27, 28), (29, 77, 29), (30, 21, 30), (34, 32, 34), (35, 54, 35),
        (36, 33, 36), (37, 43, 37), (38, 100, 38), (39, 36, 39), (40, 24, 40), (41, 98, 41), (42, 39, 42), (43, 18, 43),
        (44, 41, 44), (45, 127, 45), (46, 35, 46), (47, 44, 47), (51, 48, 51), (52, 57, 52), (53, 85, 53), (54, 58, 54),
        (55, 71, 55), (56, 61, 56), (57, 53, 57), (58, 115, 58), (59, 123, 59), (60, 56, 60), (61, 50, 61), (62, 94, 62),
        (63, 79, 63), (68, 72, 68), (69, 20, 69), (70, 73, 70), (71, 52, 71), (72, 76, 72), (73, 84, 73), (74, 26, 74),
        (75, 70, 75), (76, 8, 76), (77, 109, 77), (78, 74, 78), (79, 67, 79), (85, 5, 85), (86, 103, 86), (87, 90, 87),
        (88, 82, 88), (89, 69, 89), (90, 92, 90), (91, 101, 91), (92, 95, 92), (93, 88, 93), (94, 81, 94), (95, 29, 95),
        (102, 96, 102), (103, 22, 103), (104, 38, 104), (105, 89, 105), (106, 99, 106), (107, 86, 107), (108, 110, 108), (109, 13, 109),
        (110, 118, 110), (111, 104, 111), (119, 112, 119), (121, 122, 121), (122, 114, 122), (123, 75, 123), (124, 117, 124), (125, 126, 125),
        (127, 15, 127),
    ],
]
SECOND = [
    [
        (0, 7, 0), (1, 16, 10), (3, 53, 3), (4, 48, 4), (5, 64, 5), (6, 22, 6), (7, 15, 7), (8, 4, 76),
        (9, 1, 26), (10, 9, 2), (11, 116, 75), (12, 60, 12), (13, 95, 93), (14, 13, 14), (15, 0, 8), (16, 31, 25),
        (17, 114, 18), (18, 33, 27), (19, 27, 21), (20, 87, 69), (21, 5, 86), (22, 21, 31), (23, 30, 23), (24, 17, 26),
        (25, 23, 25), (26, 25, 19), (27, 77, 20), (28, 12, 77), (29, 24, 17), (30, 81, 30), (31, 29, 31), (32, 40, 43),
        (33, 18, 36), (34, 2, 34), (35, 41, 35), (36, 52, 79), (37, 45, 39), (38, 46, 41), (39, 122, 42), (40, 106, 10),
        (41, 26, 44), (42, 37, 88), (43, 108, 38), (44, 74, 47), (45, 38, 2), (46, 62, 30), (47, 105, 31), (48, 78, 52),
        (49, 35, 53), (50, 19, 61), (52, 36, 71), (53, 54, 57), (54, 50, 38), (56, 32, 11), (57, 58, 61), (58, 42, 45),
        (59, 63, 59), (60, 44, 79), (61, 49, 61), (62, 59, 62), (63, 51, 63), (64, 76, 4), (66, 65, 78), (67, 83, 3),
        (68, 69, 20), (69, 72, 69), (70, 100, 75), (71, 67, 55), (72, 68, 72), (73, 57, 89), (74, 70, 74), (75, 91, 11),
        (76, 79, 76), (77, 73, 29), (78, 66, 46), (79, 75, 79), (80, 96, 14), (81, 89, 94), (82, 126, 87), (83, 99, 19),
        (84, 93, 37), (85, 101, 53), (86, 20, 70), (87, 71, 124), (88, 90, 88), (89, 84, 89), (90, 80, 5), (91, 86, 91),
        (92, 28, 92), (93, 34, 45), (94, 88, 94), (95, 94, 92), (96, 98, 6), (97, 113, 1), (98, 97, 104), (99, 115, 35),
        (100, 107, 38), (101, 109, 54), (102, 110, 70), (103, 118, 86), (105, 39, 121), (106, 111, 102), (107, 123, 43), (108, 92, 44),
        (109, 43, 61), (110, 104, 110), (111, 127, 111), (113, 121, 7), (114, 55, 122), (115, 82, 39), (116, 3, 52), (117, 125, 87),
        (118, 6, 102), (119, 103, 126), (120, 112, 15), (123, 124, 123), (124, 117, 71), (126, 14, 110), (127, 119, 127),
    ],
    [
        (0, 112, 0), (1, 32, 10), (3, 19, 60), (4, 11, 4), (5, 13, 5), (6, 5, 14), (7, 23, 120), (8, 12, 76),
        (9, 122, 26), (10, 2, 42), (11, 72, 12), (12, 4, 12), (13, 29, 109), (14, 30, 126), (15, 7, 127), (16, 22, 1),
        (17, 1, 18), (18, 33, 19), (19, 49, 28), (20, 27, 29), (22, 89, 31), (23, 39, 23), (24, 25, 18), (25, 9, 25),
        (26, 10, 43), (27, 90, 10), (28, 20, 77), (30, 46, 14), (31, 81, 31), (32, 41, 43), (33, 18, 44), (35, 50, 46),
        (36, 82, 47), (37, 44, 39), (38, 36, 38), (39, 55, 39), (40, 24, 10), (41, 42, 36), (42, 47, 42), (43, 92, 37),
        (44, 66, 47), (45, 37, 2), (47, 97, 31), (48, 115, 51), (49, 53, 21), (50, 35, 61), (51, 63, 51), (53, 62, 19),
        (54, 38, 105), (55, 3, 59), (56, 52, 72), (57, 58, 53), (58, 54, 106), (59, 60, 55), (60, 61, 3), (61, 57, 29),
        (63, 31, 1), (64, 68, 4), (65, 98, 22), (66, 65, 70), (67, 48, 3), (68, 76, 20), (69, 85, 90), (70, 78, 36),
        (71, 116, 71), (72, 80, 13), (73, 74, 70), (74, 75, 71), (75, 71, 123), (76, 64, 12), (77, 125, 77), (78, 94, 78),
        (79, 67, 63), (80, 95, 85), (81, 113, 23), (82, 16, 2), (83, 91, 21), (84, 69, 74), (85, 88, 85), (86, 70, 107),
        (87, 21, 87), (88, 111, 86), (89, 73, 30), (90, 83, 5), (91, 107, 27), (92, 86, 92), (93, 77, 45), (94, 93, 91),
        (95, 87, 92), (96, 105, 6), (97, 114, 23), (99, 40, 35), (100, 84, 36), (101, 117, 92), (102, 101, 70), (103, 110, 86),
        (104, 106, 104), (105, 121, 9), (106, 108, 106), (107, 43, 107), (108, 14, 111), (109, 102, 109), (110, 28, 108), (111, 103, 109),
        (112, 120, 127), (115, 99, 58), (116, 100, 52), (117, 118, 87), (118, 6, 110), (119, 127, 103), (120, 104, 15), (123, 59, 123),
        (124, 96, 15), (126, 45, 125),
    ],
    [
        (1, 0, 1), (2, 48, 11), (3, 27, 60), (4, 75, 4), (5, 106, 6), (6, 38, 6), (7, 14, 7), (8, 120, 8),
        (9, 24, 9), (10, 26, 58), (11, 56, 12), (12, 3, 12), (13, 5, 93), (14, 13, 6), (15, 112, 8), (16, 1, 25),
        (17, 23, 17), (18, 2, 35), (19, 92, 21), (20, 86, 69), (21, 28, 21), (22, 54, 22), (23, 21, 23), (24, 8, 24),
        (25, 41, 57), (26, 16, 26), (27, 43, 91), (28, 76, 28), (29, 31, 17), (30, 6, 111), (31, 97, 24), (32, 114, 42),
        (33, 34, 36), (35, 50, 37), (36, 90, 47), (37, 122, 39), (38, 22, 104), (39, 40, 34), (40, 45, 40), (41, 42, 44),
        (42, 84, 90), (43, 44, 38), (44, 36, 78), (45, 32, 2), (46, 65, 30), (47, 46, 18), (48, 19, 52), (49, 69, 21),
        (50, 35, 62), (53, 61, 19), (54, 70, 38), (55, 51, 55), (56, 57, 60), (57, 79, 52), (58, 100, 106), (59, 124, 55),
        (60, 52, 3), (61, 49, 29), (62, 58, 62), (63, 30, 1), (64, 71, 76), (65, 81, 22), (67, 83, 56), (69, 53, 89),
        (70, 77, 36), (71, 4, 68), (72, 64, 13), (73, 109, 70), (74, 20, 78), (75, 67, 72), (76, 72, 76), (78, 62, 46),
        (79, 95, 79), (80, 87, 93), (81, 82, 95), (82, 98, 2), (83, 17, 19), (84, 85, 37), (86, 94, 53), (87, 37, 87),
        (89, 91, 89), (90, 89, 95), (91, 25, 27), (93, 125, 93), (94, 110, 94), (95, 12, 92), (96, 80, 6), (98, 47, 41),
        (99, 33, 35), (100, 66, 38), (101, 108, 54), (102, 104, 102), (104, 88, 104), (105, 73, 105), (107, 99, 22), (108, 101, 108),
        (109, 93, 61), (110, 103, 110), (111, 118, 109), (112, 127, 119), (113, 96, 7), (114, 39, 122), (115, 123, 39), (116, 55, 123),
        (118, 117, 125), (119, 126, 103), (121, 113, 25), (122, 74, 122), (123, 115, 59), (124, 116, 76), (126, 29, 125),
    ],
    [
        (0, 16, 9), (1, 2, 10), (2, 1, 2), (3, 11, 60), (4, 5, 13), (5, 12, 5), (6, 7, 15), (7, 120, 7),
        (9, 25, 41), (10, 9, 10), (11, 10, 3), (12, 15, 0), (13, 61, 13), (15, 31, 15), (17, 98, 18), (18, 17, 27),
        (19, 18, 28), (20, 21, 22), (21, 37, 95), (22, 6, 103), (23, 29, 23), (24, 106, 26), (25, 83, 57), (26, 42, 74),
        (27, 26, 28), (28, 33, 28), (29, 28, 30), (30, 22, 111), (31, 30, 24), (33, 34, 44), (34, 47, 34), (35, 36, 46),
        (37, 38, 40), (38, 39, 41), (40, 46, 40), (41, 57, 28), (42, 40, 42), (43, 58, 46), (44, 110, 78), (47, 45, 47),
        (48, 49, 52), (49, 50, 53), (50, 51, 62), (51, 55, 51), (52, 71, 52), (53, 54, 19), (54, 35, 54), (56, 48, 59),
        (57, 56, 52), (58, 43, 45), (59, 52, 63), (61, 62, 57), (63, 60, 63), (64, 3, 4), (65, 64, 77), (66, 67, 71),
        (67, 74, 79), (68, 116, 68), (69, 73, 69), (70, 69, 36), (71, 87, 71), (72, 88, 13), (73, 4, 77), (74, 70, 106),
        (77, 65, 29), (78, 77, 74), (79, 75, 63), (80, 117, 93), (81, 80, 94), (82, 81, 87), (83, 84, 21), (84, 100, 74),
        (85, 19, 53), (86, 93, 53), (87, 89, 87), (88, 72, 88), (89, 92, 89), (90, 82, 5), (91, 53, 88), (94, 78, 62),
        (95, 111, 95), (96, 97, 103), (97, 23, 1), (98, 114, 41), (99, 32, 35), (100, 99, 38), (101, 85, 91), (102, 86, 108),
        (103, 102, 86), (104, 105, 111), (106, 107, 106), (107, 59, 107), (109, 27, 61), (110, 44, 108), (111, 96, 110), (113, 112, 120),
        (114, 113, 121), (115, 66, 39), (116, 115, 55), (117, 101, 69), (118, 103, 125), (119, 118, 103), (120, 104, 120), (121, 122, 23),
        (122, 90, 122), (124, 108, 60), (126, 13, 94),
    ],
    [
        (0, 1, 9), (2, 3, 11), (3, 32, 3), (4, 52, 4), (5, 21, 94), (7, 6, 7), (9, 8, 1), (11, 27, 75),
        (13, 12, 13), (15, 14, 15), (17, 16, 18), (18, 2, 43), (19, 18, 20), (20, 4, 69), (21, 20, 30), (22, 38, 22),
        (23, 22, 24), (24, 25, 26), (25, 24, 25), (27, 26, 20), (28, 29, 22), (29, 45, 95), (30, 88, 14), (31, 113, 24),
        (32, 33, 43), (33, 49, 20), (35, 34, 37), (36, 37, 47), (38, 39, 18), (41, 57, 73), (42, 58, 90), (43, 42, 37),
        (44, 28, 78), (45, 46, 2), (47, 43, 62), (48, 56, 51), (49, 48, 60), (50, 51, 54), (52, 53, 56), (53, 99, 57),
        (54, 55, 35), (55, 54, 58), (56, 40, 11), (58, 59, 54), (59, 11, 59), (60, 44, 124), (61, 60, 56), (62, 63, 35),
        (63, 62, 58), (64, 67, 4), (65, 64, 69), (67, 66, 79), (68, 84, 20), (69, 68, 73), (70, 71, 75), (71, 123, 55),
        (72, 79, 68), (73, 72, 77), (74, 73, 78), (76, 77, 73), (77, 19, 29), (78, 74, 46), (79, 78, 75), (80, 104, 14),
        (81, 80, 86), (82, 83, 88), (83, 65, 21), (84, 69, 37), (86, 70, 54), (87, 103, 87), (88, 89, 86), (89, 23, 121),
        (90, 91, 5), (91, 41, 27), (92, 93, 90), (93, 35, 45), (94, 92, 28), (95, 94, 69), (96, 97, 6), (97, 96, 111),
        (98, 82, 40), (99, 98, 105), (100, 101, 107), (101, 100, 54), (102, 36, 70), (104, 105, 103), (106, 107, 105), (107, 106, 22),
        (109, 108, 107), (111, 110, 109), (113, 112, 7), (114, 115, 122), (115, 114, 39), (117, 116, 124), (118, 87, 125), (119, 118, 126),
        (120, 121, 120), (124, 125, 71), (126, 127, 126), (127, 50, 45),
    ],
]
NRELAY = 4
NBUF = 1 + len(FIRST) + len(SECOND)


def holders():
    held = [{d: 0} for d in range(ND)]
    for n, edges in enumerate(FIRST):
        for _, there, tile in edges:
            held[there].setdefault(tile, 1 + n)
    source = np.zeros((len(SECOND), ND), np.int32)
    for n, edges in enumerate(SECOND):
        for here, _, tile in edges:
            source[n, here] = held[here][tile]
    for n, edges in enumerate(SECOND):
        for _, there, tile in edges:
            held[there].setdefault(tile, 1 + len(FIRST) + n)
    place = np.zeros((ND, 8), np.int32)
    for a in range(NR):
        for b in range(NC):
            for s in range(2):
                k = (a + b + s) % NR
                low = b < NR
                need = [
                    (k, b) if not low or k <= b else (b, k),
                    (b, k + NR) if low else (k, b) if k + NR <= b else (b - NR, k + NR),
                    (a, k) if a <= k else (k, a),
                    (a, k + NR),
                ]
                d = a * NC + b
                for kind, (r, c) in enumerate(need):
                    place[d, 4 * s + kind] = held[d][r * NC + c]
    return source, place


def slot_table(occupancy):
    i = np.arange(NB)
    before_col = (i[:, None] // CB == i[None, :] // CB) & (i[:, None] < i[None, :])
    panel = i[:, None] // CB == i[None, :] // CB
    before_row = (i[:, None] // CB % NR == i[None, :] // CB % NR) & (i[None, :] < i[:, None])
    occ = occupancy.astype(jnp.float32)
    dot = functools.partial(jnp.dot, precision=lax.Precision.HIGHEST)
    rank = dot(occ, jnp.asarray(before_col, jnp.float32)) + dot(
        jnp.asarray(before_row, jnp.float32), dot(occ, jnp.asarray(panel, jnp.float32))
    )
    return jnp.where(occupancy == 1, rank.astype(jnp.int32), -1)


def pick_kernel(source, lists, *refs):
    bufs, outs, sems = refs[: 1 + NRELAY], refs[1 + NRELAY : -1], refs[-1]
    here = lax.axis_index("row") * NC + lax.axis_index("col")
    for n, out in enumerate(outs):
        which = source[n * ND + here]
        for i in range(1 + NRELAY):

            @pl.when(which == i)
            def _():
                pltpu.make_async_copy(bufs[i], out, sems.at[n]).start()

    for n, out in enumerate(outs):
        pltpu.make_async_copy(bufs[0], out, sems.at[n]).wait()


def index_kernel(table, place, lists, blank, used):
    a = lax.axis_index("row")
    b = lax.axis_index("col")
    here = a * NC + b
    blank[...] = jnp.zeros_like(blank)

    def clear_used(t, carry):
        used[t] = 0
        return carry

    lax.fori_loop(0, 80, clear_used, 0)

    def step(t, n):
        s = t // 32
        kk = lax.rem(t // 2, 16)
        i = lax.rem(t, 2)
        half = kk // CB
        k = lax.rem(a + b + s, NR)
        inner = (half * NR + k) * CB + lax.rem(kk, CB)
        row = a * CB + i
        lslot = table[jnp.minimum(row, inner), jnp.maximum(row, inner)]
        lplace = (4 * s + 2 + half) * SLOTS + lslot
        turned = jnp.where(row > inner, 1, 0)

        def one_col(j, n0):
            n, fresh = n0
            col = b * CB + j
            rslot = table[jnp.minimum(inner, col), jnp.maximum(inner, col)]
            rplace = (4 * s + half) * SLOTS + rslot
            hit = rslot >= 0

            @pl.when(hit)
            def _():
                first = jnp.where(used[64 + i * CB + j] == 0, 1, 0)
                lists[n] = (
                    lplace
                    + (rplace << 6)
                    + ((i * CB + j) << 12)
                    + (turned << 16)
                    + (jnp.where(inner > col, 1, 0) << 17)
                    + (fresh << 18)
                    + (first << 19)
                )
                used[64 + i * CB + j] = 1
                used[lplace] = 1
                used[rplace] = 1

            one = jnp.where(hit, 1, 0)
            return n + one, fresh * (1 - one)

        return lax.cond(lslot >= 0, lambda m: lax.fori_loop(0, CB, one_col, (m, 1))[0], lambda m: m, n)

    count = lax.fori_loop(0, 64, step, 1)
    lists[0] = count
    for t in range(16):
        lists[FETCH + 112 + t] = used[64 + t]

    def by_buffer(buf, n):
        lists[FETCH + buf] = n

        def by_kind(kind, n):
            def by_slot(slot, n):
                @pl.when(used[kind * SLOTS + slot] == 1)
                def _():
                    lists[FETCH + n] = kind * SLOTS + slot

                return n + used[kind * SLOTS + slot]

            return lax.cond(
                place[here * 8 + kind] == buf, lambda m: lax.fori_loop(0, SLOTS, by_slot, m), lambda m: m, n
            )

        return lax.fori_loop(0, 8, by_kind, n)

    lists[FETCH + NBUF] = lax.fori_loop(0, NBUF, by_buffer, 32)


def product_kernel(lists, *refs):
    bufs = refs[:NBUF]
    blank, out, tiles, left, acc, sems, out_sems = refs[NBUF:]
    for n, buf in enumerate(bufs):

        def start(q, carry):
            t = lists[FETCH + q]
            pltpu.make_async_copy(buf.at[lax.rem(t, SLOTS)], tiles.at[t], sems.at[t]).start()
            return carry

        lax.fori_loop(lists[FETCH + n], lists[FETCH + n + 1], start, 0)

    def finish(q, carry):
        t = lists[FETCH + q]
        pltpu.make_async_copy(bufs[0].at[0], tiles.at[t], sems.at[t]).wait()
        return carry

    lax.fori_loop(32, lists[FETCH + NBUF], finish, 0)

    def product(q, carry):
        code = lists[q]
        lt = tiles.at[code & 63]
        rt = tiles.at[(code >> 6) & 63]
        to = acc.at[(code >> 12) & 15]

        @pl.when(((code >> 18) & 1) == 1)
        def _():
            @pl.when(((code >> 16) & 1) == 0)
            def _():
                left[...] = lt[...]

            @pl.when(((code >> 16) & 1) == 1)
            def _():
                left[...] = lt[...].T

        @pl.when(((code >> 19) & 1) == 1)
        def _():
            to[...] = jnp.zeros_like(to)

        @pl.when(((code >> 17) & 1) == 0)
        def _():
            to[...] += jnp.dot(left[...], rt[...], preferred_element_type=jnp.float32)

        @pl.when(((code >> 17) & 1) == 1)
        def _():
            to[...] += lax.dot_general(
                left[...], rt[...], (((1,), (1,)), ((), ())), preferred_element_type=jnp.float32
            )

        return carry

    lax.fori_loop(1, lists[0], product, 0)

    def copy_out(t):
        return pltpu.make_async_copy(
            acc.at[t], out.at[pl.ds(t // CB * BS, BS), pl.ds(t % CB * BS, BS)], out_sems.at[t]
        )

    for t in range(16):

        @pl.when(lists[FETCH + 112 + t] == 1)
        def _():
            copy_out(t).start()

    for t in range(16):

        @pl.when(lists[FETCH + 112 + t] == 1)
        def _():
            copy_out(t).wait()


def tile_shape():
    return jax.ShapeDtypeStruct((SLOTS, BS, BS), jnp.bfloat16)


SMEM = pl.BlockSpec(memory_space=pltpu.SMEM)
ANY = pl.BlockSpec(memory_space=pl.ANY)


def local(occupancy, stored):
    own = stored.reshape(SLOTS, BS, BS)
    source, place = holders()
    bufs = [own]
    for edges in FIRST:
        bufs.append(lax.ppermute(own, ("row", "col"), [(u, v) for u, v, _ in edges]))
    lists, blank = pl.pallas_call(
        index_kernel,
        out_shape=(
            jax.ShapeDtypeStruct((FETCH + 128,), jnp.int32),
            jax.ShapeDtypeStruct((SR * BS, CB * BS), jnp.float32),
        ),
        in_specs=[SMEM, SMEM],
        out_specs=(SMEM, pl.BlockSpec(memory_space=pltpu.VMEM)),
        scratch_shapes=[pltpu.SMEM((80,), jnp.int32)],
        cost_estimate=pl.CostEstimate(flops=10**9, bytes_accessed=4 * MIB, transcendentals=0),
        name="index",
    )(slot_table(occupancy), jnp.asarray(place.reshape(-1)))
    flat_source = jnp.asarray(source.reshape(-1))
    sends = pl.pallas_call(
        pick_kernel,
        out_shape=[pltpu.VMEM((SLOTS, BS, BS), jnp.bfloat16)] * len(SECOND),
        in_specs=[SMEM, SMEM] + [ANY] * (1 + NRELAY),
        out_specs=[pl.BlockSpec(memory_space=pltpu.VMEM)] * len(SECOND),
        compiler_params=pltpu.CompilerParams(vmem_limit_bytes=16 * MIB),
        scratch_shapes=[pltpu.SemaphoreType.DMA((len(SECOND),))],
        cost_estimate=pl.CostEstimate(flops=0, bytes_accessed=2 * MIB, transcendentals=0),
        name="pick",
    )(flat_source, lists, *bufs[: 1 + NRELAY])
    later = [
        lax.ppermute(send, ("row", "col"), [(u, v) for u, v, _ in edges])
        for send, edges in zip(sends, SECOND, strict=True)
    ]
    bufs += later
    return pl.pallas_call(
        product_kernel,
        out_shape=jax.ShapeDtypeStruct((SR * BS, CB * BS), jnp.float32),
        in_specs=[SMEM] + [ANY] * (NBUF + 1),
        out_specs=ANY,
        scratch_shapes=[
            pltpu.VMEM((64, BS, BS), jnp.bfloat16),
            pltpu.VMEM((BS, BS), jnp.bfloat16),
            pltpu.VMEM((16, BS, BS), jnp.float32),
            pltpu.SemaphoreType.DMA((64,)),
            pltpu.SemaphoreType.DMA((16,)),
        ],
        input_output_aliases={1 + NBUF: 0},
        compiler_params=pltpu.CompilerParams(vmem_limit_bytes=60 * MIB),
        cost_estimate=pl.CostEstimate(flops=10**9, bytes_accessed=12 * MIB, transcendentals=0),
        name="products",
    )(lists, *bufs, blank)


def solution(mesh):
    placed = (P(), P("row", "col", None, None, None))
    return jax.shard_map(
        local, mesh=mesh, in_specs=placed, out_specs=P("row", "col"), check_vma=False
    )
```

time: 110 us -> 103 us (0.936)
  the two profiles are of different devices: /device:TPU:41 before, /device:TPU:82 now
where the time goes in v3:
time: 103 us; the launch traced here: 102 us
  waiting for transfers between devices  46.3 us (45%)
  starting transfers between devices  32.5 us (32%)
  Pallas kernels  17.6 us (17%)
  matrix products  4.01 us (4%)
  local copies, waits for them, and re-layouts  1.77 us (2%)
    ppermute x5, waiting for transfers between devices, local(): lax.ppermute(send, ('row', 'col'), [(u, v) for u, v, _ in edges])  33.7 us
    ppermute x5, starting transfers between devices, local(): lax.ppermute(send, ('row', 'col'), [(u, v) for u, v, _ in edges])  22.9 us
    ppermute x4, waiting for transfers between devices, local(): lax.ppermute(own, ('row', 'col'), [(u, v) for u, v, _ in edges])  12.7 us
    ppermute x4, starting transfers between devices, local(): lax.ppermute(own, ('row', 'col'), [(u, v) for u, v, _ in edges])  9.56 us
    pallas_call x1, Pallas kernels, local(): pl.pallas_call(index_kernel, out_shape=(jax.ShapeDtypeStruct((FETCH + 128...  9.52 us
    pallas_call x1, Pallas kernels, local(): pl.pallas_call(product_kernel, out_shape=jax.ShapeDtypeStruct((SR * BS, C...  5.73 us
    pallas_call x1, Pallas kernels, local(): pl.pallas_call(pick_kernel, out_shape=[pltpu.VMEM((SLOTS, BS, BS), jnp.bf...  2.36 us
  transfers between devices with their start and end apart: 9, of which 6 were waited for; matrix products, arithmetic and copies ran while one was open for 4% of the time, Pallas kernels for 9%

profile of v3, /device:TPU:82, one launch (start us, length us, event | category | flops | bytes accessed | tf_op | source)
XLA Modules:
  0.0 102.3 jit_solution(4236077083510242315)
XLA Ops:
  0.0 3.4 %collective-permute-start.3 = (bf16[8,256,256]{2,1,0:T(8,128)(2,1)}, bf16[8,256,256]{2,1,0:T(8,128)(2,1)S(1)}, u32[]{:S(2)}, u32[]{:S(2)}) collective-permute-start(bf16[8,256,256]{2,1,0:T(8,128)(2,1)} %bitcast.7), channel_id=1, source_target_pairs={{0,12},{1,63},{2,10},{3,60},{4,64},{5,37},{6,14},{7,113},{8,7},{9,... | collective-permute-start | bytes 3145736 | tf_op jit(solution)/shard_map/ppermute | solution.py:380
  3.4 2.6 %collective-permute-start.2 = (bf16[8,256,256]{2,1,0:T(8,128)(2,1)}, bf16[8,256,256]{2,1,0:T(8,128)(2,1)S(1)}, u32[]{:S(2)}, u32[]{:S(2)}) collective-permute-start(bf16[8,256,256]{2,1,0:T(8,128)(2,1)} %bitcast.8), channel_id=1, source_target_pairs={{0,8},{1,16},{2,45},{3,11},{4,12},{5,53},{6,96},{9,105},{10,1},{11... | collective-permute-start | bytes 3145736 | tf_op jit(solution)/shard_map/ppermute | solution.py:380
  6.0 2.3 %collective-permute-start.1 = (bf16[8,256,256]{2,1,0:T(8,128)(2,1)}, bf16[8,256,256]{2,1,0:T(8,128)(2,1)}, u32[]{:S(2)}, u32[]{:S(2)}) collective-permute-start(bf16[8,256,256]{2,1,0:T(8,128)(2,1)} %bitcast.9), channel_id=1, source_target_pairs={{1,97},{2,82},{3,67},{5,90},{6,5},{7,23},{8,15},{9,8},{10,27},{11,... | collective-permute-start | bytes 3145736 | tf_op jit(solution)/shard_map/ppermute | solution.py:380
  8.3 1.3 %collective-permute-start = (bf16[8,256,256]{2,1,0:T(8,128)(2,1)}, bf16[8,256,256]{2,1,0:T(8,128)(2,1)}, u32[]{:S(2)}, u32[]{:S(2)}) collective-permute-start(bf16[8,256,256]{2,1,0:T(8,128)(2,1)} %bitcast.10), channel_id=1, source_target_pairs={{1,9},{3,2},{5,4},{11,10},{17,16},{18,24},{19,18},{20,27},{21,20},... | collective-permute-start | bytes 3145736 | tf_op jit(solution)/shard_map/ppermute | solution.py:380
  9.6 1.1 %convolution_bitcast_fusion = f32[128,128]{1,0:T(8,128)S(1)} fusion(f32[128,128]{1,0:T(8,128)} %constant.14.clone, s32[128,128]{1,0:T(8,128)} %param.7), kind=kOutput, calls=%fused_computation.3 | convolution fusion | flops 25182208 | bytes 196608 | tf_op jit(solution)/shard_map/dot_general | solution.py:198
  10.7 1.2 %fusion.2 = f32[128,128]{1,0:T(8,128)S(1)} fusion(f32[128,128]{1,0:T(8,128)} %constant.16.clone, s32[128,128]{1,0:T(8,128)} %param.7), kind=kOutput, calls=%fused_computation.4 | convolution fusion | flops 25182208 | bytes 196608 | tf_op jit(solution)/shard_map/dot_general | solution.py:199
  11.8 1.8 %fusion.1.table = s32[128,128]{1,0:T(8,128)} fusion(f32[128,128]{1,0:T(8,128)S(1)} %convolution_bitcast_fusion, f32[128,128]{1,0:T(8,128)} %constant.15.clone, f32[128,128]{1,0:T(8,128)S(1)} %fusion.2, s32[128,128]{1,0:T(8,128)} %param.7), kind=kOutput, calls=%fused_computation.2 | convolution fusion | flops 25231360 | bytes 327680 | tf_op jit(solution)/shard_map/dot_general | solution.py:198
  13.6 9.5 %index.1 = (s32[768]{0:T(1024)}, f32[512,2048]{1,0:T(8,128)}) custom-call(s32[128,128]{1,0:T(8,128)} %fusion.1.table, s32[1024]{0:T(1024)} %constant.17.clone.place), custom_call_target="tpu_custom_call" | custom-call | flops 1000000000 | bytes 4194304 | tf_op jit(solution)/shard_map/index/pallas_call | solution.py:381
  23.2 4.5 %collective-permute-done.3.refs_4_ = bf16[8,256,256]{2,1,0:T(8,128)(2,1)S(1)} collective-permute-done((bf16[8,256,256]{2,1,0:T(8,128)(2,1)}, bf16[8,256,256]{2,1,0:T(8,128)(2,1)S(1)}, u32[]{:S(2)}, u32[]{:S(2)}) %collective-permute-start.3) | collective-permute-done | bytes 1048608 | tf_op jit(solution)/shard_map/ppermute | solution.py:380
  27.7 0.0 collective-permute-done.2.refs_3_
  27.7 8.1 %collective-permute-done.1.refs_2_ = bf16[8,256,256]{2,1,0:T(8,128)(2,1)} collective-permute-done((bf16[8,256,256]{2,1,0:T(8,128)(2,1)}, bf16[8,256,256]{2,1,0:T(8,128)(2,1)}, u32[]{:S(2)}, u32[]{:S(2)}) %collective-permute-start.1) | collective-permute-done | bytes 1048608 | tf_op jit(solution)/shard_map/ppermute | solution.py:380
  35.8 0.0 collective-permute-done.refs_1_
  35.8 0.0 copy-done.4
  35.8 0.0 copy-done
  35.8 0.7 copy-done.3
  36.5 2.4 %pick.1 = (bf16[8,256,256]{2,1,0:T(8,128)(2,1)S(1)}, bf16[8,256,256]{2,1,0:T(8,128)(2,1)S(1)}, bf16[8,256,256]{2,1,0:T(8,128)(2,1)S(1)}, bf16[8,256,256]{2,1,0:T(8,128)(2,1)S(1)}, bf16[8,256,256]{2,1,0:T(8,128)(2,1)S(1)}) custom-call(s32[640]{0:T(1024)S(1)} %copy-done.4, s32[768]{0:T(1024)S(1)} %copy-done.3, bf16[8,256,256]{2,1,0:T(8,128)(2,1)S(1)} %bitcast.12, ...), custom_call_target="tpu_custom_call" | custom-call | bytes 2097152 | tf_op jit(solution)/shard_map/pick/pallas_call | solution.py:394
  38.9 13.5 %collective-permute-start.4 = (bf16[8,256,256]{2,1,0:T(8,128)(2,1)S(1)}, bf16[8,256,256]{2,1,0:T(8,128)(2,1)S(1)}, u32[]{:S(2)}, u32[]{:S(2)}) collective-permute-start(bf16[8,256,256]{2,1,0:T(8,128)(2,1)S(1)} %get-tuple-element.13), channel_id=1, source_target_pairs={{0,7},{1,16},{3,53},{4,48},{5,64},{6,22},{7,15},{8,4},{9,1},{10,9}... | collective-permute-start | bytes 3145736 | tf_op jit(solution)/shard_map/ppermute | solution.py:405
  52.4 1.9 %collective-permute-start.5 = (bf16[8,256,256]{2,1,0:T(8,128)(2,1)S(1)}, bf16[8,256,256]{2,1,0:T(8,128)(2,1)S(1)}, u32[]{:S(2)}, u32[]{:S(2)}) collective-permute-start(bf16[8,256,256]{2,1,0:T(8,128)(2,1)S(1)} %get-tuple-element.14), channel_id=1, source_target_pairs={{0,112},{1,32},{3,19},{4,11},{5,13},{6,5},{7,23},{8,12},{9,122},{1... | collective-permute-start | bytes 3145736 | tf_op jit(solution)/shard_map/ppermute | solution.py:405
  54.3 1.3 %collective-permute-start.6 = (bf16[8,256,256]{2,1,0:T(8,128)(2,1)S(1)}, bf16[8,256,256]{2,1,0:T(8,128)(2,1)S(1)}, u32[]{:S(2)}, u32[]{:S(2)}) collective-permute-start(bf16[8,256,256]{2,1,0:T(8,128)(2,1)S(1)} %get-tuple-element.15), channel_id=1, source_target_pairs={{1,0},{2,48},{3,27},{4,75},{5,106},{6,38},{7,14},{8,120},{9,24},{1... | collective-permute-start | bytes 3145736 | tf_op jit(solution)/shard_map/ppermute | solution.py:405
  55.6 1.9 %collective-permute-start.7 = (bf16[8,256,256]{2,1,0:T(8,128)(2,1)S(1)}, bf16[8,256,256]{2,1,0:T(8,128)(2,1)S(1)}, u32[]{:S(2)}, u32[]{:S(2)}) collective-permute-start(bf16[8,256,256]{2,1,0:T(8,128)(2,1)S(1)} %get-tuple-element.16), channel_id=1, source_target_pairs={{0,16},{1,2},{2,1},{3,11},{4,5},{5,12},{6,7},{7,120},{9,25},{10,9}... | collective-permute-start | bytes 3145736 | tf_op jit(solution)/shard_map/ppermute | solution.py:405
  57.5 4.3 %collective-permute-start.8 = (bf16[8,256,256]{2,1,0:T(8,128)(2,1)S(1)}, bf16[8,256,256]{2,1,0:T(8,128)(2,1)S(1)}, u32[]{:S(2)}, u32[]{:S(2)}) collective-permute-start(bf16[8,256,256]{2,1,0:T(8,128)(2,1)S(1)} %get-tuple-element.17), channel_id=1, source_target_pairs={{0,1},{2,3},{3,32},{4,52},{5,21},{7,6},{9,8},{11,27},{13,12},{15,1... | collective-permute-start | bytes 3145736 | tf_op jit(solution)/shard_map/ppermute | solution.py:405
  61.8 10.2 %collective-permute-done.4.refs_5_ = bf16[8,256,256]{2,1,0:T(8,128)(2,1)S(1)} collective-permute-done((bf16[8,256,256]{2,1,0:T(8,128)(2,1)S(1)}, bf16[8,256,256]{2,1,0:T(8,128)(2,1)S(1)}, u32[]{:S(2)}, u32[]{:S(2)}) %collective-permute-start.4) | collective-permute-done | bytes 1048608 | tf_op jit(solution)/shard_map/ppermute | solution.py:405
  72.1 4.1 %collective-permute-done.5.refs_6_ = bf16[8,256,256]{2,1,0:T(8,128)(2,1)S(1)} collective-permute-done((bf16[8,256,256]{2,1,0:T(8,128)(2,1)S(1)}, bf16[8,256,256]{2,1,0:T(8,128)(2,1)S(1)}, u32[]{:S(2)}, u32[]{:S(2)}) %collective-permute-start.5) | collective-permute-done | bytes 1048608 | tf_op jit(solution)/shard_map/ppermute | solution.py:405
  76.2 0.0 collective-permute-done.6.refs_7_
  76.2 10.0 %collective-permute-done.7.refs_8_ = bf16[8,256,256]{2,1,0:T(8,128)(2,1)S(1)} collective-permute-done((bf16[8,256,256]{2,1,0:T(8,128)(2,1)S(1)}, bf16[8,256,256]{2,1,0:T(8,128)(2,1)S(1)}, u32[]{:S(2)}, u32[]{:S(2)}) %collective-permute-start.7) | collective-permute-done | bytes 1048608 | tf_op jit(solution)/shard_map/ppermute | solution.py:405
  86.2 9.3 %collective-permute-done.8.refs_9_ = bf16[8,256,256]{2,1,0:T(8,128)(2,1)S(1)} collective-permute-done((bf16[8,256,256]{2,1,0:T(8,128)(2,1)S(1)}, bf16[8,256,256]{2,1,0:T(8,128)(2,1)S(1)}, u32[]{:S(2)}, u32[]{:S(2)}) %collective-permute-start.8) | collective-permute-done | bytes 1048608 | tf_op jit(solution)/shard_map/ppermute | solution.py:405
  95.5 0.0 copy-done.6
  95.5 0.0 copy-done.7
  95.5 0.0 copy-done.8
  95.5 1.1 %copy-done.9 = bf16[8,256,256]{2,1,0:T(8,128)(2,1)} copy-done((bf16[8,256,256]{2,1,0:T(8,128)(2,1)}, bf16[8,256,256]{2,1,0:T(8,128)(2,1)S(1)}, u32[]{:S(2)}) %copy-start.9) | copy-done | bytes 1048600
  96.6 0.0 copy-done.2
  96.6 5.7 %products.1 = f32[512,2048]{1,0:T(8,128)} custom-call(s32[768]{0:T(1024)} %get-tuple-element.12.lists, bf16[8,256,256]{2,1,0:T(8,128)(2,1)} %bitcast.11, bf16[8,256,256]{2,1,0:T(8,128)(2,1)} %collective-permute-done.refs_1_, bf16[8,256,256]{2,1,0:T(8,128)(2,1)} %collective-permute-done.1.refs_2_, ...), custom_call_target="tpu_custom_call", output_to_operand_aliasing={{}: (11, {})} | custom-call | flops 1000000000 | bytes 12582912 | tf_op jit(solution)/shard_map/products/pallas_call | solution.py:409
  (12 shorter events, 0.0 us)
Async XLA Ops:
  0.0 35.8 %copy-start.4 = (s32[640]{0:T(1024)S(1)}, s32[640]{0:T(1024)}, u32[]{:S(2)}) copy-start(s32[640]{0:T(1024)} %constant.18.clone.source) | copy-start | bytes 7684
  0.0 35.8 %copy-start = (bf16[1,1,8,256,256]{4,3,2,1,0:T(8,128)(2,1)S(1)}, bf16[1,1,8,256,256]{4,3,2,1,0:T(8,128)(2,1)}, u32[]{:S(2)}) copy-start(bf16[1,1,8,256,256]{4,3,2,1,0:T(8,128)(2,1)} %param.8) | copy-start | bytes 3145732
  0.0 27.7 %collective-permute-start.3 = (bf16[8,256,256]{2,1,0:T(8,128)(2,1)}, bf16[8,256,256]{2,1,0:T(8,128)(2,1)S(1)}, u32[]{:S(2)}, u32[]{:S(2)}) collective-permute-start(bf16[8,256,256]{2,1,0:T(8,128)(2,1)} %bitcast.7), channel_id=1, source_target_pairs={{0,12},{1,63},{2,10},{3,60},{4,64},{5,37},{6,14},{7,113},{8,7},{9,... | collective-permute-start | bytes 3145736 | tf_op jit(solution)/shard_map/ppermute | solution.py:380
  3.4 24.3 %collective-permute-start.2 = (bf16[8,256,256]{2,1,0:T(8,128)(2,1)}, bf16[8,256,256]{2,1,0:T(8,128)(2,1)S(1)}, u32[]{:S(2)}, u32[]{:S(2)}) collective-permute-start(bf16[8,256,256]{2,1,0:T(8,128)(2,1)} %bitcast.8), channel_id=1, source_target_pairs={{0,8},{1,16},{2,45},{3,11},{4,12},{5,53},{6,96},{9,105},{10,1},{11... | collective-permute-start | bytes 3145736 | tf_op jit(solution)/shard_map/ppermute | solution.py:380
  6.0 29.8 %collective-permute-start.1 = (bf16[8,256,256]{2,1,0:T(8,128)(2,1)}, bf16[8,256,256]{2,1,0:T(8,128)(2,1)}, u32[]{:S(2)}, u32[]{:S(2)}) collective-permute-start(bf16[8,256,256]{2,1,0:T(8,128)(2,1)} %bitcast.9), channel_id=1, source_target_pairs={{1,97},{2,82},{3,67},{5,90},{6,5},{7,23},{8,15},{9,8},{10,27},{11,... | collective-permute-start | bytes 3145736 | tf_op jit(solution)/shard_map/ppermute | solution.py:380
  8.3 27.5 %collective-permute-start = (bf16[8,256,256]{2,1,0:T(8,128)(2,1)}, bf16[8,256,256]{2,1,0:T(8,128)(2,1)}, u32[]{:S(2)}, u32[]{:S(2)}) collective-permute-start(bf16[8,256,256]{2,1,0:T(8,128)(2,1)} %bitcast.10), channel_id=1, source_target_pairs={{1,9},{3,2},{5,4},{11,10},{17,16},{18,24},{19,18},{20,27},{21,20},... | collective-permute-start | bytes 3145736 | tf_op jit(solution)/shard_map/ppermute | solution.py:380
  27.7 68.9 %copy-start.1 = (bf16[8,256,256]{2,1,0:T(8,128)(2,1)}, bf16[8,256,256]{2,1,0:T(8,128)(2,1)S(1)}, u32[]{:S(2)}) copy-start(bf16[8,256,256]{2,1,0:T(8,128)(2,1)S(1)} %collective-permute-done.3.refs_4_) | copy-start | bytes 3145732
  27.7 68.9 %copy-start.2 = (bf16[8,256,256]{2,1,0:T(8,128)(2,1)}, bf16[8,256,256]{2,1,0:T(8,128)(2,1)S(1)}, u32[]{:S(2)}) copy-start(bf16[8,256,256]{2,1,0:T(8,128)(2,1)S(1)} %collective-permute-done.2.refs_3_) | copy-start | bytes 3145732
  35.8 0.7 copy-start.3
  38.9 33.2 %collective-permute-start.4 = (bf16[8,256,256]{2,1,0:T(8,128)(2,1)S(1)}, bf16[8,256,256]{2,1,0:T(8,128)(2,1)S(1)}, u32[]{:S(2)}, u32[]{:S(2)}) collective-permute-start(bf16[8,256,256]{2,1,0:T(8,128)(2,1)S(1)} %get-tuple-element.13), channel_id=1, source_target_pairs={{0,7},{1,16},{3,53},{4,48},{5,64},{6,22},{7,15},{8,4},{9,1},{10,9}... | collective-permute-start | bytes 3145736 | tf_op jit(solution)/shard_map/ppermute | solution.py:405
  52.4 23.8 %collective-permute-start.5 = (bf16[8,256,256]{2,1,0:T(8,128)(2,1)S(1)}, bf16[8,256,256]{2,1,0:T(8,128)(2,1)S(1)}, u32[]{:S(2)}, u32[]{:S(2)}) collective-permute-start(bf16[8,256,256]{2,1,0:T(8,128)(2,1)S(1)} %get-tuple-element.14), channel_id=1, source_target_pairs={{0,112},{1,32},{3,19},{4,11},{5,13},{6,5},{7,23},{8,12},{9,122},{1... | collective-permute-start | bytes 3145736 | tf_op jit(solution)/shard_map/ppermute | solution.py:405
  54.3 21.9 %collective-permute-start.6 = (bf16[8,256,256]{2,1,0:T(8,128)(2,1)S(1)}, bf16[8,256,256]{2,1,0:T(8,128)(2,1)S(1)}, u32[]{:S(2)}, u32[]{:S(2)}) collective-permute-start(bf16[8,256,256]{2,1,0:T(8,128)(2,1)S(1)} %get-tuple-element.15), channel_id=1, source_target_pairs={{1,0},{2,48},{3,27},{4,75},{5,106},{6,38},{7,14},{8,120},{9,24},{1... | collective-permute-start | bytes 3145736 | tf_op jit(solution)/shard_map/ppermute | solution.py:405
  55.6 30.6 %collective-permute-start.7 = (bf16[8,256,256]{2,1,0:T(8,128)(2,1)S(1)}, bf16[8,256,256]{2,1,0:T(8,128)(2,1)S(1)}, u32[]{:S(2)}, u32[]{:S(2)}) collective-permute-start(bf16[8,256,256]{2,1,0:T(8,128)(2,1)S(1)} %get-tuple-element.16), channel_id=1, source_target_pairs={{0,16},{1,2},{2,1},{3,11},{4,5},{5,12},{6,7},{7,120},{9,25},{10,9}... | collective-permute-start | bytes 3145736 | tf_op jit(solution)/shard_map/ppermute | solution.py:405
  57.5 38.0 %collective-permute-start.8 = (bf16[8,256,256]{2,1,0:T(8,128)(2,1)S(1)}, bf16[8,256,256]{2,1,0:T(8,128)(2,1)S(1)}, u32[]{:S(2)}, u32[]{:S(2)}) collective-permute-start(bf16[8,256,256]{2,1,0:T(8,128)(2,1)S(1)} %get-tuple-element.17), channel_id=1, source_target_pairs={{0,1},{2,3},{3,32},{4,52},{5,21},{7,6},{9,8},{11,27},{13,12},{15,1... | collective-permute-start | bytes 3145736 | tf_op jit(solution)/shard_map/ppermute | solution.py:405
  72.1 24.5 %copy-start.5 = (bf16[8,256,256]{2,1,0:T(8,128)(2,1)}, bf16[8,256,256]{2,1,0:T(8,128)(2,1)S(1)}, u32[]{:S(2)}) copy-start(bf16[8,256,256]{2,1,0:T(8,128)(2,1)S(1)} %collective-permute-done.4.refs_5_) | copy-start | bytes 3145732
  76.2 19.3 %copy-start.6 = (bf16[8,256,256]{2,1,0:T(8,128)(2,1)}, bf16[8,256,256]{2,1,0:T(8,128)(2,1)S(1)}, u32[]{:S(2)}) copy-start(bf16[8,256,256]{2,1,0:T(8,128)(2,1)S(1)} %collective-permute-done.5.refs_6_) | copy-start | bytes 3145732
  76.2 19.3 %copy-start.7 = (bf16[8,256,256]{2,1,0:T(8,128)(2,1)}, bf16[8,256,256]{2,1,0:T(8,128)(2,1)S(1)}, u32[]{:S(2)}) copy-start(bf16[8,256,256]{2,1,0:T(8,128)(2,1)S(1)} %collective-permute-done.6.refs_7_) | copy-start | bytes 3145732
  86.2 9.3 %copy-start.8 = (bf16[8,256,256]{2,1,0:T(8,128)(2,1)}, bf16[8,256,256]{2,1,0:T(8,128)(2,1)S(1)}, u32[]{:S(2)}) copy-start(bf16[8,256,256]{2,1,0:T(8,128)(2,1)S(1)} %collective-permute-done.7.refs_8_) | copy-start | bytes 3145732
  95.5 1.1 %copy-start.9 = (bf16[8,256,256]{2,1,0:T(8,128)(2,1)}, bf16[8,256,256]{2,1,0:T(8,128)(2,1)S(1)}, u32[]{:S(2)}) copy-start(bf16[8,256,256]{2,1,0:T(8,128)(2,1)S(1)} %collective-permute-done.8.refs_9_) | copy-start | bytes 3145732

commit v4 on v3

v4 whole, which is shorter than its diff:
```python
import functools

import jax
import jax.numpy as jnp
import numpy as np
from jax import lax
from jax.experimental import pallas as pl
from jax.experimental.pallas import tpu as pltpu
from jax.sharding import PartitionSpec as P

BS = 256
CB = 8
SLOTS = 8
SR = 2
NB = 128
NR = 8
NC = 16
ND = NR * NC
MIB = 1024 * 1024
FETCH = 640

FIRST = [
    [
        (1, 9, 1), (3, 2, 3), (5, 4, 5), (9, 8, 9), (11, 10, 11), (17, 29, 17), (18, 17, 18), (19, 18, 19),
        (20, 33, 20), (21, 20, 21), (22, 107, 22), (23, 81, 23), (25, 16, 25), (28, 27, 28), (29, 28, 29), (30, 21, 30),
        (31, 30, 31), (35, 99, 35), (36, 41, 36), (38, 35, 38), (39, 115, 39), (40, 37, 40), (43, 26, 43), (46, 43, 46),
        (52, 116, 52), (53, 57, 53), (54, 101, 54), (55, 52, 55), (56, 61, 56), (58, 63, 58), (60, 56, 60), (62, 50, 62),
        (68, 64, 68), (69, 117, 69), (70, 86, 70), (71, 66, 71), (73, 84, 73), (76, 124, 76), (77, 109, 77), (85, 80, 85),
        (86, 103, 86), (87, 82, 87), (94, 5, 94), (95, 90, 95), (102, 118, 102), (103, 22, 103), (104, 105, 104), (105, 89, 105),
        (106, 58, 106), (108, 102, 108), (110, 111, 110), (111, 108, 111), (119, 7, 119), (121, 122, 121), (124, 60, 124),
    ],
    [
        (1, 97, 1), (2, 45, 2), (3, 11, 3), (5, 90, 5), (6, 14, 6), (7, 23, 7), (9, 0, 9), (10, 27, 10),
        (11, 2, 11), (12, 76, 12), (13, 4, 13), (14, 30, 14), (15, 6, 15), (17, 16, 17), (18, 24, 18), (19, 83, 19),
        (20, 19, 20), (21, 49, 21), (22, 20, 22), (23, 22, 23), (25, 121, 25), (26, 9, 26), (27, 18, 27), (28, 94, 28),
        (29, 61, 29), (30, 29, 30), (34, 39, 34), (35, 54, 35), (36, 33, 36), (37, 43, 37), (38, 100, 38), (40, 98, 40),
        (41, 38, 41), (42, 32, 42), (43, 107, 43), (44, 41, 44), (45, 127, 45), (46, 78, 46), (47, 36, 47), (51, 48, 51),
        (52, 70, 52), (53, 85, 53), (54, 58, 54), (55, 116, 55), (56, 40, 56), (57, 53, 57), (58, 10, 58), (59, 123, 59),
        (60, 124, 60), (61, 50, 61), (62, 47, 62), (69, 65, 69), (70, 66, 70), (71, 74, 71), (72, 56, 72), (73, 69, 73),
        (74, 26, 74), (75, 79, 75), (77, 28, 77), (78, 44, 78), (79, 67, 79), (85, 5, 85), (86, 21, 86), (87, 117, 87),
        (88, 91, 88), (89, 73, 89), (90, 92, 90), (91, 101, 91), (93, 80, 93), (94, 126, 94), (95, 81, 95), (102, 103, 102),
        (103, 96, 103), (105, 99, 105), (107, 86, 107), (108, 109, 108), (111, 104, 111), (119, 120, 119), (120, 113, 120), (121, 89, 121),
        (122, 114, 122), (123, 75, 123), (124, 87, 124), (125, 118, 125), (126, 119, 126),
    ],
    [
        (0, 12, 0), (1, 16, 1), (2, 10, 2), (3, 60, 3), (4, 64, 4), (5, 53, 5), (6, 96, 6), (8, 7, 8),
        (10, 1, 10), (11, 75, 11), (12, 11, 12), (13, 45, 13), (14, 80, 14), (15, 124, 15), (17, 113, 17), (18, 47, 18),
        (19, 26, 19), (20, 27, 20), (21, 83, 21), (22, 28, 22), (23, 121, 23), (24, 23, 24), (27, 91, 27), (28, 19, 28),
        (29, 77, 29), (30, 46, 30), (31, 22, 31), (34, 114, 34), (35, 18, 35), (36, 100, 36), (37, 35, 37), (38, 43, 38),
        (39, 37, 39), (40, 24, 40), (41, 98, 41), (42, 39, 42), (43, 32, 43), (44, 108, 44), (45, 93, 45), (46, 44, 46),
        (47, 63, 47), (51, 3, 51), (52, 48, 52), (53, 86, 53), (54, 50, 54), (55, 71, 55), (56, 67, 56), (57, 61, 57),
        (58, 55, 58), (59, 56, 59), (60, 49, 60), (61, 57, 61), (63, 59, 63), (68, 72, 68), (69, 20, 69), (70, 73, 70),
        (71, 52, 71), (72, 76, 72), (73, 41, 73), (74, 84, 74), (75, 70, 75), (76, 8, 76), (77, 65, 77), (78, 66, 78),
        (79, 36, 79), (85, 117, 85), (86, 88, 86), (88, 82, 88), (89, 69, 89), (90, 42, 90), (91, 94, 91), (92, 95, 92),
        (93, 13, 93), (94, 81, 94), (95, 29, 95), (102, 106, 102), (103, 119, 103), (104, 38, 104), (105, 54, 105), (106, 74, 106),
        (107, 109, 107), (109, 111, 109), (110, 118, 110), (111, 97, 111), (119, 112, 119), (121, 105, 121), (122, 123, 122), (123, 115, 123),
        (124, 125, 124), (125, 126, 125), (127, 15, 127),
    ],
    [
        (0, 8, 0), (1, 63, 1), (2, 82, 2), (3, 67, 3), (4, 12, 4), (5, 37, 5), (6, 5, 6), (7, 113, 7),
        (8, 15, 8), (9, 105, 9), (10, 40, 10), (11, 56, 11), (12, 48, 12), (13, 72, 13), (14, 6, 14), (15, 120, 15),
        (17, 1, 17), (18, 38, 18), (19, 53, 19), (20, 68, 20), (21, 19, 21), (22, 65, 22), (23, 97, 23), (24, 31, 24),
        (26, 24, 26), (27, 26, 27), (28, 41, 28), (29, 20, 29), (30, 89, 30), (31, 47, 31), (34, 32, 34), (35, 62, 35),
        (36, 70, 36), (37, 84, 37), (38, 54, 38), (39, 36, 39), (41, 9, 41), (42, 10, 42), (43, 18, 43), (44, 33, 44),
        (45, 58, 45), (46, 35, 46), (47, 44, 47), (52, 57, 52), (53, 49, 53), (54, 86, 54), (55, 59, 55), (56, 52, 56),
        (57, 25, 57), (58, 115, 58), (59, 55, 59), (60, 3, 60), (61, 109, 61), (62, 94, 62), (63, 79, 63), (68, 71, 68),
        (69, 95, 69), (70, 102, 70), (71, 124, 71), (72, 75, 72), (73, 76, 73), (74, 78, 74), (75, 11, 75), (76, 64, 76),
        (77, 73, 77), (78, 74, 78), (79, 60, 79), (85, 87, 85), (86, 81, 86), (87, 90, 87), (88, 42, 88), (89, 83, 89),
        (90, 69, 90), (91, 27, 91), (92, 101, 92), (93, 88, 93), (94, 29, 94), (95, 21, 95), (102, 96, 102), (103, 104, 103),
        (104, 98, 104), (105, 106, 105), (106, 99, 106), (107, 100, 107), (108, 110, 108), (109, 13, 109), (110, 126, 110), (111, 30, 111),
        (120, 7, 120), (121, 114, 121), (123, 116, 123), (124, 117, 124), (126, 14, 126), (127, 112, 127),
    ],
]
SECOND = [
    [
        (0, 112, 0), (1, 16, 10), (2, 48, 11), (3, 32, 3), (4, 11, 4), (5, 13, 5), (6, 22, 6), (7, 15, 7),
        (8, 4, 76), (9, 24, 9), (10, 9, 10), (11, 116, 75), (12, 3, 12), (13, 29, 109), (14, 30, 126), (15, 0, 8),
        (16, 31, 25), (17, 1, 18), (18, 2, 35), (19, 27, 21), (20, 87, 69), (21, 5, 86), (22, 21, 31), (23, 39, 23),
        (24, 17, 26), (25, 23, 25), (26, 25, 19), (27, 77, 20), (28, 33, 28), (30, 46, 14), (31, 81, 31), (32, 41, 43),
        (33, 18, 36), (35, 50, 46), (36, 82, 47), (37, 44, 39), (38, 36, 38), (39, 122, 42), (40, 45, 40), (41, 26, 44),
        (42, 47, 42), (43, 92, 37), (44, 74, 47), (46, 62, 30), (47, 43, 62), (48, 115, 51), (49, 53, 21), (50, 35, 61),
        (53, 61, 19), (54, 38, 105), (55, 54, 58), (56, 52, 72), (57, 79, 52), (58, 42, 45), (59, 63, 59), (61, 49, 61),
        (62, 58, 62), (63, 51, 63), (64, 68, 4), (65, 98, 22), (66, 65, 70), (67, 83, 3), (68, 84, 20), (69, 72, 69),
        (70, 78, 36), (71, 123, 55), (72, 88, 13), (73, 57, 89), (74, 20, 78), (75, 71, 123), (76, 64, 12), (77, 19, 29),
        (78, 94, 78), (79, 67, 63), (80, 95, 85), (81, 89, 94), (82, 126, 87), (83, 91, 21), (84, 69, 37), (85, 101, 53),
        (86, 70, 107), (87, 37, 87), (88, 111, 86), (89, 73, 30), (90, 80, 5), (91, 107, 27), (92, 86, 92), (93, 34, 45),
        (94, 93, 91), (95, 12, 92), (96, 105, 6), (97, 114, 23), (98, 97, 104), (99, 40, 35), (100, 66, 38), (101, 109, 54),
        (102, 110, 70), (103, 118, 86), (104, 106, 104), (105, 121, 9), (106, 108, 106), (107, 59, 107), (109, 102, 109), (110, 28, 108),
        (111, 127, 111), (112, 120, 127), (113, 96, 7), (114, 55, 122), (115, 99, 58), (116, 100, 52), (117, 125, 87), (118, 6, 110),
        (119, 103, 126), (120, 104, 15), (121, 113, 25), (122, 90, 122), (123, 124, 123), (124, 117, 71), (126, 14, 110), (127, 119, 127),
    ],
    [
        (0, 7, 0), (1, 32, 10), (3, 27, 60), (4, 75, 4), (5, 64, 5), (6, 5, 14), (7, 120, 7), (8, 12, 76),
        (9, 25, 41), (10, 26, 58), (11, 56, 12), (12, 4, 12), (13, 61, 13), (15, 112, 8), (16, 1, 25), (17, 23, 17),
        (18, 33, 27), (19, 49, 28), (20, 86, 69), (21, 37, 95), (22, 6, 103), (23, 30, 23), (24, 106, 26), (25, 9, 25),
        (26, 16, 26), (27, 90, 10), (28, 29, 22), (29, 24, 17), (30, 88, 14), (31, 97, 24), (32, 114, 42), (33, 18, 44),
        (34, 2, 34), (35, 36, 46), (36, 52, 79), (37, 45, 39), (38, 22, 104), (39, 40, 34), (40, 46, 40), (41, 42, 44),
        (42, 84, 90), (43, 108, 38), (44, 66, 47), (45, 38, 2), (47, 105, 31), (48, 78, 52), (49, 35, 53), (50, 19, 61),
        (53, 62, 19), (54, 50, 38), (55, 3, 59), (56, 48, 59), (57, 58, 53), (58, 54, 106), (59, 60, 55), (60, 44, 79),
        (61, 57, 29), (63, 31, 1), (64, 71, 76), (65, 81, 22), (66, 65, 78), (67, 83, 56), (68, 76, 20), (69, 73, 69),
        (70, 69, 36), (71, 67, 55), (72, 68, 72), (73, 109, 70), (74, 70, 106), (76, 79, 76), (77, 125, 77), (78, 74, 46),
        (79, 95, 79), (80, 96, 14), (81, 113, 23), (82, 98, 2), (83, 17, 19), (84, 100, 74), (86, 94, 53), (87, 21, 87),
        (88, 72, 88), (89, 91, 89), (90, 89, 95), (91, 53, 88), (92, 28, 92), (93, 77, 45), (94, 92, 28), (95, 87, 92),
        (96, 80, 6), (99, 115, 35), (100, 99, 38), (101, 85, 91), (102, 101, 70), (103, 110, 86), (105, 39, 121), (106, 111, 102),
        (107, 43, 107), (108, 14, 111), (109, 93, 61), (111, 103, 109), (112, 127, 119), (113, 121, 7), (115, 82, 39), (116, 55, 123),
        (117, 118, 87), (118, 117, 125), (119, 126, 103), (120, 104, 120), (121, 122, 23), (123, 59, 123), (124, 116, 76), (126, 13, 94),
    ],
    [
        (1, 2, 10), (3, 53, 3), (4, 48, 4), (5, 12, 5), (6, 38, 6), (7, 14, 7), (8, 120, 8), (9, 1, 26),
        (10, 9, 2), (11, 27, 75), (12, 60, 12), (13, 5, 93), (14, 13, 14), (15, 7, 127), (16, 22, 1), (17, 114, 18),
        (18, 17, 27), (19, 18, 28), (20, 21, 22), (21, 28, 21), (22, 89, 31), (23, 29, 23), (24, 25, 26), (25, 83, 57),
        (26, 42, 74), (27, 26, 28), (28, 76, 28), (29, 31, 17), (30, 81, 30), (31, 113, 24), (32, 40, 43), (33, 34, 44),
        (35, 41, 35), (36, 90, 47), (37, 122, 39), (38, 46, 41), (39, 55, 39), (40, 106, 10), (41, 57, 73), (42, 58, 90),
        (43, 44, 38), (44, 110, 78), (45, 37, 2), (47, 97, 31), (48, 19, 52), (49, 69, 21), (50, 35, 62), (51, 63, 51),
        (52, 36, 71), (53, 54, 57), (54, 70, 38), (55, 51, 55), (56, 32, 11), (58, 100, 106), (59, 124, 55), (60, 52, 3),
        (61, 49, 29), (62, 59, 62), (63, 30, 1), (64, 3, 4), (67, 66, 79), (68, 116, 68), (69, 85, 90), (70, 77, 36),
        (71, 87, 71), (72, 64, 13), (73, 4, 77), (74, 73, 78), (75, 67, 72), (76, 72, 76), (78, 62, 46), (79, 75, 79),
        (80, 117, 93), (81, 80, 94), (82, 16, 2), (83, 65, 21), (84, 93, 37), (86, 20, 70), (87, 71, 124), (89, 84, 89),
        (90, 82, 5), (91, 86, 91), (93, 125, 93), (94, 88, 94), (95, 111, 95), (96, 98, 6), (97, 23, 1), (98, 47, 41),
        (99, 33, 35), (100, 107, 38), (101, 108, 54), (102, 104, 102), (104, 105, 103), (107, 99, 22), (108, 92, 44), (109, 43, 61),
        (110, 103, 110), (111, 118, 109), (114, 39, 122), (115, 123, 39), (116, 115, 55), (117, 101, 69), (118, 6, 102), (119, 127, 103),
        (120, 112, 15), (122, 74, 122), (124, 96, 15), (126, 45, 125), (127, 50, 45),
    ],
    [
        (0, 16, 9), (1, 0, 1), (2, 1, 2), (3, 19, 60), (4, 52, 4), (5, 106, 6), (7, 6, 7), (9, 122, 26),
        (10, 2, 42), (11, 72, 12), (12, 15, 0), (13, 95, 93), (14, 13, 6), (15, 31, 15), (17, 98, 18), (18, 33, 19),
        (19, 92, 21), (20, 4, 69), (21, 20, 30), (22, 38, 22), (23, 21, 23), (24, 8, 24), (25, 41, 57), (26, 10, 43),
        (27, 26, 20), (28, 12, 77), (29, 28, 30), (30, 22, 111), (31, 30, 24), (33, 49, 20), (34, 47, 34), (35, 34, 37),
        (38, 39, 18), (40, 24, 10), (41, 57, 28), (42, 37, 88), (43, 42, 37), (44, 36, 78), (45, 46, 2), (47, 45, 47),
        (48, 56, 51), (49, 50, 53), (50, 51, 62), (52, 71, 52), (53, 54, 19), (54, 55, 35), (56, 40, 11), (57, 58, 61),
        (58, 43, 45), (59, 11, 59), (60, 44, 124), (61, 62, 57), (63, 60, 63), (64, 67, 4), (65, 64, 69), (67, 48, 3),
        (69, 53, 89), (70, 100, 75), (71, 116, 71), (72, 80, 13), (73, 74, 70), (74, 70, 74), (75, 91, 11), (77, 65, 29),
        (78, 77, 74), (79, 75, 63), (80, 87, 93), (81, 82, 95), (82, 81, 87), (83, 99, 19), (84, 69, 74), (85, 88, 85),
        (86, 93, 53), (87, 89, 87), (88, 90, 88), (89, 23, 121), (90, 83, 5), (91, 25, 27), (93, 35, 45), (94, 78, 62),
        (95, 94, 69), (96, 97, 6), (97, 96, 111), (98, 114, 41), (99, 32, 35), (100, 84, 36), (101, 117, 92), (102, 86, 108),
        (104, 105, 111), (105, 73, 105), (106, 107, 106), (107, 123, 43), (108, 101, 108), (109, 27, 61), (110, 104, 110), (111, 110, 109),
        (113, 112, 7), (114, 113, 121), (115, 66, 39), (116, 3, 52), (118, 103, 125), (119, 118, 126), (120, 121, 120), (123, 115, 59),
        (124, 108, 60), (126, 29, 125),
    ],
    [
        (0, 1, 9), (2, 3, 11), (3, 11, 60), (4, 5, 13), (5, 21, 94), (6, 7, 15), (7, 23, 120), (9, 8, 1),
        (11, 10, 3), (13, 12, 13), (15, 14, 15), (17, 16, 18), (18, 2, 43), (19, 18, 20), (20, 27, 29), (22, 54, 22),
        (23, 22, 24), (24, 25, 18), (25, 24, 25), (27, 43, 91), (28, 20, 77), (29, 45, 95), (30, 6, 111), (31, 29, 31),
        (32, 33, 43), (33, 34, 36), (35, 50, 37), (36, 37, 47), (37, 38, 40), (38, 39, 41), (41, 42, 36), (42, 40, 42),
        (43, 58, 46), (44, 28, 78), (45, 32, 2), (46, 65, 30), (47, 46, 18), (48, 49, 52), (49, 48, 60), (50, 51, 54),
        (51, 55, 51), (52, 53, 56), (53, 99, 57), (54, 35, 54), (56, 57, 60), (57, 56, 52), (58, 59, 54), (59, 52, 63),
        (60, 61, 3), (61, 60, 56), (62, 63, 35), (63, 62, 58), (64, 76, 4), (65, 64, 77), (66, 67, 71), (67, 74, 79),
        (68, 69, 20), (69, 68, 73), (70, 71, 75), (71, 4, 68), (72, 79, 68), (73, 72, 77), (74, 75, 71), (76, 77, 73),
        (77, 73, 29), (78, 66, 46), (79, 78, 75), (80, 104, 14), (81, 80, 86), (82, 83, 88), (83, 84, 21), (84, 85, 37),
        (85, 19, 53), (86, 70, 54), (87, 103, 87), (88, 89, 86), (89, 92, 89), (90, 91, 5), (91, 41, 27), (92, 93, 90),
        (94, 110, 94), (95, 94, 92), (96, 97, 103), (97, 113, 1), (98, 82, 40), (99, 98, 105), (100, 101, 107), (101, 100, 54),
        (102, 36, 70), (103, 102, 86), (104, 88, 104), (106, 107, 105), (107, 106, 22), (109, 108, 107), (110, 44, 108), (111, 96, 110),
        (113, 112, 120), (114, 115, 122), (115, 114, 39), (117, 116, 124), (118, 87, 125), (119, 118, 103), (124, 125, 71), (126, 127, 126),
    ],
]
NRELAY = 4
NBUF = 1 + len(FIRST) + len(SECOND)


def holders():
    held = [{d: 0} for d in range(ND)]
    for n, edges in enumerate(FIRST):
        for _, there, tile in edges:
            held[there].setdefault(tile, 1 + n)
    source = np.zeros((len(SECOND), ND), np.int32)
    for n, edges in enumerate(SECOND):
        for here, _, tile in edges:
            source[n, here] = held[here][tile]
    for n, edges in enumerate(SECOND):
        for _, there, tile in edges:
            held[there].setdefault(tile, 1 + len(FIRST) + n)
    place = np.zeros((ND, 8), np.int32)
    for a in range(NR):
        for b in range(NC):
            for s in range(2):
                k = (a + b + s) % NR
                low = b < NR
                need = [
                    (k, b) if not low or k <= b else (b, k),
                    (b, k + NR) if low else (k, b) if k + NR <= b else (b - NR, k + NR),
                    (a, k) if a <= k else (k, a),
                    (a, k + NR),
                ]
                d = a * NC + b
                for kind, (r, c) in enumerate(need):
                    place[d, 4 * s + kind] = held[d][r * NC + c]
    return source, place


def slot_table(occupancy):
    i = np.arange(NB)
    before_col = (i[:, None] // CB == i[None, :] // CB) & (i[:, None] < i[None, :])
    panel = i[:, None] // CB == i[None, :] // CB
    before_row = (i[:, None] // CB % NR == i[None, :] // CB % NR) & (i[None, :] < i[:, None])
    occ = occupancy.astype(jnp.float32)
    dot = functools.partial(jnp.dot, precision=lax.Precision.HIGHEST)
    rank = dot(occ, jnp.asarray(before_col, jnp.float32)) + dot(
        jnp.asarray(before_row, jnp.float32), dot(occ, jnp.asarray(panel, jnp.float32))
    )
    return jnp.where(occupancy == 1, rank.astype(jnp.int32), -1)


def pick_kernel(source, lists, *refs):
    bufs, outs, sems = refs[: 1 + NRELAY], refs[1 + NRELAY : -1], refs[-1]
    here = lax.axis_index("row") * NC + lax.axis_index("col")
    for n, out in enumerate(outs):
        which = source[n * ND + here]
        for i in range(1 + NRELAY):

            @pl.when(which == i)
            def _():
                pltpu.make_async_copy(bufs[i], out, sems.at[n]).start()

    for n, out in enumerate(outs):
        pltpu.make_async_copy(bufs[0], out, sems.at[n]).wait()


def index_kernel(table, place, lists, blank, used):
    a = lax.axis_index("row")
    b = lax.axis_index("col")
    here = a * NC + b
    blank[...] = jnp.zeros_like(blank)

    def clear_used(t, carry):
        used[t] = 0
        return carry

    lax.fori_loop(0, 80, clear_used, 0)

    def step(t, n):
        s = t // 32
        kk = lax.rem(t // 2, 16)
        i = lax.rem(t, 2)
        half = kk // CB
        k = lax.rem(a + b + s, NR)
        inner = (half * NR + k) * CB + lax.rem(kk, CB)
        row = a * CB + i
        lslot = table[jnp.minimum(row, inner), jnp.maximum(row, inner)]
        lplace = (4 * s + 2 + half) * SLOTS + lslot
        turned = jnp.where(row > inner, 1, 0)

        def one_col(j, n0):
            n, fresh = n0
            col = b * CB + j
            rslot = table[jnp.minimum(inner, col), jnp.maximum(inner, col)]
            rplace = (4 * s + half) * SLOTS + rslot
            hit = rslot >= 0

            @pl.when(hit)
            def _():
                first = jnp.where(used[64 + i * CB + j] == 0, 1, 0)
                lists[n] = (
                    lplace
                    + (rplace << 6)
                    + ((i * CB + j) << 12)
                    + (turned << 16)
                    + (jnp.where(inner > col, 1, 0) << 17)
                    + (fresh << 18)
                    + (first << 19)
                    + ((1 - used[lplace]) << 21)
                    + ((1 - used[rplace]) << 22)
                )
                used[64 + i * CB + j] = 1
                used[lplace] = 1
                used[rplace] = 1

            one = jnp.where(hit, 1, 0)
            return n + one, fresh * (1 - one)

        return lax.cond(lslot >= 0, lambda m: lax.fori_loop(0, CB, one_col, (m, 1))[0], lambda m: m, n)

    count = lax.fori_loop(0, 64, step, 1)
    lists[0] = count

    def mark_last(q, carry):
        at = count - 1 - q
        code = lists[at]
        to = 64 + ((code >> 12) & 15)

        @pl.when(used[to] == 1)
        def _():
            lists[at] = code + (1 << 20)
            used[to] = 2

        return carry

    lax.fori_loop(0, count - 1, mark_last, 0)
    for t in range(16):
        lists[FETCH + 112 + t] = jnp.minimum(used[64 + t], 1)

    def by_buffer(buf, n):
        lists[FETCH + buf] = n

        def by_kind(kind, n):
            def by_slot(slot, n):
                @pl.when(used[kind * SLOTS + slot] == 1)
                def _():
                    lists[FETCH + n] = kind * SLOTS + slot

                return n + used[kind * SLOTS + slot]

            return lax.cond(
                place[here * 8 + kind] == buf, lambda m: lax.fori_loop(0, SLOTS, by_slot, m), lambda m: m, n
            )

        return lax.fori_loop(0, 8, by_kind, n)

    lists[FETCH + NBUF] = lax.fori_loop(0, NBUF, by_buffer, 32)


def product_kernel(lists, *refs):
    bufs = refs[:NBUF]
    blank, out, tiles, left, acc, sems, out_sems = refs[NBUF:]
    for n, buf in enumerate(bufs):

        def start(q, carry):
            t = lists[FETCH + q]
            pltpu.make_async_copy(buf.at[lax.rem(t, SLOTS)], tiles.at[t], sems.at[t]).start()
            return carry

        lax.fori_loop(lists[FETCH + n], lists[FETCH + n + 1], start, 0)

    def arrived(t):
        pltpu.make_async_copy(bufs[0].at[0], tiles.at[t], sems.at[t]).wait()

    def copy_out(t):
        return pltpu.make_async_copy(
            acc.at[t],
            out.at[pl.ds(pl.multiple_of(t // CB * BS, BS), BS), pl.ds(pl.multiple_of(lax.rem(t, CB) * BS, BS), BS)],
            out_sems.at[t],
        )

    def product(q, carry):
        code = lists[q]
        lt = tiles.at[code & 63]
        rt = tiles.at[(code >> 6) & 63]
        to = acc.at[(code >> 12) & 15]

        @pl.when(((code >> 21) & 1) == 1)
        def _():
            arrived(code & 63)

        @pl.when(((code >> 22) & 1) == 1)
        def _():
            arrived((code >> 6) & 63)

        @pl.when(((code >> 18) & 1) == 1)
        def _():
            @pl.when(((code >> 16) & 1) == 0)
            def _():
                left[...] = lt[...]

            @pl.when(((code >> 16) & 1) == 1)
            def _():
                left[...] = lt[...].T

        @pl.when(((code >> 19) & 1) == 1)
        def _():
            to[...] = jnp.zeros_like(to)

        @pl.when(((code >> 17) & 1) == 0)
        def _():
            to[...] += jnp.dot(left[...], rt[...], preferred_element_type=jnp.float32)

        @pl.when(((code >> 17) & 1) == 1)
        def _():
            to[...] += lax.dot_general(
                left[...], rt[...], (((1,), (1,)), ((), ())), preferred_element_type=jnp.float32
            )

        @pl.when(((code >> 20) & 1) == 1)
        def _():
            copy_out((code >> 12) & 15).start()

        return carry

    lax.fori_loop(1, lists[0], product, 0)
    for t in range(16):

        @pl.when(lists[FETCH + 112 + t] == 1)
        def _():
            copy_out(t).wait()


def tile_shape():
    return jax.ShapeDtypeStruct((SLOTS, BS, BS), jnp.bfloat16)


SMEM = pl.BlockSpec(memory_space=pltpu.SMEM)
ANY = pl.BlockSpec(memory_space=pl.ANY)


def local(occupancy, stored):
    own = stored.reshape(SLOTS, BS, BS)
    source, place = holders()
    bufs = [own]
    for edges in FIRST:
        bufs.append(lax.ppermute(own, ("row", "col"), [(u, v) for u, v, _ in edges]))
    lists, blank = pl.pallas_call(
        index_kernel,
        out_shape=(
            jax.ShapeDtypeStruct((FETCH + 128,), jnp.int32),
            jax.ShapeDtypeStruct((SR * BS, CB * BS), jnp.float32),
        ),
        in_specs=[SMEM, SMEM],
        out_specs=(SMEM, pl.BlockSpec(memory_space=pltpu.VMEM)),
        scratch_shapes=[pltpu.SMEM((80,), jnp.int32)],
        cost_estimate=pl.CostEstimate(flops=10**9, bytes_accessed=4 * MIB, transcendentals=0),
        name="index",
    )(slot_table(occupancy), jnp.asarray(place.reshape(-1)))
    flat_source = jnp.asarray(source.reshape(-1))
    sends = pl.pallas_call(
        pick_kernel,
        out_shape=[pltpu.VMEM((SLOTS, BS, BS), jnp.bfloat16)] * len(SECOND),
        in_specs=[SMEM, SMEM] + [ANY] * (1 + NRELAY),
        out_specs=[pl.BlockSpec(memory_space=pltpu.VMEM)] * len(SECOND),
        compiler_params=pltpu.CompilerParams(vmem_limit_bytes=16 * MIB),
        scratch_shapes=[pltpu.SemaphoreType.DMA((len(SECOND),))],
        cost_estimate=pl.CostEstimate(flops=0, bytes_accessed=2 * MIB, transcendentals=0),
        name="pick",
    )(flat_source, lists, *bufs[: 1 + NRELAY])
    later = [
        lax.ppermute(send, ("row", "col"), [(u, v) for u, v, _ in edges])
        for send, edges in zip(sends, SECOND, strict=True)
    ]
    bufs += later
    return pl.pallas_call(
        product_kernel,
        out_shape=jax.ShapeDtypeStruct((SR * BS, CB * BS), jnp.float32),
        in_specs=[SMEM] + [ANY] * (NBUF + 1),
        out_specs=ANY,
        scratch_shapes=[
            pltpu.VMEM((64, BS, BS), jnp.bfloat16),
            pltpu.VMEM((BS, BS), jnp.bfloat16),
            pltpu.VMEM((16, BS, BS), jnp.float32),
            pltpu.SemaphoreType.DMA((64,)),
            pltpu.SemaphoreType.DMA((16,)),
        ],
        input_output_aliases={1 + NBUF: 0},
        compiler_params=pltpu.CompilerParams(vmem_limit_bytes=60 * MIB),
        cost_estimate=pl.CostEstimate(flops=10**9, bytes_accessed=12 * MIB, transcendentals=0),
        name="products",
    )(lists, *bufs, blank)


def solution(mesh):
    placed = (P(), P("row", "col", None, None, None))
    return jax.shard_map(
        local, mesh=mesh, in_specs=placed, out_specs=P("row", "col"), check_vma=False
    )
```

time: 103 us -> 102 us (level)
  the two profiles are of different devices: /device:TPU:82 before, /device:TPU:5 now
where the time goes in v4:
time: 102 us
  waiting for transfers between devices  48.7 us (48%)
  starting transfers between devices  28.6 us (28%)
  Pallas kernels  18.5 us (18%)
  matrix products  4.01 us (4%)
  local copies, waits for them, and re-layouts  1.77 us (2%)
    ppermute x4, waiting for transfers between devices, local(): lax.ppermute(own, ('row', 'col'), [(u, v) for u, v, _ in edges])  26.8 us
    ppermute x5, starting transfers between devices, local(): lax.ppermute(send, ('row', 'col'), [(u, v) for u, v, _ in edges])  23.9 us
    ppermute x5, waiting for transfers between devices, local(): lax.ppermute(send, ('row', 'col'), [(u, v) for u, v, _ in edges])  21.9 us
    pallas_call x1, Pallas kernels, local(): pl.pallas_call(index_kernel, out_shape=(jax.ShapeDtypeStruct((FETCH + 128...  10.4 us
    pallas_call x1, Pallas kernels, local(): pl.pallas_call(product_kernel, out_shape=jax.ShapeDtypeStruct((SR * BS, C...  5.51 us
    ppermute x4, starting transfers between devices, local(): lax.ppermute(own, ('row', 'col'), [(u, v) for u, v, _ in edges])  4.72 us
    pallas_call x1, Pallas kernels, local(): pl.pallas_call(pick_kernel, out_shape=[pltpu.VMEM((SLOTS, BS, BS), jnp.bf...  2.59 us
  transfers between devices with their start and end apart: 9, of which 5 were waited for; matrix products, arithmetic and copies ran while one was open for 4% of the time, Pallas kernels for 10%

profile of v4, /device:TPU:5, one launch (start us, length us, event | category | flops | bytes accessed | tf_op | source)
XLA Modules:
  0.0 101.7 jit_solution(10736471661880174538)
XLA Ops:
  0.0 1.4 %collective-permute-start.3 = (bf16[8,256,256]{2,1,0:T(8,128)(2,1)}, bf16[8,256,256]{2,1,0:T(8,128)(2,1)S(1)}, u32[]{:S(2)}, u32[]{:S(2)}) collective-permute-start(bf16[8,256,256]{2,1,0:T(8,128)(2,1)} %bitcast.7), channel_id=1, source_target_pairs={{0,8},{1,63},{2,82},{3,67},{4,12},{5,37},{6,5},{7,113},{8,15},{9,1... | collective-permute-start | bytes 3145736 | tf_op jit(solution)/shard_map/ppermute | solution.py:398
  1.4 0.7 collective-permute-start.2
  2.2 1.3 %collective-permute-start.1 = (bf16[8,256,256]{2,1,0:T(8,128)(2,1)}, bf16[8,256,256]{2,1,0:T(8,128)(2,1)}, u32[]{:S(2)}, u32[]{:S(2)}) collective-permute-start(bf16[8,256,256]{2,1,0:T(8,128)(2,1)} %bitcast.9), channel_id=1, source_target_pairs={{1,97},{2,45},{3,11},{5,90},{6,14},{7,23},{9,0},{10,27},{11,2},{12... | collective-permute-start | bytes 3145736 | tf_op jit(solution)/shard_map/ppermute | solution.py:398
  3.5 1.3 %collective-permute-start = (bf16[8,256,256]{2,1,0:T(8,128)(2,1)}, bf16[8,256,256]{2,1,0:T(8,128)(2,1)}, u32[]{:S(2)}, u32[]{:S(2)}) collective-permute-start(bf16[8,256,256]{2,1,0:T(8,128)(2,1)} %bitcast.10), channel_id=1, source_target_pairs={{1,9},{3,2},{5,4},{9,8},{11,10},{17,29},{18,17},{19,18},{20,33},{2... | collective-permute-start | bytes 3145736 | tf_op jit(solution)/shard_map/ppermute | solution.py:398
  4.8 1.1 %convolution_bitcast_fusion = f32[128,128]{1,0:T(8,128)S(1)} fusion(f32[128,128]{1,0:T(8,128)} %constant.14.clone, s32[128,128]{1,0:T(8,128)} %param.7), kind=kOutput, calls=%fused_computation.3 | convolution fusion | flops 25182208 | bytes 196608 | tf_op jit(solution)/shard_map/dot_general | solution.py:197
  5.8 1.2 %fusion.2 = f32[128,128]{1,0:T(8,128)S(1)} fusion(f32[128,128]{1,0:T(8,128)} %constant.16.clone, s32[128,128]{1,0:T(8,128)} %param.7), kind=kOutput, calls=%fused_computation.4 | convolution fusion | flops 25182208 | bytes 196608 | tf_op jit(solution)/shard_map/dot_general | solution.py:198
  7.0 1.8 %fusion.1.table = s32[128,128]{1,0:T(8,128)} fusion(f32[128,128]{1,0:T(8,128)S(1)} %convolution_bitcast_fusion, f32[128,128]{1,0:T(8,128)} %constant.15.clone, f32[128,128]{1,0:T(8,128)S(1)} %fusion.2, s32[128,128]{1,0:T(8,128)} %param.7), kind=kOutput, calls=%fused_computation.2 | convolution fusion | flops 25231360 | bytes 327680 | tf_op jit(solution)/shard_map/dot_general | solution.py:197
  8.8 10.4 %index.1 = (s32[768]{0:T(1024)}, f32[512,2048]{1,0:T(8,128)}) custom-call(s32[128,128]{1,0:T(8,128)} %fusion.1.table, s32[1024]{0:T(1024)} %constant.17.clone.place), custom_call_target="tpu_custom_call" | custom-call | flops 1000000000 | bytes 4194304 | tf_op jit(solution)/shard_map/index/pallas_call | solution.py:399
  19.2 21.3 %collective-permute-done.3.refs_4_ = bf16[8,256,256]{2,1,0:T(8,128)(2,1)S(1)} collective-permute-done((bf16[8,256,256]{2,1,0:T(8,128)(2,1)}, bf16[8,256,256]{2,1,0:T(8,128)(2,1)S(1)}, u32[]{:S(2)}, u32[]{:S(2)}) %collective-permute-start.3) | collective-permute-done | bytes 1048608 | tf_op jit(solution)/shard_map/ppermute | solution.py:398
  40.5 0.0 collective-permute-done.2.refs_3_
  40.5 5.5 %collective-permute-done.1.refs_2_ = bf16[8,256,256]{2,1,0:T(8,128)(2,1)} collective-permute-done((bf16[8,256,256]{2,1,0:T(8,128)(2,1)}, bf16[8,256,256]{2,1,0:T(8,128)(2,1)}, u32[]{:S(2)}, u32[]{:S(2)}) %collective-permute-start.1) | collective-permute-done | bytes 1048608 | tf_op jit(solution)/shard_map/ppermute | solution.py:398
  46.0 0.0 collective-permute-done.refs_1_
  46.0 0.0 copy-done.4
  46.0 0.0 copy-done
  46.0 0.0 copy-start.3
  46.0 0.7 copy-done.3
  46.7 2.6 %pick.1 = (bf16[8,256,256]{2,1,0:T(8,128)(2,1)S(1)}, bf16[8,256,256]{2,1,0:T(8,128)(2,1)S(1)}, bf16[8,256,256]{2,1,0:T(8,128)(2,1)S(1)}, bf16[8,256,256]{2,1,0:T(8,128)(2,1)S(1)}, bf16[8,256,256]{2,1,0:T(8,128)(2,1)S(1)}) custom-call(s32[640]{0:T(1024)S(1)} %copy-done.4, s32[768]{0:T(1024)S(1)} %copy-done.3, bf16[8,256,256]{2,1,0:T(8,128)(2,1)S(1)} %bitcast.12, ...), custom_call_target="tpu_custom_call" | custom-call | bytes 2097152 | tf_op jit(solution)/shard_map/pick/pallas_call | solution.py:412
  49.3 1.9 %collective-permute-start.4 = (bf16[8,256,256]{2,1,0:T(8,128)(2,1)S(1)}, bf16[8,256,256]{2,1,0:T(8,128)(2,1)S(1)}, u32[]{:S(2)}, u32[]{:S(2)}) collective-permute-start(bf16[8,256,256]{2,1,0:T(8,128)(2,1)S(1)} %get-tuple-element.13), channel_id=1, source_target_pairs={{0,112},{1,16},{2,48},{3,32},{4,11},{5,13},{6,22},{7,15},{8,4},{9,... | collective-permute-start | bytes 3145736 | tf_op jit(solution)/shard_map/ppermute | solution.py:423
  51.2 1.9 %collective-permute-start.5 = (bf16[8,256,256]{2,1,0:T(8,128)(2,1)S(1)}, bf16[8,256,256]{2,1,0:T(8,128)(2,1)S(1)}, u32[]{:S(2)}, u32[]{:S(2)}) collective-permute-start(bf16[8,256,256]{2,1,0:T(8,128)(2,1)S(1)} %get-tuple-element.14), channel_id=1, source_target_pairs={{0,7},{1,32},{3,27},{4,75},{5,64},{6,5},{7,120},{8,12},{9,25},{10,... | collective-permute-start | bytes 3145736 | tf_op jit(solution)/shard_map/ppermute | solution.py:423
  53.1 16.2 %collective-permute-start.6 = (bf16[8,256,256]{2,1,0:T(8,128)(2,1)S(1)}, bf16[8,256,256]{2,1,0:T(8,128)(2,1)S(1)}, u32[]{:S(2)}, u32[]{:S(2)}) collective-permute-start(bf16[8,256,256]{2,1,0:T(8,128)(2,1)S(1)} %get-tuple-element.15), channel_id=1, source_target_pairs={{1,2},{3,53},{4,48},{5,12},{6,38},{7,14},{8,120},{9,1},{10,9},{11,... | collective-permute-start | bytes 3145736 | tf_op jit(solution)/shard_map/ppermute | solution.py:423
  69.3 1.9 %collective-permute-start.7 = (bf16[8,256,256]{2,1,0:T(8,128)(2,1)S(1)}, bf16[8,256,256]{2,1,0:T(8,128)(2,1)S(1)}, u32[]{:S(2)}, u32[]{:S(2)}) collective-permute-start(bf16[8,256,256]{2,1,0:T(8,128)(2,1)S(1)} %get-tuple-element.16), channel_id=1, source_target_pairs={{0,16},{1,0},{2,1},{3,19},{4,52},{5,106},{7,6},{9,122},{10,2},{11,... | collective-permute-start | bytes 3145736 | tf_op jit(solution)/shard_map/ppermute | solution.py:423
  71.3 1.9 %collective-permute-start.8 = (bf16[8,256,256]{2,1,0:T(8,128)(2,1)S(1)}, bf16[8,256,256]{2,1,0:T(8,128)(2,1)S(1)}, u32[]{:S(2)}, u32[]{:S(2)}) collective-permute-start(bf16[8,256,256]{2,1,0:T(8,128)(2,1)S(1)} %get-tuple-element.17), channel_id=1, source_target_pairs={{0,1},{2,3},{3,11},{4,5},{5,21},{6,7},{7,23},{9,8},{11,10},{13,12}... | collective-permute-start | bytes 3145736 | tf_op jit(solution)/shard_map/ppermute | solution.py:423
  73.2 0.0 collective-permute-done.4.refs_5_
  73.2 0.0 copy-start.5
  73.2 12.2 %collective-permute-done.5.refs_6_ = bf16[8,256,256]{2,1,0:T(8,128)(2,1)S(1)} collective-permute-done((bf16[8,256,256]{2,1,0:T(8,128)(2,1)S(1)}, bf16[8,256,256]{2,1,0:T(8,128)(2,1)S(1)}, u32[]{:S(2)}, u32[]{:S(2)}) %collective-permute-start.5) | collective-permute-done | bytes 1048608 | tf_op jit(solution)/shard_map/ppermute | solution.py:423
  85.4 0.0 collective-permute-done.6.refs_7_
  85.4 4.9 %collective-permute-done.7.refs_8_ = bf16[8,256,256]{2,1,0:T(8,128)(2,1)S(1)} collective-permute-done((bf16[8,256,256]{2,1,0:T(8,128)(2,1)S(1)}, bf16[8,256,256]{2,1,0:T(8,128)(2,1)S(1)}, u32[]{:S(2)}, u32[]{:S(2)}) %collective-permute-start.7) | collective-permute-done | bytes 1048608 | tf_op jit(solution)/shard_map/ppermute | solution.py:423
  90.3 4.8 %collective-permute-done.8.refs_9_ = bf16[8,256,256]{2,1,0:T(8,128)(2,1)S(1)} collective-permute-done((bf16[8,256,256]{2,1,0:T(8,128)(2,1)S(1)}, bf16[8,256,256]{2,1,0:T(8,128)(2,1)S(1)}, u32[]{:S(2)}, u32[]{:S(2)}) %collective-permute-start.8) | collective-permute-done | bytes 1048608 | tf_op jit(solution)/shard_map/ppermute | solution.py:423
  95.1 0.0 copy-done.6
  95.1 0.0 copy-done.7
  95.1 1.1 %copy-done.9 = bf16[8,256,256]{2,1,0:T(8,128)(2,1)} copy-done((bf16[8,256,256]{2,1,0:T(8,128)(2,1)}, bf16[8,256,256]{2,1,0:T(8,128)(2,1)S(1)}, u32[]{:S(2)}) %copy-start.9) | copy-done | bytes 1048600
  96.2 5.5 %products.1 = f32[512,2048]{1,0:T(8,128)} custom-call(s32[768]{0:T(1024)} %get-tuple-element.12.lists, bf16[8,256,256]{2,1,0:T(8,128)(2,1)} %bitcast.11, bf16[8,256,256]{2,1,0:T(8,128)(2,1)} %collective-permute-done.refs_1_, bf16[8,256,256]{2,1,0:T(8,128)(2,1)} %collective-permute-done.1.refs_2_, ...), custom_call_target="tpu_custom_call", output_to_operand_aliasing={{}: (11, {})} | custom-call | flops 1000000000 | bytes 12582912 | tf_op jit(solution)/shard_map/products/pallas_call | solution.py:427
  (12 shorter events, 0.0 us)
Async XLA Ops:
  0.0 46.0 %copy-start.4 = (s32[640]{0:T(1024)S(1)}, s32[640]{0:T(1024)}, u32[]{:S(2)}) copy-start(s32[640]{0:T(1024)} %constant.18.clone.source) | copy-start | bytes 7684
  0.0 46.0 %copy-start = (bf16[1,1,8,256,256]{4,3,2,1,0:T(8,128)(2,1)S(1)}, bf16[1,1,8,256,256]{4,3,2,1,0:T(8,128)(2,1)}, u32[]{:S(2)}) copy-start(bf16[1,1,8,256,256]{4,3,2,1,0:T(8,128)(2,1)} %param.8) | copy-start | bytes 3145732
  0.0 40.5 %collective-permute-start.3 = (bf16[8,256,256]{2,1,0:T(8,128)(2,1)}, bf16[8,256,256]{2,1,0:T(8,128)(2,1)S(1)}, u32[]{:S(2)}, u32[]{:S(2)}) collective-permute-start(bf16[8,256,256]{2,1,0:T(8,128)(2,1)} %bitcast.7), channel_id=1, source_target_pairs={{0,8},{1,63},{2,82},{3,67},{4,12},{5,37},{6,5},{7,113},{8,15},{9,1... | collective-permute-start | bytes 3145736 | tf_op jit(solution)/shard_map/ppermute | solution.py:398
  1.4 39.1 %collective-permute-start.2 = (bf16[8,256,256]{2,1,0:T(8,128)(2,1)}, bf16[8,256,256]{2,1,0:T(8,128)(2,1)S(1)}, u32[]{:S(2)}, u32[]{:S(2)}) collective-permute-start(bf16[8,256,256]{2,1,0:T(8,128)(2,1)} %bitcast.8), channel_id=1, source_target_pairs={{0,12},{1,16},{2,10},{3,60},{4,64},{5,53},{6,96},{8,7},{10,1},{11,... | collective-permute-start | bytes 3145736 | tf_op jit(solution)/shard_map/ppermute | solution.py:398
  2.2 43.8 %collective-permute-start.1 = (bf16[8,256,256]{2,1,0:T(8,128)(2,1)}, bf16[8,256,256]{2,1,0:T(8,128)(2,1)}, u32[]{:S(2)}, u32[]{:S(2)}) collective-permute-start(bf16[8,256,256]{2,1,0:T(8,128)(2,1)} %bitcast.9), channel_id=1, source_target_pairs={{1,97},{2,45},{3,11},{5,90},{6,14},{7,23},{9,0},{10,27},{11,2},{12... | collective-permute-start | bytes 3145736 | tf_op jit(solution)/shard_map/ppermute | solution.py:398
  3.5 42.5 %collective-permute-start = (bf16[8,256,256]{2,1,0:T(8,128)(2,1)}, bf16[8,256,256]{2,1,0:T(8,128)(2,1)}, u32[]{:S(2)}, u32[]{:S(2)}) collective-permute-start(bf16[8,256,256]{2,1,0:T(8,128)(2,1)} %bitcast.10), channel_id=1, source_target_pairs={{1,9},{3,2},{5,4},{9,8},{11,10},{17,29},{18,17},{19,18},{20,33},{2... | collective-permute-start | bytes 3145736 | tf_op jit(solution)/shard_map/ppermute | solution.py:398
  40.5 55.7 %copy-start.1 = (bf16[8,256,256]{2,1,0:T(8,128)(2,1)}, bf16[8,256,256]{2,1,0:T(8,128)(2,1)S(1)}, u32[]{:S(2)}) copy-start(bf16[8,256,256]{2,1,0:T(8,128)(2,1)S(1)} %collective-permute-done.3.refs_4_) | copy-start | bytes 3145732
  40.5 55.7 %copy-start.2 = (bf16[8,256,256]{2,1,0:T(8,128)(2,1)}, bf16[8,256,256]{2,1,0:T(8,128)(2,1)S(1)}, u32[]{:S(2)}) copy-start(bf16[8,256,256]{2,1,0:T(8,128)(2,1)S(1)} %collective-permute-done.2.refs_3_) | copy-start | bytes 3145732
  46.0 0.7 copy-start.3
  49.3 23.9 %collective-permute-start.4 = (bf16[8,256,256]{2,1,0:T(8,128)(2,1)S(1)}, bf16[8,256,256]{2,1,0:T(8,128)(2,1)S(1)}, u32[]{:S(2)}, u32[]{:S(2)}) collective-permute-start(bf16[8,256,256]{2,1,0:T(8,128)(2,1)S(1)} %get-tuple-element.13), channel_id=1, source_target_pairs={{0,112},{1,16},{2,48},{3,32},{4,11},{5,13},{6,22},{7,15},{8,4},{9,... | collective-permute-start | bytes 3145736 | tf_op jit(solution)/shard_map/ppermute | solution.py:423
  51.2 34.2 %collective-permute-start.5 = (bf16[8,256,256]{2,1,0:T(8,128)(2,1)S(1)}, bf16[8,256,256]{2,1,0:T(8,128)(2,1)S(1)}, u32[]{:S(2)}, u32[]{:S(2)}) collective-permute-start(bf16[8,256,256]{2,1,0:T(8,128)(2,1)S(1)} %get-tuple-element.14), channel_id=1, source_target_pairs={{0,7},{1,32},{3,27},{4,75},{5,64},{6,5},{7,120},{8,12},{9,25},{10,... | collective-permute-start | bytes 3145736 | tf_op jit(solution)/shard_map/ppermute | solution.py:423
  53.1 32.3 %collective-permute-start.6 = (bf16[8,256,256]{2,1,0:T(8,128)(2,1)S(1)}, bf16[8,256,256]{2,1,0:T(8,128)(2,1)S(1)}, u32[]{:S(2)}, u32[]{:S(2)}) collective-permute-start(bf16[8,256,256]{2,1,0:T(8,128)(2,1)S(1)} %get-tuple-element.15), channel_id=1, source_target_pairs={{1,2},{3,53},{4,48},{5,12},{6,38},{7,14},{8,120},{9,1},{10,9},{11,... | collective-permute-start | bytes 3145736 | tf_op jit(solution)/shard_map/ppermute | solution.py:423
  69.3 20.9 %collective-permute-start.7 = (bf16[8,256,256]{2,1,0:T(8,128)(2,1)S(1)}, bf16[8,256,256]{2,1,0:T(8,128)(2,1)S(1)}, u32[]{:S(2)}, u32[]{:S(2)}) collective-permute-start(bf16[8,256,256]{2,1,0:T(8,128)(2,1)S(1)} %get-tuple-element.16), channel_id=1, source_target_pairs={{0,16},{1,0},{2,1},{3,19},{4,52},{5,106},{7,6},{9,122},{10,2},{11,... | collective-permute-start | bytes 3145736 | tf_op jit(solution)/shard_map/ppermute | solution.py:423
  71.3 23.8 %collective-permute-start.8 = (bf16[8,256,256]{2,1,0:T(8,128)(2,1)S(1)}, bf16[8,256,256]{2,1,0:T(8,128)(2,1)S(1)}, u32[]{:S(2)}, u32[]{:S(2)}) collective-permute-start(bf16[8,256,256]{2,1,0:T(8,128)(2,1)S(1)} %get-tuple-element.17), channel_id=1, source_target_pairs={{0,1},{2,3},{3,11},{4,5},{5,21},{6,7},{7,23},{9,8},{11,10},{13,12}... | collective-permute-start | bytes 3145736 | tf_op jit(solution)/shard_map/ppermute | solution.py:423
  73.2 23.0 %copy-start.5 = (bf16[8,256,256]{2,1,0:T(8,128)(2,1)}, bf16[8,256,256]{2,1,0:T(8,128)(2,1)S(1)}, u32[]{:S(2)}) copy-start(bf16[8,256,256]{2,1,0:T(8,128)(2,1)S(1)} %collective-permute-done.4.refs_5_) | copy-start | bytes 3145732
  85.4 9.7 %copy-start.6 = (bf16[8,256,256]{2,1,0:T(8,128)(2,1)}, bf16[8,256,256]{2,1,0:T(8,128)(2,1)S(1)}, u32[]{:S(2)}) copy-start(bf16[8,256,256]{2,1,0:T(8,128)(2,1)S(1)} %collective-permute-done.5.refs_6_) | copy-start | bytes 3145732
  85.4 9.7 %copy-start.7 = (bf16[8,256,256]{2,1,0:T(8,128)(2,1)}, bf16[8,256,256]{2,1,0:T(8,128)(2,1)S(1)}, u32[]{:S(2)}) copy-start(bf16[8,256,256]{2,1,0:T(8,128)(2,1)S(1)} %collective-permute-done.6.refs_7_) | copy-start | bytes 3145732
  90.3 4.8 %copy-start.8 = (bf16[8,256,256]{2,1,0:T(8,128)(2,1)}, bf16[8,256,256]{2,1,0:T(8,128)(2,1)S(1)}, u32[]{:S(2)}) copy-start(bf16[8,256,256]{2,1,0:T(8,128)(2,1)S(1)} %collective-permute-done.7.refs_8_) | copy-start | bytes 3145732
  95.1 1.1 %copy-start.9 = (bf16[8,256,256]{2,1,0:T(8,128)(2,1)}, bf16[8,256,256]{2,1,0:T(8,128)(2,1)S(1)}, u32[]{:S(2)}) copy-start(bf16[8,256,256]{2,1,0:T(8,128)(2,1)S(1)} %collective-permute-done.8.refs_9_) | copy-start | bytes 3145732

commit v5 on v4

--- a/solution.py
+++ b/solution.py
@@ -28,19 +28,6 @@
         (68, 64, 68), (69, 117, 69), (70, 86, 70), (71, 66, 71), (73, 84, 73), (76, 124, 76), (77, 109, 77), (85, 80, 85),
         (86, 103, 86), (87, 82, 87), (94, 5, 94), (95, 90, 95), (102, 118, 102), (103, 22, 103), (104, 105, 104), (105, 89, 105),
         (106, 58, 106), (108, 102, 108), (110, 111, 110), (111, 108, 111), (119, 7, 119), (121, 122, 121), (124, 60, 124),
-    ],
-    [
-        (1, 97, 1), (2, 45, 2), (3, 11, 3), (5, 90, 5), (6, 14, 6), (7, 23, 7), (9, 0, 9), (10, 27, 10),
-        (11, 2, 11), (12, 76, 12), (13, 4, 13), (14, 30, 14), (15, 6, 15), (17, 16, 17), (18, 24, 18), (19, 83, 19),
-        (20, 19, 20), (21, 49, 21), (22, 20, 22), (23, 22, 23), (25, 121, 25), (26, 9, 26), (27, 18, 27), (28, 94, 28),
-        (29, 61, 29), (30, 29, 30), (34, 39, 34), (35, 54, 35), (36, 33, 36), (37, 43, 37), (38, 100, 38), (40, 98, 40),
-        (41, 38, 41), (42, 32, 42), (43, 107, 43), (44, 41, 44), (45, 127, 45), (46, 78, 46), (47, 36, 47), (51, 48, 51),
-        (52, 70, 52), (53, 85, 53), (54, 58, 54), (55, 116, 55), (56, 40, 56), (57, 53, 57), (58, 10, 58), (59, 123, 59),
-        (60, 124, 60), (61, 50, 61), (62, 47, 62), (69, 65, 69), (70, 66, 70), (71, 74, 71), (72, 56, 72), (73, 69, 73),
-        (74, 26, 74), (75, 79, 75), (77, 28, 77), (78, 44, 78), (79, 67, 79), (85, 5, 85), (86, 21, 86), (87, 117, 87),
-        (88, 91, 88), (89, 73, 89), (90, 92, 90), (91, 101, 91), (93, 80, 93), (94, 126, 94), (95, 81, 95), (102, 103, 102),
-        (103, 96, 103), (105, 99, 105), (107, 86, 107), (108, 109, 108), (111, 104, 111), (119, 120, 119), (120, 113, 120), (121, 89, 121),
-        (122, 114, 122), (123, 75, 123), (124, 87, 124), (125, 118, 125), (126, 119, 126),
     ],
     [
         (0, 12, 0), (1, 16, 1), (2, 10, 2), (3, 60, 3), (4, 64, 4), (5, 53, 5), (6, 96, 6), (8, 7, 8),
@@ -55,6 +42,19 @@
         (93, 13, 93), (94, 81, 94), (95, 29, 95), (102, 106, 102), (103, 119, 103), (104, 38, 104), (105, 54, 105), (106, 74, 106),
         (107, 109, 107), (109, 111, 109), (110, 118, 110), (111, 97, 111), (119, 112, 119), (121, 105, 121), (122, 123, 122), (123, 115, 123),
         (124, 125, 124), (125, 126, 125), (127, 15, 127),
+    ],
+    [
+        (1, 97, 1), (2, 45, 2), (3, 11, 3), (5, 90, 5), (6, 14, 6), (7, 23, 7), (9, 0, 9), (10, 27, 10),
+        (11, 2, 11), (12, 76, 12), (13, 4, 13), (14, 30, 14), (15, 6, 15), (17, 16, 17), (18, 24, 18), (19, 83, 19),
+        (20, 19, 20), (21, 49, 21), (22, 20, 22), (23, 22, 23), (25, 121, 25), (26, 9, 26), (27, 18, 27), (28, 94, 28),
+        (29, 61, 29), (30, 29, 30), (34, 39, 34), (35, 54, 35), (36, 33, 36), (37, 43, 37), (38, 100, 38), (40, 98, 40),
+        (41, 38, 41), (42, 32, 42), (43, 107, 43), (44, 41, 44), (45, 127, 45), (46, 78, 46), (47, 36, 47), (51, 48, 51),
+        (52, 70, 52), (53, 85, 53), (54, 58, 54), (55, 116, 55), (56, 40, 56), (57, 53, 57), (58, 10, 58), (59, 123, 59),
+        (60, 124, 60), (61, 50, 61), (62, 47, 62), (69, 65, 69), (70, 66, 70), (71, 74, 71), (72, 56, 72), (73, 69, 73),
+        (74, 26, 74), (75, 79, 75), (77, 28, 77), (78, 44, 78), (79, 67, 79), (85, 5, 85), (86, 21, 86), (87, 117, 87),
+        (88, 91, 88), (89, 73, 89), (90, 92, 90), (91, 101, 91), (93, 80, 93), (94, 126, 94), (95, 81, 95), (102, 103, 102),
+        (103, 96, 103), (105, 99, 105), (107, 86, 107), (108, 109, 108), (111, 104, 111), (119, 120, 119), (120, 113, 120), (121, 89, 121),
+        (122, 114, 122), (123, 75, 123), (124, 87, 124), (125, 118, 125), (126, 119, 126),
     ],
     [
         (0, 8, 0), (1, 63, 1), (2, 82, 2), (3, 67, 3), (4, 12, 4), (5, 37, 5), (6, 5, 6), (7, 113, 7),
@@ -437,7 +437,7 @@
             pltpu.SemaphoreType.DMA((16,)),
         ],
         input_output_aliases={1 + NBUF: 0},
-        compiler_params=pltpu.CompilerParams(vmem_limit_bytes=60 * MIB),
+        compiler_params=pltpu.CompilerParams(vmem_limit_bytes=20 * MIB),
         cost_estimate=pl.CostEstimate(flops=10**9, bytes_accessed=12 * MIB, transcendentals=0),
         name="products",
     )(lists, *bufs, blank)

time: 102 us -> 102 us (level); the launches traced: 102 us -> 100 us
  starting transfers between devices: 28.6 us -> 31.9 us
  Pallas kernels: 18.5 us -> 16.3 us
  waiting for transfers between devices: 48.7 us -> 47 us
  local copies, waits for them, and re-layouts: 1.77 us -> 0.67 us
    ppermute x4, waiting for transfers between devices: 26.8 us -> 21.1 us  [local(): lax.ppermute(own, ('row', 'col'), [(u, v) for u, v, _ in edges])]
    ppermute x5, waiting for transfers between devices: 21.9 us -> 25.9 us  [local(): lax.ppermute(send, ('row', 'col'), [(u, v) for u, v, _ in edges])]
    ppermute x5, starting transfers between devices: 23.9 us -> 26.3 us  [local(): lax.ppermute(send, ('row', 'col'), [(u, v) for u, v, _ in edges])]
    pallas_call x1, Pallas kernels: 5.51 us -> 4.37 us  [local(): pl.pallas_call(product_kernel, out_shape=jax.ShapeDtypeStruct((SR * BS, C...]
    unnamed x20 -> x8, local copies, waits for them, and re-layouts: 1.77 us -> 0.67 us
where the time goes in v5:
time: 102 us; the launch traced here: 100 us
  waiting for transfers between devices  47 us (46%)
  starting transfers between devices  31.9 us (31%)
  Pallas kernels  16.3 us (16%)
  matrix products  4.01 us (4%)
    ppermute x5, starting transfers between devices, local(): lax.ppermute(send, ('row', 'col'), [(u, v) for u, v, _ in edges])  26.3 us
    ppermute x5, waiting for transfers between devices, local(): lax.ppermute(send, ('row', 'col'), [(u, v) for u, v, _ in edges])  25.9 us
    ppermute x4, waiting for transfers between devices, local(): lax.ppermute(own, ('row', 'col'), [(u, v) for u, v, _ in edges])  21.1 us
    pallas_call x1, Pallas kernels, local(): pl.pallas_call(index_kernel, out_shape=(jax.ShapeDtypeStruct((FETCH + 128...  9.71 us
    ppermute x4, starting transfers between devices, local(): lax.ppermute(own, ('row', 'col'), [(u, v) for u, v, _ in edges])  5.65 us
    pallas_call x1, Pallas kernels, local(): pl.pallas_call(product_kernel, out_shape=jax.ShapeDtypeStruct((SR * BS, C...  4.37 us
    pallas_call x1, Pallas kernels, local(): pl.pallas_call(pick_kernel, out_shape=[pltpu.VMEM((SLOTS, BS, BS), jnp.bf...  2.17 us
  transfers between devices with their start and end apart: 9, of which 5 were waited for; matrix products, arithmetic and copies ran while one was open for 4% of the time, Pallas kernels for 10%

profile of v5, /device:TPU:5, one launch (start us, length us, event | category | flops | bytes accessed | tf_op | source)
XLA Modules:
  0.0 100.0 jit_solution(4133958421553451919)
XLA Ops:
  0.0 0.0 copy-start.3
  0.0 0.0 copy-start
  0.0 1.4 %collective-permute-start.3 = (bf16[8,256,256]{2,1,0:T(8,128)(2,1)}, bf16[8,256,256]{2,1,0:T(8,128)(2,1)S(1)}, u32[]{:S(2)}, u32[]{:S(2)}) collective-permute-start(bf16[8,256,256]{2,1,0:T(8,128)(2,1)} %bitcast.7), channel_id=1, source_target_pairs={{0,8},{1,63},{2,82},{3,67},{4,12},{5,37},{6,5},{7,113},{8,15},{9,1... | collective-permute-start | bytes 3145736 | tf_op jit(solution)/shard_map/ppermute | solution.py:398
  1.4 1.3 %collective-permute-start.2 = (bf16[8,256,256]{2,1,0:T(8,128)(2,1)}, bf16[8,256,256]{2,1,0:T(8,128)(2,1)S(1)}, u32[]{:S(2)}, u32[]{:S(2)}) collective-permute-start(bf16[8,256,256]{2,1,0:T(8,128)(2,1)} %bitcast.8), channel_id=1, source_target_pairs={{1,97},{2,45},{3,11},{5,90},{6,14},{7,23},{9,0},{10,27},{11,2},{12... | collective-permute-start | bytes 3145736 | tf_op jit(solution)/shard_map/ppermute | solution.py:398
  2.7 1.7 %collective-permute-start.1 = (bf16[8,256,256]{2,1,0:T(8,128)(2,1)}, bf16[8,256,256]{2,1,0:T(8,128)(2,1)}, u32[]{:S(2)}, u32[]{:S(2)}) collective-permute-start(bf16[8,256,256]{2,1,0:T(8,128)(2,1)} %bitcast.9), channel_id=1, source_target_pairs={{0,12},{1,16},{2,10},{3,60},{4,64},{5,53},{6,96},{8,7},{10,1},{11,... | collective-permute-start | bytes 3145736 | tf_op jit(solution)/shard_map/ppermute | solution.py:398
  4.4 1.3 %collective-permute-start = (bf16[8,256,256]{2,1,0:T(8,128)(2,1)}, bf16[8,256,256]{2,1,0:T(8,128)(2,1)}, u32[]{:S(2)}, u32[]{:S(2)}) collective-permute-start(bf16[8,256,256]{2,1,0:T(8,128)(2,1)} %bitcast.10), channel_id=1, source_target_pairs={{1,9},{3,2},{5,4},{9,8},{11,10},{17,29},{18,17},{19,18},{20,33},{2... | collective-permute-start | bytes 3145736 | tf_op jit(solution)/shard_map/ppermute | solution.py:398
  5.7 1.1 %convolution_bitcast_fusion = f32[128,128]{1,0:T(8,128)S(1)} fusion(f32[128,128]{1,0:T(8,128)} %constant.14.clone, s32[128,128]{1,0:T(8,128)} %param.7), kind=kOutput, calls=%fused_computation.3 | convolution fusion | flops 25182208 | bytes 196608 | tf_op jit(solution)/shard_map/dot_general | solution.py:197
  6.8 1.2 %fusion.2 = f32[128,128]{1,0:T(8,128)S(1)} fusion(f32[128,128]{1,0:T(8,128)} %constant.16.clone, s32[128,128]{1,0:T(8,128)} %param.7), kind=kOutput, calls=%fused_computation.4 | convolution fusion | flops 25182208 | bytes 196608 | tf_op jit(solution)/shard_map/dot_general | solution.py:198
  7.9 1.8 %fusion.1.table = s32[128,128]{1,0:T(8,128)} fusion(f32[128,128]{1,0:T(8,128)S(1)} %convolution_bitcast_fusion, f32[128,128]{1,0:T(8,128)} %constant.15.clone, f32[128,128]{1,0:T(8,128)S(1)} %fusion.2, s32[128,128]{1,0:T(8,128)} %param.7), kind=kOutput, calls=%fused_computation.2 | convolution fusion | flops 25231360 | bytes 327680 | tf_op jit(solution)/shard_map/dot_general | solution.py:197
  9.7 9.7 %index.1 = (s32[768]{0:T(1024)}, f32[512,2048]{1,0:T(8,128)}) custom-call(s32[128,128]{1,0:T(8,128)} %fusion.1.table, s32[1024]{0:T(1024)} %constant.17.clone.place), custom_call_target="tpu_custom_call" | custom-call | flops 1000000000 | bytes 4194304 | tf_op jit(solution)/shard_map/index/pallas_call | solution.py:399
  19.4 21.1 %collective-permute-done.3.refs_4_ = bf16[8,256,256]{2,1,0:T(8,128)(2,1)S(1)} collective-permute-done((bf16[8,256,256]{2,1,0:T(8,128)(2,1)}, bf16[8,256,256]{2,1,0:T(8,128)(2,1)S(1)}, u32[]{:S(2)}, u32[]{:S(2)}) %collective-permute-start.3) | collective-permute-done | bytes 1048608 | tf_op jit(solution)/shard_map/ppermute | solution.py:398
  40.5 0.0 collective-permute-done.2.refs_3_
  40.5 0.0 collective-permute-done.1.refs_2_
  40.5 0.0 collective-permute-done.refs_1_
  40.5 0.0 copy-done.3
  40.5 0.0 copy-done
  40.5 0.0 copy-start.1
  40.5 0.7 copy-done.1
  41.2 0.0 copy-start.2
  41.2 2.2 %pick.1 = (bf16[8,256,256]{2,1,0:T(8,128)(2,1)S(1)}, bf16[8,256,256]{2,1,0:T(8,128)(2,1)S(1)}, bf16[8,256,256]{2,1,0:T(8,128)(2,1)S(1)}, bf16[8,256,256]{2,1,0:T(8,128)(2,1)S(1)}, bf16[8,256,256]{2,1,0:T(8,128)(2,1)S(1)}) custom-call(s32[640]{0:T(1024)S(1)} %copy-done.3, s32[768]{0:T(1024)S(1)} %copy-done.1, bf16[8,256,256]{2,1,0:T(8,128)(2,1)S(1)} %bitcast.11, ...), custom_call_target="tpu_custom_call" | custom-call | bytes 2097152 | tf_op jit(solution)/shard_map/pick/pallas_call | solution.py:412
  43.4 4.3 %collective-permute-start.4 = (bf16[8,256,256]{2,1,0:T(8,128)(2,1)S(1)}, bf16[8,256,256]{2,1,0:T(8,128)(2,1)S(1)}, u32[]{:S(2)}, u32[]{:S(2)}) collective-permute-start(bf16[8,256,256]{2,1,0:T(8,128)(2,1)S(1)} %get-tuple-element.13), channel_id=1, source_target_pairs={{0,112},{1,16},{2,48},{3,32},{4,11},{5,13},{6,22},{7,15},{8,4},{9,... | collective-permute-start | bytes 3145736 | tf_op jit(solution)/shard_map/ppermute | solution.py:423
  47.6 1.9 %collective-permute-start.5 = (bf16[8,256,256]{2,1,0:T(8,128)(2,1)S(1)}, bf16[8,256,256]{2,1,0:T(8,128)(2,1)S(1)}, u32[]{:S(2)}, u32[]{:S(2)}) collective-permute-start(bf16[8,256,256]{2,1,0:T(8,128)(2,1)S(1)} %get-tuple-element.14), channel_id=1, source_target_pairs={{0,7},{1,32},{3,27},{4,75},{5,64},{6,5},{7,120},{8,12},{9,25},{10,... | collective-permute-start | bytes 3145736 | tf_op jit(solution)/shard_map/ppermute | solution.py:423
  49.6 16.3 %collective-permute-start.6 = (bf16[8,256,256]{2,1,0:T(8,128)(2,1)S(1)}, bf16[8,256,256]{2,1,0:T(8,128)(2,1)S(1)}, u32[]{:S(2)}, u32[]{:S(2)}) collective-permute-start(bf16[8,256,256]{2,1,0:T(8,128)(2,1)S(1)} %get-tuple-element.15), channel_id=1, source_target_pairs={{1,2},{3,53},{4,48},{5,12},{6,38},{7,14},{8,120},{9,1},{10,9},{11,... | collective-permute-start | bytes 3145736 | tf_op jit(solution)/shard_map/ppermute | solution.py:423
  65.8 1.9 %collective-permute-start.7 = (bf16[8,256,256]{2,1,0:T(8,128)(2,1)S(1)}, bf16[8,256,256]{2,1,0:T(8,128)(2,1)S(1)}, u32[]{:S(2)}, u32[]{:S(2)}) collective-permute-start(bf16[8,256,256]{2,1,0:T(8,128)(2,1)S(1)} %get-tuple-element.16), channel_id=1, source_target_pairs={{0,16},{1,0},{2,1},{3,19},{4,52},{5,106},{7,6},{9,122},{10,2},{11,... | collective-permute-start | bytes 3145736 | tf_op jit(solution)/shard_map/ppermute | solution.py:423
  67.8 1.9 %collective-permute-start.8 = (bf16[8,256,256]{2,1,0:T(8,128)(2,1)S(1)}, bf16[8,256,256]{2,1,0:T(8,128)(2,1)S(1)}, u32[]{:S(2)}, u32[]{:S(2)}) collective-permute-start(bf16[8,256,256]{2,1,0:T(8,128)(2,1)S(1)} %get-tuple-element.17), channel_id=1, source_target_pairs={{0,1},{2,3},{3,11},{4,5},{5,21},{6,7},{7,23},{9,8},{11,10},{13,12}... | collective-permute-start | bytes 3145736 | tf_op jit(solution)/shard_map/ppermute | solution.py:423
  69.7 0.0 collective-permute-done.4.refs_5_
  69.7 8.5 %collective-permute-done.5.refs_6_ = bf16[8,256,256]{2,1,0:T(8,128)(2,1)S(1)} collective-permute-done((bf16[8,256,256]{2,1,0:T(8,128)(2,1)S(1)}, bf16[8,256,256]{2,1,0:T(8,128)(2,1)S(1)}, u32[]{:S(2)}, u32[]{:S(2)}) %collective-permute-start.5) | collective-permute-done | bytes 1048608 | tf_op jit(solution)/shard_map/ppermute | solution.py:423
  78.2 6.2 %collective-permute-done.6.refs_7_ = bf16[8,256,256]{2,1,0:T(8,128)(2,1)S(1)} collective-permute-done((bf16[8,256,256]{2,1,0:T(8,128)(2,1)S(1)}, bf16[8,256,256]{2,1,0:T(8,128)(2,1)S(1)}, u32[]{:S(2)}, u32[]{:S(2)}) %collective-permute-start.6) | collective-permute-done | bytes 1048608 | tf_op jit(solution)/shard_map/ppermute | solution.py:423
  84.4 3.0 %collective-permute-done.7.refs_8_ = bf16[8,256,256]{2,1,0:T(8,128)(2,1)S(1)} collective-permute-done((bf16[8,256,256]{2,1,0:T(8,128)(2,1)S(1)}, bf16[8,256,256]{2,1,0:T(8,128)(2,1)S(1)}, u32[]{:S(2)}, u32[]{:S(2)}) %collective-permute-start.7) | collective-permute-done | bytes 1048608 | tf_op jit(solution)/shard_map/ppermute | solution.py:423
  87.4 8.2 %collective-permute-done.8.refs_9_ = bf16[8,256,256]{2,1,0:T(8,128)(2,1)S(1)} collective-permute-done((bf16[8,256,256]{2,1,0:T(8,128)(2,1)S(1)}, bf16[8,256,256]{2,1,0:T(8,128)(2,1)S(1)}, u32[]{:S(2)}, u32[]{:S(2)}) %collective-permute-start.8) | collective-permute-done | bytes 1048608 | tf_op jit(solution)/shard_map/ppermute | solution.py:423
  95.6 0.0 copy-done.2
  95.6 4.4 %products.1 = f32[512,2048]{1,0:T(8,128)} custom-call(s32[768]{0:T(1024)S(1)} %copy-done.2, bf16[8,256,256]{2,1,0:T(8,128)(2,1)S(1)} %bitcast.12, bf16[8,256,256]{2,1,0:T(8,128)(2,1)} %collective-permute-done.refs_1_, bf16[8,256,256]{2,1,0:T(8,128)(2,1)} %collective-permute-done.1.refs_2_, ...), custom_call_target="tpu_custom_call", output_to_operand_aliasing={{}: (11, {})} | custom-call | flops 1000000000 | bytes 12582912 | tf_op jit(solution)/shard_map/products/pallas_call | solution.py:427
Async XLA Ops:
  0.0 40.5 %copy-start.3 = (s32[640]{0:T(1024)S(1)}, s32[640]{0:T(1024)}, u32[]{:S(2)}) copy-start(s32[640]{0:T(1024)} %constant.18.clone.source) | copy-start | bytes 7684
  0.0 40.5 %copy-start = (bf16[1,1,8,256,256]{4,3,2,1,0:T(8,128)(2,1)S(1)}, bf16[1,1,8,256,256]{4,3,2,1,0:T(8,128)(2,1)}, u32[]{:S(2)}) copy-start(bf16[1,1,8,256,256]{4,3,2,1,0:T(8,128)(2,1)} %param.8) | copy-start | bytes 3145732
  0.0 40.5 %collective-permute-start.3 = (bf16[8,256,256]{2,1,0:T(8,128)(2,1)}, bf16[8,256,256]{2,1,0:T(8,128)(2,1)S(1)}, u32[]{:S(2)}, u32[]{:S(2)}) collective-permute-start(bf16[8,256,256]{2,1,0:T(8,128)(2,1)} %bitcast.7), channel_id=1, source_target_pairs={{0,8},{1,63},{2,82},{3,67},{4,12},{5,37},{6,5},{7,113},{8,15},{9,1... | collective-permute-start | bytes 3145736 | tf_op jit(solution)/shard_map/ppermute | solution.py:398
  1.4 39.1 %collective-permute-start.2 = (bf16[8,256,256]{2,1,0:T(8,128)(2,1)}, bf16[8,256,256]{2,1,0:T(8,128)(2,1)S(1)}, u32[]{:S(2)}, u32[]{:S(2)}) collective-permute-start(bf16[8,256,256]{2,1,0:T(8,128)(2,1)} %bitcast.8), channel_id=1, source_target_pairs={{1,97},{2,45},{3,11},{5,90},{6,14},{7,23},{9,0},{10,27},{11,2},{12... | collective-permute-start | bytes 3145736 | tf_op jit(solution)/shard_map/ppermute | solution.py:398
  2.7 37.8 %collective-permute-start.1 = (bf16[8,256,256]{2,1,0:T(8,128)(2,1)}, bf16[8,256,256]{2,1,0:T(8,128)(2,1)}, u32[]{:S(2)}, u32[]{:S(2)}) collective-permute-start(bf16[8,256,256]{2,1,0:T(8,128)(2,1)} %bitcast.9), channel_id=1, source_target_pairs={{0,12},{1,16},{2,10},{3,60},{4,64},{5,53},{6,96},{8,7},{10,1},{11,... | collective-permute-start | bytes 3145736 | tf_op jit(solution)/shard_map/ppermute | solution.py:398
  4.4 36.1 %collective-permute-start = (bf16[8,256,256]{2,1,0:T(8,128)(2,1)}, bf16[8,256,256]{2,1,0:T(8,128)(2,1)}, u32[]{:S(2)}, u32[]{:S(2)}) collective-permute-start(bf16[8,256,256]{2,1,0:T(8,128)(2,1)} %bitcast.10), channel_id=1, source_target_pairs={{1,9},{3,2},{5,4},{9,8},{11,10},{17,29},{18,17},{19,18},{20,33},{2... | collective-permute-start | bytes 3145736 | tf_op jit(solution)/shard_map/ppermute | solution.py:398
  40.5 0.7 copy-start.1
  41.2 54.4 %copy-start.2 = (s32[768]{0:T(1024)S(1)}, s32[768]{0:T(1024)}, u32[]{:S(2)}) copy-start(s32[768]{0:T(1024)} %get-tuple-element.12.lists) | copy-start | bytes 9220
  43.4 26.3 %collective-permute-start.4 = (bf16[8,256,256]{2,1,0:T(8,128)(2,1)S(1)}, bf16[8,256,256]{2,1,0:T(8,128)(2,1)S(1)}, u32[]{:S(2)}, u32[]{:S(2)}) collective-permute-start(bf16[8,256,256]{2,1,0:T(8,128)(2,1)S(1)} %get-tuple-element.13), channel_id=1, source_target_pairs={{0,112},{1,16},{2,48},{3,32},{4,11},{5,13},{6,22},{7,15},{8,4},{9,... | collective-permute-start | bytes 3145736 | tf_op jit(solution)/shard_map/ppermute | solution.py:423
  47.6 30.6 %collective-permute-start.5 = (bf16[8,256,256]{2,1,0:T(8,128)(2,1)S(1)}, bf16[8,256,256]{2,1,0:T(8,128)(2,1)S(1)}, u32[]{:S(2)}, u32[]{:S(2)}) collective-permute-start(bf16[8,256,256]{2,1,0:T(8,128)(2,1)S(1)} %get-tuple-element.14), channel_id=1, source_target_pairs={{0,7},{1,32},{3,27},{4,75},{5,64},{6,5},{7,120},{8,12},{9,25},{10,... | collective-permute-start | bytes 3145736 | tf_op jit(solution)/shard_map/ppermute | solution.py:423
  49.6 34.8 %collective-permute-start.6 = (bf16[8,256,256]{2,1,0:T(8,128)(2,1)S(1)}, bf16[8,256,256]{2,1,0:T(8,128)(2,1)S(1)}, u32[]{:S(2)}, u32[]{:S(2)}) collective-permute-start(bf16[8,256,256]{2,1,0:T(8,128)(2,1)S(1)} %get-tuple-element.15), channel_id=1, source_target_pairs={{1,2},{3,53},{4,48},{5,12},{6,38},{7,14},{8,120},{9,1},{10,9},{11,... | collective-permute-start | bytes 3145736 | tf_op jit(solution)/shard_map/ppermute | solution.py:423
  65.8 21.6 %collective-permute-start.7 = (bf16[8,256,256]{2,1,0:T(8,128)(2,1)S(1)}, bf16[8,256,256]{2,1,0:T(8,128)(2,1)S(1)}, u32[]{:S(2)}, u32[]{:S(2)}) collective-permute-start(bf16[8,256,256]{2,1,0:T(8,128)(2,1)S(1)} %get-tuple-element.16), channel_id=1, source_target_pairs={{0,16},{1,0},{2,1},{3,19},{4,52},{5,106},{7,6},{9,122},{10,2},{11,... | collective-permute-start | bytes 3145736 | tf_op jit(solution)/shard_map/ppermute | solution.py:423
  67.8 27.9 %collective-permute-start.8 = (bf16[8,256,256]{2,1,0:T(8,128)(2,1)S(1)}, bf16[8,256,256]{2,1,0:T(8,128)(2,1)S(1)}, u32[]{:S(2)}, u32[]{:S(2)}) collective-permute-start(bf16[8,256,256]{2,1,0:T(8,128)(2,1)S(1)} %get-tuple-element.17), channel_id=1, source_target_pairs={{0,1},{2,3},{3,11},{4,5},{5,21},{6,7},{7,23},{9,8},{11,10},{13,12}... | collective-permute-start | bytes 3145736 | tf_op jit(solution)/shard_map/ppermute | solution.py:423
